TPU v7x, 32 devices: a whole 2x2x4 slice. The times are simulated.
32 devices in a mesh: samp: 4 (over x, core), pair: 8 (over z, y).
Axes of the slice: x: 2, y: 2, z: 4, core: 2. Of those that a mesh axis runs over, the one named last changes fastest.
Arguments:
- matrix: bfloat16 [32768, 4096], P('samp', 'pair'), may hold values from -48 to 48
- tournament: int32 [2, 8], replicated, may hold values from 0 to 1
Outputs:
- result: bfloat16 [32768, 4096], P('samp', 'pair')
All inputs are finite; a program needn't handle non-finite values.
Results may differ from a plain program's by a relative error of at most 0.008.
Values may be sent and summed in bfloat16 or wider, within the bound.
No kernel may reach another device: no remote copies, remote signals or barrier semaphores. Data moves between devices by JAX's collectives and lax.ppermute only.
A program may use at most 128 MiB of HBM per device.

v0:
```python
import jax
import jax.numpy as jnp
from jax import lax
from jax.sharding import PartitionSpec as P

ROUNDS = 2
POLAR_STEPS = 5


coupling = 2.0
start_scale = 6.0


def passed_along(value, axis, by):
    length = lax.axis_size(axis)
    return lax.ppermute(value, axis, [(i, (i + by) % length) for i in range(length)])


def polar_rotation(cross_gram):
    block_width = cross_gram.shape[0]
    frobenius = jnp.sqrt(jnp.sum(cross_gram * cross_gram) + 1e-06)
    coupled = coupling * cross_gram / frobenius
    blank_block = jnp.zeros_like(coupled)
    skew_matrix = jnp.concatenate(
        [jnp.concatenate([blank_block, -coupled], 1), jnp.concatenate([coupled.T, blank_block], 1)],
        0,
    )
    iterate = (jnp.eye(2 * block_width, dtype=coupled.dtype) + skew_matrix) / start_scale
    for iteration in range(POLAR_STEPS):
        rounded = iterate.astype(jnp.bfloat16)
        square = lax.dot_general(
            rounded, rounded, (((0,), (0,)), ((), ())), preferred_element_type=jnp.float32
        ).astype(jnp.bfloat16)
        iterate = 1.5 * iterate - 0.5 * jnp.dot(rounded, square, preferred_element_type=jnp.float32)
    return iterate.astype(jnp.bfloat16)


def local_cross(rows, block_width):
    return lax.dot_general(
        rows[:, :block_width],
        rows[:, block_width:],
        (((0,), (0,)), ((), ())),
        preferred_element_type=jnp.float32,
    )


def pair_gram(current, block_width):
    cross_gram = lax.psum(local_cross(current, block_width).astype(jnp.bfloat16), "samp").astype(
        jnp.float32
    )
    return cross_gram


def shards(matrix, tournament):
    cycle_size = lax.axis_size("pair")
    half_cycle = cycle_size // 2
    position = lax.axis_index("pair")
    block_width = matrix.shape[1] // 2
    current = matrix
    for tourney in range(ROUNDS):
        slot_index = (position + half_cycle * (tourney % 2)) % cycle_size
        selector = tournament[tourney, slot_index]
        rotation = polar_rotation(pair_gram(current, block_width))
        first_cols = rotation[:, :block_width]
        second_cols = rotation[:, block_width:]
        keep_columns = jnp.where(selector == 1, second_cols, first_cols)
        move_columns = jnp.where(selector == 1, first_cols, second_cols)
        moving_block = jnp.dot(current, move_columns, preferred_element_type=jnp.float32).astype(
            jnp.bfloat16
        )
        arrived = passed_along(moving_block, "pair", half_cycle + 1)
        kept_block = jnp.dot(current, keep_columns, preferred_element_type=jnp.float32).astype(
            jnp.bfloat16
        )
        current = jnp.concatenate([kept_block, arrived], axis=1)
    return current


def solution(mesh):
    placed = (P("samp", "pair"), P())
    return jax.shard_map(
        shards, mesh=mesh, in_specs=placed, out_specs=P("samp", "pair"), check_vma=False
    )
```

profile of v0, /device:TPU:4, one launch (start us, length us, event | category | flops | bytes accessed | tf_op | source)
XLA Modules:
  0.0 500.6 jit_solution(6991794256014966504)
XLA Ops:
  6.5 5.4 %fusion.16 = bf16[256,256]{1,0:T(8,128)(2,1)} fusion(bf16[8192,512]{1,0:T(8,128)(2,1)} %param.2), kind=kOutput, calls=%fused_computation.44 | convolution fusion | flops 1073807360 | bytes 8519680 | tf_op jit(solution)/shard_map/dot_general | solution.py:39
  13.4 31.4 %all-reduce.7.cloned.1.call-done = bf16[256,256]{1,0:T(8,128)(2,1)} async-done(((bf16[256,256]{1,0:T(8,128)(2,1)}), bf16[256,256]{1,0:T(8,128)(2,1)}) %all-reduce.7.cloned.1.call-update) | async-done | bytes 131088 | tf_op jit(solution)/shard_map/psum | solution.py:48
  44.8 1.6 fusion.50
  47.0 0.9 fusion.49
  51.6 0.9 fusion.14
  52.5 5.8 %fusion = bf16[8192,256]{0,1:T(8,128)(2,1)S(1)} fusion(bf16[8192,512]{1,0:T(8,128)(2,1)} %param.2, pred[]{:T(512)} %bitcast, bf16[512,512]{0,1:T(8,128)(2,1)S(1)} %fusion.14), kind=kOutput, calls=%fused_computation.4 | convolution fusion | flops 2149711872 | bytes 13107201 | tf_op jit(solution)/shard_map/dot_general | solution.py:68
  58.2 3.6 collective-permute-start
  61.8 5.8 %convolution_convert_fusion.3 = bf16[256,8192]{1,0:T(8,128)(2,1)S(1)} fusion(bf16[8192,512]{1,0:T(8,128)(2,1)} %param.2, pred[]{:T(512)} %bitcast, bf16[512,512]{0,1:T(8,128)(2,1)S(1)} %fusion.14), kind=kOutput, calls=%fused_computation.3 | convolution fusion | flops 2149711872 | bytes 13107201 | tf_op jit(solution)/shard_map/dot_general | solution.py:72
  67.6 173.9 %collective-permute-done = bf16[8192,256]{0,1:T(8,128)(2,1)S(1)} collective-permute-done((bf16[8192,256]{0,1:T(8,128)(2,1)S(1)}, bf16[8192,256]{0,1:T(8,128)(2,1)S(1)}, u32[]{:S(2)}, u32[]{:S(2)}) %collective-permute-start) | collective-permute-done | bytes 4194336 | tf_op jit(solution)/shard_map/ppermute | solution.py:16
  241.5 2.0 copy-done.3
  243.5 1.9 convolution_convert_fusion.14
  246.1 31.2 %all-reduce.9.cloned.1.call-done = bf16[256,256]{1,0:T(8,128)(2,1)} async-done(((bf16[256,256]{1,0:T(8,128)(2,1)}), bf16[256,256]{1,0:T(8,128)(2,1)}) %all-reduce.9.cloned.1.call-update) | async-done | bytes 131088 | tf_op jit(solution)/shard_map/psum | solution.py:48
  277.2 1.7 fusion.52
  279.6 0.9 fusion.70
  281.6 0.9 fusion.7
  282.4 0.9 fusion.6
  283.3 0.9 fusion.5
  284.2 0.9 fusion.15
  285.1 6.0 %convolution_convert_fusion = bf16[8192,256]{0,1:T(8,128)(2,1)S(1)} fusion(bf16[8192,256]{0,1:T(8,128)(2,1)} %copy-done.3, bf16[8192,256]{0,1:T(8,128)(2,1)} %bitcast.13, pred[]{:T(512)} %bitcast.4, bf16[512,512]{0,1:T(8,128)(2,1)S(1)} %fusion.15), kind=kOutput, calls=%fused_computation | convolution fusion | flops 2166489088 | bytes 13107201 | tf_op jit(solution)/shard_map/dot_general | solution.py:68
  291.0 3.4 collective-permute-start.1
  294.4 3.9 convolution_convert_fusion.1
  298.3 175.8 %collective-permute-done.1 = bf16[8192,256]{0,1:T(8,128)(2,1)} collective-permute-done((bf16[8192,256]{0,1:T(8,128)(2,1)S(1)}, bf16[8192,256]{0,1:T(8,128)(2,1)}, u32[]{:S(2)}, u32[]{:S(2)}) %collective-permute-start.1) | collective-permute-done | bytes 4194336 | tf_op jit(solution)/shard_map/ppermute | solution.py:16
  474.2 7.7 %pad_maximum_fusion.1 = bf16[8192,512]{0,1:T(8,128)(2,1)} fusion(bf16[8192,256]{0,1:T(8,128)(2,1)} %collective-permute-done.1, bf16[8192,256]{0,1:T(8,128)(2,1)} %convolution_convert_fusion.1), kind=kLoop, calls=%fused_computation.6 | loop fusion | flops 16777216 | bytes 16777216 | tf_op jit(solution)/shard_map/concatenate | solution.py:75
  481.8 11.9 %copy.16 = bf16[8192,512]{1,0:T(8,128)(2,1)} copy(bf16[8192,512]{0,1:T(8,128)(2,1)} %pad_maximum_fusion.1) | data formatting | bytes 16777216 | tf_op jit(solution)/shard_map/concatenate | solution.py:75
  (22 shorter events, 5.3 us)
Async XLA Ops:
  6.5 5.5 %copy-start.2 = (s32[2,8]{1,0:T(2,128)S(1)}, s32[2,8]{1,0:T(2,128)}, u32[]{:S(2)}) copy-start(s32[2,8]{1,0:T(2,128)} %param.3) | copy-start | bytes 196
  6.5 38.2 %all-reduce.7.cloned.1.call-start = ((), (), s32[]{:S(2)}) async-start(), calls=%async_computation | async-start | bytes 262144 | tf_op jit(solution)/shard_map/psum | solution.py:48
  12.0 265.2 %all-reduce.9.cloned.1.call-start = ((), (), s32[]{:S(2)}) async-start(), calls=%async_computation.1 | async-start | bytes 262144 | tf_op jit(solution)/shard_map/psum | solution.py:48
  58.2 183.2 %collective-permute-start = (bf16[8192,256]{0,1:T(8,128)(2,1)S(1)}, bf16[8192,256]{0,1:T(8,128)(2,1)S(1)}, u32[]{:S(2)}, u32[]{:S(2)}) collective-permute-start(bf16[8192,256]{0,1:T(8,128)(2,1)S(1)} %fusion), channel_id=1, source_target_pairs={{0,5},{1,6},{2,7},{3,0},{4,1},{5,2},{6,3},{7,4},{8,13},{9,14},{10,... | collective-permute-start | bytes 12582920 | tf_op jit(solution)/shard_map/ppermute | solution.py:16
  67.6 173.9 %copy-start = (bf16[256,8192]{1,0:T(8,128)(2,1)}, bf16[256,8192]{1,0:T(8,128)(2,1)S(1)}, u32[]{:S(2)}) copy-start(bf16[256,8192]{1,0:T(8,128)(2,1)S(1)} %convolution_convert_fusion.3) | copy-start | bytes 12582916
  241.5 2.0 copy-start.3
  285.1 9.4 %copy-start.1 = (bf16[256,8192]{1,0:T(8,128)(2,1)S(1)}, bf16[256,8192]{1,0:T(8,128)(2,1)}, u32[]{:S(2)}) copy-start(bf16[256,8192]{1,0:T(8,128)(2,1)} %copy-done) | copy-start | bytes 12582916
  285.1 9.3 %copy-start.4 = (bf16[8192,256]{0,1:T(8,128)(2,1)S(1)}, bf16[8192,256]{0,1:T(8,128)(2,1)}, u32[]{:S(2)}) copy-start(bf16[8192,256]{0,1:T(8,128)(2,1)} %copy-done.3) | copy-start | bytes 12582916
  291.0 183.1 %collective-permute-start.1 = (bf16[8192,256]{0,1:T(8,128)(2,1)S(1)}, bf16[8192,256]{0,1:T(8,128)(2,1)}, u32[]{:S(2)}, u32[]{:S(2)}) collective-permute-start(bf16[8192,256]{0,1:T(8,128)(2,1)S(1)} %convolution_convert_fusion), channel_id=1, source_target_pairs={{0,5},{1,6},{2,7},{3,0},{4,1},{5,2},{6,3},{7,4},{8,13},{9,14},{10,... | collective-permute-start | bytes 12582920 | tf_op jit(solution)/shard_map/ppermute | solution.py:16
Sparse Core Ops, SparseCore 0:
  12.1 32.5 all-reduce.6
  245.5 31.6 all-reduce.8
where the time goes:
time: 501 us
  waiting for transfers between devices  412 us (82%)
  matrix products  37.4 us (7%)
  between operations  16.3 us (3%)
  local copies, waits for them, and re-layouts  14.9 us (3%)
  other arithmetic  12.8 us (3%)
  starting transfers between devices  6.97 us (1%)
    ppermute x2, waiting for transfers between devices, passed_along(): lax.ppermute(value, axis, [(i, (i + by) % length) for i in range(length)])  350 us
    psum x2, waiting for transfers between devices, pair_gram(): lax.psum(local_cross(current, block_width).astype(jnp.bfloat16), 'samp')  62.5 us
    concatenate x1, local copies, waits for them, and re-layouts, shards(): current = jnp.concatenate([kept_block, arrived], axis=1)  11.9 us
    dot_general x2, matrix products, shards(): jnp.dot(current, move_columns, preferred_element_type=jnp.float32)  11.7 us
  transfers between devices with their start and end apart: 4, of which 4 were waited for; matrix products, arithmetic and copies ran while one was open for 2% of the time, Pallas kernels for 0%

commit v1 on v0

v1 whole, which is shorter than its diff:
```python
import jax
import jax.numpy as jnp
from jax import lax
from jax.sharding import PartitionSpec as P

ROUNDS = 2
POLAR_STEPS = 5
CHUNKS = 4


coupling = 2.0
start_scale = 6.0


def polar_rotation(cross_gram):
    block_width = cross_gram.shape[0]
    frobenius = jnp.sqrt(jnp.sum(cross_gram * cross_gram) + 1e-06)
    coupled = coupling * cross_gram / frobenius
    blank_block = jnp.zeros_like(coupled)
    skew_matrix = jnp.concatenate(
        [jnp.concatenate([blank_block, -coupled], 1), jnp.concatenate([coupled.T, blank_block], 1)],
        0,
    )
    iterate = (jnp.eye(2 * block_width, dtype=coupled.dtype) + skew_matrix) / start_scale
    for iteration in range(POLAR_STEPS):
        rounded = iterate.astype(jnp.bfloat16)
        square = lax.dot_general(
            rounded, rounded, (((0,), (0,)), ((), ())), preferred_element_type=jnp.float32
        ).astype(jnp.bfloat16)
        iterate = 1.5 * iterate - 0.5 * jnp.dot(rounded, square, preferred_element_type=jnp.float32)
    return iterate.astype(jnp.bfloat16)


def summed(value):
    length = lax.axis_size("samp")
    if length & (length - 1):
        return lax.psum(value.astype(jnp.bfloat16), "samp").astype(jnp.float32)
    total = value.astype(jnp.bfloat16)
    step = 1
    while step < length:
        other = lax.ppermute(total, "samp", [(i, i ^ step) for i in range(length)])
        total = total.astype(jnp.float32) + other.astype(jnp.float32)
        step *= 2
        if step < length:
            total = total.astype(jnp.bfloat16)
    return total.astype(jnp.float32)


def cross(first, second):
    return lax.dot_general(
        first, second, (((0,), (0,)), ((), ())), preferred_element_type=jnp.float32
    )


def shards(matrix, tournament):
    cycle_size = lax.axis_size("pair")
    half_cycle = cycle_size // 2
    position = lax.axis_index("pair")
    odd = position % 2 == 1
    rows, width = matrix.shape[0], matrix.shape[1] // 2
    piece = rows // CHUNKS

    def target(p):
        return (p + half_cycle + 1) % cycle_size

    everyone = [(p, target(p)) for p in range(cycle_size)]
    from_odd = [(p, target(p)) for p in range(1, cycle_size, 2)]
    to_neighbour = [(p, p + 1) for p in range(0, cycle_size, 2)]
    forward = [(p + 1, target(p)) for p in range(0, cycle_size, 2)]

    kept, arrived = matrix[:, :width], [matrix[i * piece : (i + 1) * piece, width:] for i in range(CHUNKS)]
    for tourney in range(ROUNDS):
        slot_index = (position + half_cycle * (tourney % 2)) % cycle_size
        selector = tournament[tourney, slot_index]
        if tourney == 0:
            gram = cross(matrix[:, :width], matrix[:, width:])
            parts = [matrix[i * piece : (i + 1) * piece] for i in range(CHUNKS)]
        else:
            parts = [
                jnp.concatenate([kept[i * piece : (i + 1) * piece], arrived[i]], axis=1)
                for i in range(CHUNKS)
            ]
            gram = sum(cross(kept[i * piece : (i + 1) * piece], arrived[i]) for i in range(CHUNKS))
        rotation = polar_rotation(summed(gram))
        first_cols = rotation[:, :width]
        second_cols = rotation[:, width:]
        keep_columns = jnp.where(selector == 1, second_cols, first_cols)
        move_columns = jnp.where(selector == 1, first_cols, second_cols)

        def times(part, columns):
            return jnp.dot(part, columns, preferred_element_type=jnp.float32).astype(jnp.bfloat16)

        last = times(parts[-1], move_columns)
        passed = lax.ppermute(last, "pair", to_neighbour)
        got = [lax.ppermute(times(part, move_columns), "pair", everyone) for part in parts[:-1]]
        own = lax.ppermute(last, "pair", from_odd)
        kept = jnp.concatenate([times(part, keep_columns) for part in parts], axis=0)
        far = lax.ppermute(passed, "pair", forward)
        arrived = got + [jnp.where(odd, far, own)]
    return jnp.concatenate([kept, jnp.concatenate(arrived, axis=0)], axis=1)


def solution(mesh):
    placed = (P("samp", "pair"), P())
    return jax.shard_map(
        shards, mesh=mesh, in_specs=placed, out_specs=P("samp", "pair"), check_vma=False
    )
```

time: 501 us -> 426 us (0.85)
  waiting for transfers between devices: 412 us -> 147 us
  starting transfers between devices: 6.97 us -> 142 us
  other arithmetic: 12.8 us -> 68.2 us
  between operations: 16.3 us -> 3.15 us
  matrix products: 37.4 us -> 49.9 us
    ppermute x2 -> x16, waiting for transfers between devices: 350 us -> 147 us  [the longest x6 66.7 us: shards(): lax.ppermute(times(part, move_columns), 'pair', everyone)]
    ppermute x2 -> x16, starting transfers between devices: 6.93 us -> 142 us  [the longest x2 117 us: shards(): far = lax.ppermute(passed, 'pair', forward)]
    psum x2 -> x0, waiting for transfers between devices: 62.5 us -> none  [pair_gram(): lax.psum(local_cross(current, block_width).astype(jnp.bfloat16), 'samp')]
    concatenate x1, other arithmetic: 7.68 us -> 63.6 us  [shards(): return jnp.concatenate([kept, jnp.concatenate(arrived, axis=0)], axis=1)]
    dot_general x10, matrix products: 8.6 us -> 24.9 us  [polar_rotation(): jnp.dot(rounded, square, preferred_element_type=jnp.float32)]
    dot_general x6 -> x21, matrix products: 28.7 us -> 25 us  [the longest x16 18.4 us: times(): jnp.dot(part, columns, preferred_element_type=jnp.float32)]
  transfers between devices with their start and end apart: 4 -> 16, of which waited for: 4 -> 12; matrix products, arithmetic and copies ran while one was open for 2% -> 3% of each run, Pallas kernels for 0% -> 0%
where the time goes in v1:
time: 426 us; the launch traced here: 425 us
  waiting for transfers between devices  147 us (35%)
  starting transfers between devices  142 us (33%)
  other arithmetic  68.2 us (16%)
  matrix products  49.9 us (12%)
  local copies, waits for them, and re-layouts  14.2 us (3%)
    ppermute x2, starting transfers between devices, shards(): far = lax.ppermute(passed, 'pair', forward)  117 us
    ppermute x6, waiting for transfers between devices, shards(): lax.ppermute(times(part, move_columns), 'pair', everyone)  66.7 us
    concatenate x1, other arithmetic, shards(): return jnp.concatenate([kept, jnp.concatenate(arrived, axis=0)], axis=1)  63.6 us
    ppermute x2, waiting for transfers between devices, shards(): far = lax.ppermute(passed, 'pair', forward)  45.9 us
    ppermute x2, waiting for transfers between devices, shards(): passed = lax.ppermute(last, 'pair', to_neighbour)  26 us
    dot_general x10, matrix products, polar_rotation(): jnp.dot(rounded, square, preferred_element_type=jnp.float32)  24.9 us
    dot_general x16, matrix products, times(): jnp.dot(part, columns, preferred_element_type=jnp.float32)  18.4 us
    concatenate x1, local copies, waits for them, and re-layouts, shards(): return jnp.concatenate([kept, jnp.concatenate(arrived, axis=0)], axis=1)  11.9 us
  transfers between devices with their start and end apart: 16, of which 12 were waited for; matrix products, arithmetic and copies ran while one was open for 3% of the time, Pallas kernels for 0%

profile of v1, /device:TPU:4, one launch (start us, length us, event | category | flops | bytes accessed | tf_op | source)
XLA Modules:
  0.0 424.8 jit_solution(8850052902751101115)
XLA Ops:
  0.0 4.8 %fusion.29 = bf16[256,256]{1,0:T(8,128)(2,1)S(1)} fusion(bf16[8192,512]{1,0:T(8,128)(2,1)} %param.2), kind=kOutput, calls=%fused_computation.74 | convolution fusion | flops 1073807360 | bytes 8519680 | tf_op jit(solution)/shard_map/dot_general | solution.py:50
  9.1 2.8 collective-permute-done.1
  17.8 2.5 convolution_convert_fusion.9
  20.3 2.3 convolution_convert_fusion.11
  22.7 2.5 fusion.6
  28.8 5.8 %collective-permute-start.3 = (bf16[2048,256]{0,1:T(8,128)(2,1)S(1)}, bf16[2048,256]{0,1:T(8,128)(2,1)S(1)}, u32[]{:S(2)}, u32[]{:S(2)}) collective-permute-start(bf16[2048,256]{0,1:T(8,128)(2,1)S(1)} %fusion.4), channel_id=1, source_target_pairs={{0,5},{1,6},{2,7},{3,0},{4,1},{5,2},{6,3},{7,4},{8,13},{9,14},{10,... | collective-permute-start | bytes 3145736 | tf_op jit(solution)/shard_map/ppermute | solution.py:95
  36.2 3.6 collective-permute-start.7
  40.6 11.9 %collective-permute-done.5 = bf16[2048,256]{0,1:T(8,128)(2,1)S(1)} collective-permute-done((bf16[2048,256]{0,1:T(8,128)(2,1)S(1)}, bf16[2048,256]{0,1:T(8,128)(2,1)S(1)}, u32[]{:S(2)}, u32[]{:S(2)}) %collective-permute-start.5) | collective-permute-done | bytes 1048608 | tf_op jit(solution)/shard_map/ppermute | solution.py:94
  52.6 71.0 %collective-permute-start.6 = (bf16[2048,256]{0,1:T(8,128)(2,1)S(1)}, bf16[2048,256]{0,1:T(8,128)(2,1)S(1)}, u32[]{:S(2)}, u32[]{:S(2)}) collective-permute-start(bf16[2048,256]{0,1:T(8,128)(2,1)S(1)} %collective-permute-done.5), channel_id=1, source_target_pairs={{1,5},{3,7},{5,1},{7,3},{9,13},{11,15},{13,9},{15,11},{17,21},{19,... | collective-permute-start | bytes 3145736 | tf_op jit(solution)/shard_map/ppermute | solution.py:98
  125.0 22.0 %collective-permute-done.4 = bf16[2048,256]{0,1:T(8,128)(2,1)S(1)} collective-permute-done((bf16[2048,256]{0,1:T(8,128)(2,1)S(1)}, bf16[2048,256]{0,1:T(8,128)(2,1)S(1)}, u32[]{:S(2)}, u32[]{:S(2)}) %collective-permute-start.4) | collective-permute-done | bytes 1048608 | tf_op jit(solution)/shard_map/ppermute | solution.py:95
  147.5 20.8 %collective-permute-done.2 = bf16[2048,256]{0,1:T(8,128)(2,1)S(1)} collective-permute-done((bf16[2048,256]{0,1:T(8,128)(2,1)S(1)}, bf16[2048,256]{0,1:T(8,128)(2,1)S(1)}, u32[]{:S(2)}, u32[]{:S(2)}) %collective-permute-start.2) | collective-permute-done | bytes 1048608 | tf_op jit(solution)/shard_map/ppermute | solution.py:95
  173.1 3.4 collective-permute-done.9
  181.0 3.8 fusion.19
  184.8 4.2 fusion.18
  189.0 4.3 %fusion.17 = f32[512,512]{0,1:T(8,128)} fusion(f32[512,512]{0,1:T(8,128)} %fusion.18), kind=kOutput, calls=%fused_computation.43 | convolution fusion | flops 538443776 | bytes 2097152 | tf_op jit(solution)/shard_map/dot_general | solution.py:30
  193.3 4.2 fusion.16
  197.5 4.1 fusion.26
  204.8 8.2 %collective-permute-start.15 = (bf16[2048,256]{0,1:T(8,128)(2,1)S(1)}, bf16[2048,256]{0,1:T(8,128)(2,1)S(1)}, u32[]{:S(2)}, u32[]{:S(2)}) collective-permute-start(bf16[2048,256]{0,1:T(8,128)(2,1)S(1)} %convolution_convert_fusion), channel_id=1, source_target_pairs={{1,6},{3,0},{5,2},{7,4},{9,14},{11,8},{13,10},{15,12},{17,22},{19,... | collective-permute-start | bytes 3145736 | tf_op jit(solution)/shard_map/ppermute | solution.py:96
  215.8 14.1 %collective-permute-done.13 = bf16[2048,256]{0,1:T(8,128)(2,1)S(1)} collective-permute-done((bf16[2048,256]{0,1:T(8,128)(2,1)S(1)}, bf16[2048,256]{0,1:T(8,128)(2,1)S(1)}, u32[]{:S(2)}, u32[]{:S(2)}) %collective-permute-start.13) | collective-permute-done | bytes 1048608 | tf_op jit(solution)/shard_map/ppermute | solution.py:94
  229.9 45.9 %collective-permute-start.14 = (bf16[2048,256]{0,1:T(8,128)(2,1)S(1)}, bf16[2048,256]{0,1:T(8,128)(2,1)S(1)}, u32[]{:S(2)}, u32[]{:S(2)}) collective-permute-start(bf16[2048,256]{0,1:T(8,128)(2,1)S(1)} %collective-permute-done.13), channel_id=1, source_target_pairs={{1,5},{3,7},{5,1},{7,3},{9,13},{11,15},{13,9},{15,11},{17,21},{19,... | collective-permute-start | bytes 3145736 | tf_op jit(solution)/shard_map/ppermute | solution.py:98
  279.6 45.9 %collective-permute-done.14 = bf16[2048,256]{0,1:T(8,128)(2,1)S(1)} collective-permute-done((bf16[2048,256]{0,1:T(8,128)(2,1)S(1)}, bf16[2048,256]{0,1:T(8,128)(2,1)S(1)}, u32[]{:S(2)}, u32[]{:S(2)}) %collective-permute-start.14) | collective-permute-done | bytes 1048608 | tf_op jit(solution)/shard_map/ppermute | solution.py:98
  326.9 22.4 %collective-permute-done.10 = bf16[2048,256]{0,1:T(8,128)(2,1)S(1)} collective-permute-done((bf16[2048,256]{0,1:T(8,128)(2,1)S(1)}, bf16[2048,256]{0,1:T(8,128)(2,1)S(1)}, u32[]{:S(2)}, u32[]{:S(2)}) %collective-permute-start.10) | collective-permute-done | bytes 1048608 | tf_op jit(solution)/shard_map/ppermute | solution.py:95
  349.3 63.6 %maximum_maximum_fusion = bf16[8192,512]{0,1:T(8,128)(2,1)} fusion(bf16[2048,256]{0,1:T(8,128)(2,1)S(1)} %broadcast_select_fusion, bf16[2048,256]{0,1:T(8,128)(2,1)S(1)} %collective-permute-done.12, bf16[2048,256]{0,1:T(8,128)(2,1)S(1)} %collective-permute-done.11, bf16[2048,256]{0,1:T(8,128)(2,1)S(1)} %collective-permute-done.10, ...), kind=kLoop, calls=%fused_computation | loop fusion | flops 67108864 | bytes 16777216 | tf_op jit(solution)/shard_map/concatenate | solution.py:100
  412.9 11.9 %copy.23 = bf16[8192,512]{1,0:T(8,128)(2,1)} copy(bf16[8192,512]{0,1:T(8,128)(2,1)} %maximum_maximum_fusion) | data formatting | bytes 16777216 | tf_op jit(solution)/shard_map/concatenate | solution.py:100
  (84 shorter events, 35.7 us)
Async XLA Ops:
  4.8 1.4 collective-permute-start
  6.2 5.6 %collective-permute-start.1 = (bf16[256,256]{1,0:T(8,128)(2,1)S(1)}, bf16[256,256]{1,0:T(8,128)(2,1)S(1)}, u32[]{:S(2)}, u32[]{:S(2)}) collective-permute-start(bf16[256,256]{1,0:T(8,128)(2,1)S(1)} %add_convert_fusion.1), channel_id=1, source_target_pairs={{0,16},{8,24},{16,0},{24,8},{1,17},{9,25},{17,1},{25,9},{2,18},{10... | collective-permute-start | bytes 393224 | tf_op jit(solution)/shard_map/ppermute | solution.py:41
  17.8 16.8 %slice-start = ((s8[8388608]{0:T(1024)(128)(4,1)}), s8[4194304]{0:T(1024)(128)(4,1)S(1)}, s32[]{:S(2)}) async-start(s8[8388608]{0:T(1024)(128)(4,1)} %bitcast.50), calls=%async_computation | async-start | bytes 8388608
  22.7 11.9 %slice-start.1 = ((s8[8388608]{0:T(1024)(128)(4,1)}), s8[4194304]{0:T(1024)(128)(4,1)S(1)}, s32[]{:S(2)}) async-start(s8[8388608]{0:T(1024)(128)(4,1)} %bitcast.50), calls=%async_computation.1 | async-start | bytes 8388608
  25.2 27.4 %collective-permute-start.5 = (bf16[2048,256]{0,1:T(8,128)(2,1)S(1)}, bf16[2048,256]{0,1:T(8,128)(2,1)S(1)}, u32[]{:S(2)}, u32[]{:S(2)}) collective-permute-start(bf16[2048,256]{0,1:T(8,128)(2,1)S(1)} %fusion.6), channel_id=1, source_target_pairs={{0,1},{2,3},{4,5},{6,7},{8,9},{10,11},{12,13},{14,15},{16,17},{18,... | collective-permute-start | bytes 3145736 | tf_op jit(solution)/shard_map/ppermute | solution.py:94
  28.8 95.7 %collective-permute-start.3 = (bf16[2048,256]{0,1:T(8,128)(2,1)S(1)}, bf16[2048,256]{0,1:T(8,128)(2,1)S(1)}, u32[]{:S(2)}, u32[]{:S(2)}) collective-permute-start(bf16[2048,256]{0,1:T(8,128)(2,1)S(1)} %fusion.4), channel_id=1, source_target_pairs={{0,5},{1,6},{2,7},{3,0},{4,1},{5,2},{6,3},{7,4},{8,13},{9,14},{10,... | collective-permute-start | bytes 3145736 | tf_op jit(solution)/shard_map/ppermute | solution.py:95
  35.3 111.7 %collective-permute-start.4 = (bf16[2048,256]{0,1:T(8,128)(2,1)S(1)}, bf16[2048,256]{0,1:T(8,128)(2,1)S(1)}, u32[]{:S(2)}, u32[]{:S(2)}) collective-permute-start(bf16[2048,256]{0,1:T(8,128)(2,1)S(1)} %fusion.5), channel_id=1, source_target_pairs={{0,5},{1,6},{2,7},{3,0},{4,1},{5,2},{6,3},{7,4},{8,13},{9,14},{10,... | collective-permute-start | bytes 3145736 | tf_op jit(solution)/shard_map/ppermute | solution.py:95
  36.2 132.6 %collective-permute-start.7 = (bf16[2048,256]{0,1:T(8,128)(2,1)S(1)}, bf16[2048,256]{0,1:T(8,128)(2,1)S(1)}, u32[]{:S(2)}, u32[]{:S(2)}) collective-permute-start(bf16[2048,256]{0,1:T(8,128)(2,1)S(1)} %fusion.6), channel_id=1, source_target_pairs={{1,6},{3,0},{5,2},{7,4},{9,14},{11,8},{13,10},{15,12},{17,22},{19,... | collective-permute-start | bytes 3145736 | tf_op jit(solution)/shard_map/ppermute | solution.py:96
  39.8 128.5 %collective-permute-start.2 = (bf16[2048,256]{0,1:T(8,128)(2,1)S(1)}, bf16[2048,256]{0,1:T(8,128)(2,1)S(1)}, u32[]{:S(2)}, u32[]{:S(2)}) collective-permute-start(bf16[2048,256]{0,1:T(8,128)(2,1)S(1)} %fusion.3), channel_id=1, source_target_pairs={{0,5},{1,6},{2,7},{3,0},{4,1},{5,2},{6,3},{7,4},{8,13},{9,14},{10,... | collective-permute-start | bytes 3145736 | tf_op jit(solution)/shard_map/ppermute | solution.py:95
  40.6 106.9 %copy-start.4 = (bf16[256,2048]{1,0:T(8,128)(2,1)}, bf16[256,2048]{1,0:T(8,128)(2,1)S(1)}, u32[]{:S(2)}) copy-start(bf16[256,2048]{1,0:T(8,128)(2,1)S(1)} %convolution_convert_fusion.13) | copy-start | bytes 3145732
  52.6 116.2 %collective-permute-start.6 = (bf16[2048,256]{0,1:T(8,128)(2,1)S(1)}, bf16[2048,256]{0,1:T(8,128)(2,1)S(1)}, u32[]{:S(2)}, u32[]{:S(2)}) collective-permute-start(bf16[2048,256]{0,1:T(8,128)(2,1)S(1)} %collective-permute-done.5), channel_id=1, source_target_pairs={{1,5},{3,7},{5,1},{7,3},{9,13},{11,15},{13,9},{15,11},{17,21},{19,... | collective-permute-start | bytes 3145736 | tf_op jit(solution)/shard_map/ppermute | solution.py:98
  124.3 44.7 %copy-start.8 = (bf16[256,2048]{1,0:T(8,128)(2,1)}, bf16[256,2048]{1,0:T(8,128)(2,1)S(1)}, u32[]{:S(2)}) copy-start(bf16[256,2048]{1,0:T(8,128)(2,1)S(1)} %convolution_convert_fusion.15) | copy-start | bytes 3145732
  124.5 44.4 %copy-start = (bf16[2048,256]{0,1:T(8,128)(2,1)}, bf16[2048,256]{0,1:T(8,128)(2,1)S(1)}, u32[]{:S(2)}) copy-start(bf16[2048,256]{0,1:T(8,128)(2,1)S(1)} %collective-permute-done.3) | copy-start | bytes 3145732
  147.0 21.9 %copy-start.2 = (bf16[2048,256]{0,1:T(8,128)(2,1)}, bf16[2048,256]{0,1:T(8,128)(2,1)S(1)}, u32[]{:S(2)}) copy-start(bf16[2048,256]{0,1:T(8,128)(2,1)S(1)} %collective-permute-done.4) | copy-start | bytes 3145732
  169.4 1.4 collective-permute-start.8
  170.9 5.6 %collective-permute-start.9 = (bf16[256,256]{1,0:T(8,128)(2,1)S(1)}, bf16[256,256]{1,0:T(8,128)(2,1)S(1)}, u32[]{:S(2)}, u32[]{:S(2)}) collective-permute-start(bf16[256,256]{1,0:T(8,128)(2,1)S(1)} %add_convert_fusion), channel_id=1, source_target_pairs={{0,16},{8,24},{16,0},{24,8},{1,17},{9,25},{17,1},{25,9},{2,18},{10... | collective-permute-start | bytes 393224 | tf_op jit(solution)/shard_map/ppermute | solution.py:41
  203.5 26.4 %collective-permute-start.13 = (bf16[2048,256]{0,1:T(8,128)(2,1)S(1)}, bf16[2048,256]{0,1:T(8,128)(2,1)S(1)}, u32[]{:S(2)}, u32[]{:S(2)}) collective-permute-start(bf16[2048,256]{0,1:T(8,128)(2,1)S(1)} %convolution_convert_fusion), channel_id=1, source_target_pairs={{0,1},{2,3},{4,5},{6,7},{8,9},{10,11},{12,13},{14,15},{16,17},{18,... | collective-permute-start | bytes 3145736 | tf_op jit(solution)/shard_map/ppermute | solution.py:94
  204.8 74.8 %collective-permute-start.15 = (bf16[2048,256]{0,1:T(8,128)(2,1)S(1)}, bf16[2048,256]{0,1:T(8,128)(2,1)S(1)}, u32[]{:S(2)}, u32[]{:S(2)}) collective-permute-start(bf16[2048,256]{0,1:T(8,128)(2,1)S(1)} %convolution_convert_fusion), channel_id=1, source_target_pairs={{1,6},{3,0},{5,2},{7,4},{9,14},{11,8},{13,10},{15,12},{17,22},{19,... | collective-permute-start | bytes 3145736 | tf_op jit(solution)/shard_map/ppermute | solution.py:96
  213.0 62.9 %copy-start.7 = (bf16[2048,256]{0,1:T(8,128)(2,1)S(1)}, bf16[2048,256]{0,1:T(8,128)(2,1)}, u32[]{:S(2)}) copy-start(bf16[2048,256]{0,1:T(8,128)(2,1)} %copy-done.6) | copy-start | bytes 3145732
  213.0 62.9 %copy-start.9 = (bf16[256,2048]{1,0:T(8,128)(2,1)S(1)}, bf16[256,2048]{1,0:T(8,128)(2,1)}, u32[]{:S(2)}) copy-start(bf16[256,2048]{1,0:T(8,128)(2,1)} %copy-done.8) | copy-start | bytes 3145732
  213.8 111.9 %collective-permute-start.12 = (bf16[2048,256]{0,1:T(8,128)(2,1)S(1)}, bf16[2048,256]{0,1:T(8,128)(2,1)S(1)}, u32[]{:S(2)}, u32[]{:S(2)}) collective-permute-start(bf16[2048,256]{0,1:T(8,128)(2,1)S(1)} %convolution_convert_fusion.1), channel_id=1, source_target_pairs={{0,5},{1,6},{2,7},{3,0},{4,1},{5,2},{6,3},{7,4},{8,13},{9,14},{10,... | collective-permute-start | bytes 3145736 | tf_op jit(solution)/shard_map/ppermute | solution.py:95
  214.6 112.3 %collective-permute-start.11 = (bf16[2048,256]{0,1:T(8,128)(2,1)S(1)}, bf16[2048,256]{0,1:T(8,128)(2,1)S(1)}, u32[]{:S(2)}, u32[]{:S(2)}) collective-permute-start(bf16[2048,256]{0,1:T(8,128)(2,1)S(1)} %convolution_convert_fusion.2), channel_id=1, source_target_pairs={{0,5},{1,6},{2,7},{3,0},{4,1},{5,2},{6,3},{7,4},{8,13},{9,14},{10,... | collective-permute-start | bytes 3145736 | tf_op jit(solution)/shard_map/ppermute | solution.py:95
  229.9 95.6 %collective-permute-start.14 = (bf16[2048,256]{0,1:T(8,128)(2,1)S(1)}, bf16[2048,256]{0,1:T(8,128)(2,1)S(1)}, u32[]{:S(2)}, u32[]{:S(2)}) collective-permute-start(bf16[2048,256]{0,1:T(8,128)(2,1)S(1)} %collective-permute-done.13), channel_id=1, source_target_pairs={{1,5},{3,7},{5,1},{7,3},{9,13},{11,15},{13,9},{15,11},{17,21},{19,... | collective-permute-start | bytes 3145736 | tf_op jit(solution)/shard_map/ppermute | solution.py:98
  276.6 72.7 %collective-permute-start.10 = (bf16[2048,256]{0,1:T(8,128)(2,1)S(1)}, bf16[2048,256]{0,1:T(8,128)(2,1)S(1)}, u32[]{:S(2)}, u32[]{:S(2)}) collective-permute-start(bf16[2048,256]{0,1:T(8,128)(2,1)S(1)} %convolution_convert_fusion.3), channel_id=1, source_target_pairs={{0,5},{1,6},{2,7},{3,0},{4,1},{5,2},{6,3},{7,4},{8,13},{9,14},{10,... | collective-permute-start | bytes 3145736 | tf_op jit(solution)/shard_map/ppermute | solution.py:95
  (6 other events, 43.1 us)

commit v2 on v1

v2 whole, which is shorter than its diff:
```python
import functools

import jax
import jax.numpy as jnp
from jax import lax
from jax.experimental import pallas as pl
from jax.experimental.pallas import tpu as pltpu
from jax.sharding import PartitionSpec as P

ROUNDS = 2
POLAR_STEPS = 5
CHUNKS = 4
TILE = 1024
VMEM_LIMIT = 32 * 1024 * 1024


coupling = 2.0
start_scale = 6.0


def rotation_kernel(selector, mine, other, moving, keeping, iterate):
    width = mine.shape[0]
    gram = mine[...].astype(jnp.float32) + other[...].astype(jnp.float32)
    frobenius = jnp.sqrt(jnp.sum(gram * gram, keepdims=True) + 1e-06)
    coupled = coupling * gram / frobenius
    row = lax.broadcasted_iota(jnp.int32, (width, width), 0)
    column = lax.broadcasted_iota(jnp.int32, (width, width), 1)
    diagonal = (row == column).astype(jnp.float32) / start_scale
    iterate[:width, :width] = diagonal
    iterate[width:, width:] = diagonal
    iterate[:width, width:] = -coupled / start_scale
    iterate[width:, :width] = coupled.T / start_scale

    def step(_, carry):
        current = iterate[...]
        rounded = current.astype(jnp.bfloat16)
        square = lax.dot_general(
            rounded, rounded, (((0,), (0,)), ((), ())), preferred_element_type=jnp.float32
        ).astype(jnp.bfloat16)
        iterate[...] = 1.5 * current - 0.5 * jnp.dot(
            rounded, square, preferred_element_type=jnp.float32
        )
        return carry

    lax.fori_loop(0, POLAR_STEPS, step, 0)
    first = iterate[:, :width].astype(jnp.bfloat16)
    second = iterate[:, width:].astype(jnp.bfloat16)
    second_stays = selector[0] == 1

    @pl.when(second_stays)
    def _():
        moving[...] = first
        keeping[...] = second

    @pl.when(jnp.logical_not(second_stays))
    def _():
        moving[...] = second
        keeping[...] = first


def rotation_columns(selector, mine, other):
    width = mine.shape[0]
    columns = jax.ShapeDtypeStruct((2 * width, width), jnp.bfloat16)
    vmem = pl.BlockSpec(memory_space=pltpu.VMEM)
    return pl.pallas_call(
        rotation_kernel,
        out_shape=(columns, columns),
        in_specs=[pl.BlockSpec(memory_space=pltpu.SMEM), vmem, vmem],
        out_specs=(vmem, vmem),
        scratch_shapes=[pltpu.VMEM((2 * width, 2 * width), jnp.float32)],
        compiler_params=pltpu.CompilerParams(vmem_limit_bytes=VMEM_LIMIT),
        cost_estimate=pl.CostEstimate(
            flops=2 * 2 * POLAR_STEPS * (2 * width) ** 3, bytes_accessed=10 * width**2, transcendentals=0
        ),
    )(selector, mine, other)


def place_rotated_kernel(kept, arrived, columns, *rest):
    out = rest[-1]
    width = kept.shape[1]
    out[...] = (
        jnp.dot(kept[...], columns[:width], preferred_element_type=jnp.float32)
        + jnp.dot(arrived[...], columns[width:], preferred_element_type=jnp.float32)
    ).astype(out.dtype)


def place_rotated(kept, arrived, columns, out, chunk):
    rows, width = arrived.shape
    tile = min(TILE, rows)
    first = chunk * (rows // tile)
    before = [] if out is None else [out]
    return pl.pallas_call(
        place_rotated_kernel,
        grid=(rows // tile,),
        out_shape=jax.ShapeDtypeStruct((kept.shape[0], 2 * width), kept.dtype),
        in_specs=[
            pl.BlockSpec((tile, width), lambda i: (i + first, 0)),
            pl.BlockSpec((tile, width), lambda i: (i, 0)),
            pl.BlockSpec((2 * width, width), lambda i: (0, 0)),
        ]
        + [pl.BlockSpec(memory_space=pl.ANY)] * len(before),
        out_specs=pl.BlockSpec((tile, width), lambda i: (i + first, 0)),
        input_output_aliases={3: 0} if before else {},
        compiler_params=pltpu.CompilerParams(vmem_limit_bytes=VMEM_LIMIT),
        cost_estimate=pl.CostEstimate(
            flops=4 * rows * width**2, bytes_accessed=6 * rows * width, transcendentals=0
        ),
    )(kept, arrived, columns, *before)


def place_kernel(block, _, out):
    out[...] = block[...]


def place_either_kernel(pick, one, other, _, out):
    out[...] = jnp.where(pick[0] == 1, one[...], other[...])


def place(blocks, out, chunk, pick=None):
    rows, width = blocks[0].shape
    tile = min(TILE, rows)
    first = chunk * (rows // tile)
    block = pl.BlockSpec((tile, width), lambda i: (i, 0))
    ahead = [] if pick is None else [pick]
    return pl.pallas_call(
        place_kernel if pick is None else place_either_kernel,
        grid=(rows // tile,),
        out_shape=jax.ShapeDtypeStruct(out.shape, out.dtype),
        in_specs=[pl.BlockSpec(memory_space=pltpu.SMEM)] * len(ahead)
        + [block] * len(blocks)
        + [pl.BlockSpec(memory_space=pl.ANY)],
        out_specs=pl.BlockSpec((tile, width), lambda i: (i + first, 1)),
        input_output_aliases={len(ahead) + len(blocks): 0},
        compiler_params=pltpu.CompilerParams(vmem_limit_bytes=VMEM_LIMIT),
        cost_estimate=pl.CostEstimate(flops=0, bytes_accessed=4 * rows * width, transcendentals=0),
    )(*ahead, *blocks, out)


def summed(value):
    length = lax.axis_size("samp")
    total = value.astype(jnp.bfloat16)
    if length & (length - 1):
        return lax.psum(total, "samp"), jnp.zeros_like(total)
    other = jnp.zeros_like(total)
    step = 1
    while step < length:
        if step > 1:
            total = (total.astype(jnp.float32) + other.astype(jnp.float32)).astype(jnp.bfloat16)
        other = lax.ppermute(total, "samp", [(i, i ^ step) for i in range(length)])
        step *= 2
    return total, other


def cross(first, second):
    return lax.dot_general(
        first, second, (((0,), (0,)), ((), ())), preferred_element_type=jnp.float32
    )


def shards(matrix, tournament):
    cycle_size = lax.axis_size("pair")
    half_cycle = cycle_size // 2
    position = lax.axis_index("pair")
    odd = (position % 2).astype(jnp.int32)
    rows, width = matrix.shape[0], matrix.shape[1] // 2
    piece = rows // CHUNKS

    def target(p):
        return (p + half_cycle + 1) % cycle_size

    def chunk_of(array, i):
        return array[i * piece : (i + 1) * piece]

    everyone = [(p, target(p)) for p in range(cycle_size)]
    from_odd = [(p, target(p)) for p in range(1, cycle_size, 2)]
    to_neighbour = [(p, p + 1) for p in range(0, cycle_size, 2)]
    forward = [(p + 1, target(p)) for p in range(0, cycle_size, 2)]

    def times(part, columns):
        return jnp.dot(part, columns, preferred_element_type=jnp.float32).astype(jnp.bfloat16)

    def sent(parts, columns):
        last = times(parts[-1], columns)
        passed = lax.ppermute(last, "pair", to_neighbour)
        got = [lax.ppermute(times(part, columns), "pair", everyone) for part in parts[:-1]]
        near = lax.ppermute(last, "pair", from_odd)
        far = lax.ppermute(passed, "pair", forward)
        return got, far, near

    def selector(tourney):
        slot_index = (position + half_cycle * (tourney % 2)) % cycle_size
        return lax.dynamic_slice(tournament[tourney], (slot_index,), (1,))

    moving, keeping = rotation_columns(selector(0), *summed(cross(matrix[:, :width], matrix[:, width:])))
    got, far, near = sent([chunk_of(matrix, i) for i in range(CHUNKS)], moving)
    kept = times(matrix, keeping)
    arrived = got + [jnp.where(odd == 1, far, near)]

    gram = sum(cross(chunk_of(kept, i), arrived[i]) for i in range(CHUNKS))
    moving, keeping = rotation_columns(selector(1), *summed(gram))
    parts = [jnp.concatenate([chunk_of(kept, i), arrived[i]], axis=1) for i in range(CHUNKS)]
    got, far, near = sent(parts, moving)
    out = None
    for i in range(CHUNKS):
        out = place_rotated(kept, arrived[i], keeping, out, i)
    for i in range(CHUNKS - 1):
        out = place([got[i]], out, i)
    return place([far, near], out, CHUNKS - 1, odd[None])


def solution(mesh):
    placed = (P("samp", "pair"), P())
    return jax.shard_map(
        shards, mesh=mesh, in_specs=placed, out_specs=P("samp", "pair"), check_vma=False
    )
```

time: 426 us -> 326 us (0.77)
  other arithmetic: 68.2 us -> 0.18 us
  waiting for transfers between devices: 147 us -> 111 us
  matrix products: 49.9 us -> 25.4 us
  starting transfers between devices: 142 us -> 164 us
  Pallas kernels: 0 us -> 21.2 us
  local copies, waits for them, and re-layouts: 14.2 us -> 3.7 us
    concatenate x1 -> x0, other arithmetic: 63.6 us -> none  [shards(): return jnp.concatenate([kept, jnp.concatenate(arrived, axis=0)], axis=1)]
    ppermute x12, waiting for transfers between devices: 139 us -> 104 us  [the longest x6 81.7 us: sent(): lax.ppermute(times(part, columns), 'pair', everyone)]
    dot_general x10 -> x0, matrix products: 24.9 us -> none  [polar_rotation(): jnp.dot(rounded, square, preferred_element_type=jnp.float32)]
    ppermute x12, starting transfers between devices: 139 us -> 161 us  [the longest x2 138 us: sent(): far = lax.ppermute(passed, 'pair', forward)]
    pallas_call x0 -> x10, Pallas kernels: none -> 21.2 us  [the longest x2 10.4 us: rotation_columns(): pl.pallas_call(rotation_kernel, out_shape=(columns, columns), in_specs=[p...]
    concatenate x1 -> x0, local copies, waits for them, and re-layouts: 11.9 us -> none  [shards(): return jnp.concatenate([kept, jnp.concatenate(arrived, axis=0)], axis=1)]
    dot_general x16 -> x9, matrix products: 18.4 us -> 18.7 us  [times(): jnp.dot(part, columns, preferred_element_type=jnp.float32)]
  transfers between devices with their start and end apart: 16 -> 16, of which waited for: 12 -> 10; matrix products, arithmetic and copies ran while one was open for 3% -> 6% of each run, Pallas kernels for 0% -> 3%
where the time goes in v2:
time: 326 us; the launch traced here: 325 us
  starting transfers between devices  164 us (50%)
  waiting for transfers between devices  111 us (34%)
  matrix products  25.4 us (8%)
  Pallas kernels  21.2 us (7%)
  local copies, waits for them, and re-layouts  3.7 us (1%)
    ppermute x2, starting transfers between devices, sent(): far = lax.ppermute(passed, 'pair', forward)  138 us
    ppermute x6, waiting for transfers between devices, sent(): lax.ppermute(times(part, columns), 'pair', everyone)  81.7 us
    ppermute x2, waiting for transfers between devices, sent(): passed = lax.ppermute(last, 'pair', to_neighbour)  21.9 us
    dot_general x9, matrix products, times(): jnp.dot(part, columns, preferred_element_type=jnp.float32)  18.7 us
    ppermute x2, starting transfers between devices, sent(): near = lax.ppermute(last, 'pair', from_odd)  10.6 us
    pallas_call x2, Pallas kernels, rotation_columns(): pl.pallas_call(rotation_kernel, out_shape=(columns, columns), in_specs=[p...  10.4 us
    ppermute x6, starting transfers between devices, sent(): lax.ppermute(times(part, columns), 'pair', everyone)  9.44 us
    ppermute x4, waiting for transfers between devices, summed(): other = lax.ppermute(total, 'samp', [(i, i ^ step) for i in range(length)])  7.06 us
  transfers between devices with their start and end apart: 16, of which 10 were waited for; matrix products, arithmetic and copies ran while one was open for 6% of the time, Pallas kernels for 3%

profile of v2, /device:TPU:4, one launch (start us, length us, event | category | flops | bytes accessed | tf_op | source)
XLA Modules:
  0.0 325.5 jit_solution(16402452158725596933)
XLA Ops:
  0.0 4.8 %fusion.26 = bf16[256,256]{1,0:T(8,128)(2,1)S(1)} fusion(bf16[8192,512]{1,0:T(8,128)(2,1)} %param.2), kind=kOutput, calls=%fused_computation.37 | convolution fusion | flops 1073807360 | bytes 8519680 | tf_op jit(solution)/shard_map/dot_general | solution.py:155
  8.4 3.5 %collective-permute-done.1.other = bf16[256,256]{1,0:T(8,128)(2,1)S(1)} collective-permute-done((bf16[256,256]{1,0:T(8,128)(2,1)S(1)}, bf16[256,256]{1,0:T(8,128)(2,1)S(1)}, u32[]{:S(2)}, u32[]{:S(2)}) %collective-permute-start.1) | collective-permute-done | bytes 131104 | tf_op jit(solution)/shard_map/ppermute | solution.py:149
  11.8 5.2 %shard_map.28 = (bf16[512,256]{1,0:T(8,128)(2,1)S(1)}, bf16[512,256]{1,0:T(8,128)(2,1)S(1)}) custom-call(s32[1]{0:T(128)} %bitcast.1.selector, bf16[256,256]{1,0:T(8,128)(2,1)S(1)} %add_convert_fusion.1.mine, bf16[256,256]{1,0:T(8,128)(2,1)S(1)} %collective-permute-done.1.other), custom_call_target="tpu_custom_call" | custom-call | flops 2684354560 | bytes 655360 | tf_op jit(solution)/shard_map/pallas_call | solution.py:65
  17.1 3.3 %fusion.4 = bf16[2048,256]{1,0:T(8,128)(2,1)} fusion(bf16[512,256]{1,0:T(8,128)(2,1)S(1)} %get-tuple-element.10, bf16[8192,512]{1,0:T(8,128)(2,1)} %param.2), kind=kOutput, calls=%fused_computation.13 | convolution fusion | flops 537395200 | bytes 3407872 | tf_op jit(solution)/shard_map/dot_general | solution.py:180
  21.7 8.6 %collective-permute-start.4 = (bf16[2048,256]{1,0:T(8,128)(2,1)}, bf16[2048,256]{1,0:T(8,128)(2,1)S(1)}, u32[]{:S(2)}, u32[]{:S(2)}) collective-permute-start(bf16[2048,256]{1,0:T(8,128)(2,1)} %fusion.4), channel_id=1, source_target_pairs={{1,6},{3,0},{5,2},{7,4},{9,14},{11,8},{13,10},{15,12},{17,22},{19,... | collective-permute-start | bytes 3145736 | tf_op jit(solution)/shard_map/ppermute | solution.py:186
  30.3 2.3 fusion.6
  32.6 2.3 fusion.7
  34.9 1.7 collective-permute-start.7
  36.7 2.3 fusion.5
  39.0 8.0 %collective-permute-done.2 = bf16[2048,256]{1,0:T(8,128)(2,1)} collective-permute-done((bf16[2048,256]{1,0:T(8,128)(2,1)}, bf16[2048,256]{1,0:T(8,128)(2,1)}, u32[]{:S(2)}, u32[]{:S(2)}) %collective-permute-start.2) | collective-permute-done | bytes 1048608 | tf_op jit(solution)/shard_map/ppermute | solution.py:184
  47.0 71.8 %collective-permute-start.3 = (bf16[2048,256]{1,0:T(8,128)(2,1)}, bf16[2048,256]{1,0:T(8,128)(2,1)S(1)}, u32[]{:S(2)}, u32[]{:S(2)}) collective-permute-start(bf16[2048,256]{1,0:T(8,128)(2,1)} %collective-permute-done.2), channel_id=1, source_target_pairs={{1,5},{3,7},{5,1},{7,3},{9,13},{11,15},{13,9},{15,11},{17,21},{19,... | collective-permute-start | bytes 3145736 | tf_op jit(solution)/shard_map/ppermute | solution.py:187
  118.8 5.7 %fusion.kept = bf16[8192,256]{1,0:T(8,128)(2,1)S(1)} fusion(bf16[8192,512]{1,0:T(8,128)(2,1)} %param.2, bf16[512,256]{1,0:T(8,128)(2,1)S(1)} %get-tuple-element.9), kind=kOutput, calls=%fused_computation.1 | convolution fusion | flops 2149580800 | bytes 12845056 | tf_op jit(solution)/shard_map/dot_general | solution.py:180
  125.1 21.1 %collective-permute-done.7.arrived = bf16[2048,256]{1,0:T(8,128)(2,1)S(1)} collective-permute-done((bf16[2048,256]{1,0:T(8,128)(2,1)S(1)}, bf16[2048,256]{1,0:T(8,128)(2,1)S(1)}, u32[]{:S(2)}, u32[]{:S(2)}) %collective-permute-start.7) | collective-permute-done | bytes 1048608 | tf_op jit(solution)/shard_map/ppermute | solution.py:185
  146.6 21.9 %collective-permute-done.5.arrived = bf16[2048,256]{1,0:T(8,128)(2,1)S(1)} collective-permute-done((bf16[2048,256]{1,0:T(8,128)(2,1)S(1)}, bf16[2048,256]{1,0:T(8,128)(2,1)S(1)}, u32[]{:S(2)}, u32[]{:S(2)}) %collective-permute-start.5) | collective-permute-done | bytes 1048608 | tf_op jit(solution)/shard_map/ppermute | solution.py:185
  172.7 2.4 fusion.41
  176.7 5.2 %shard_map.29 = (bf16[512,256]{1,0:T(8,128)(2,1)S(1)}, bf16[512,256]{1,0:T(8,128)(2,1)S(1)}) custom-call(s32[1]{0:T(128)} %bitcast.4.selector, bf16[256,256]{1,0:T(8,128)(2,1)S(1)} %add_convert_fusion.mine, bf16[256,256]{1,0:T(8,128)(2,1)S(1)} %collective-permute-done.9.other), custom_call_target="tpu_custom_call" | custom-call | flops 2684354560 | bytes 655360 | tf_op jit(solution)/shard_map/pallas_call | solution.py:65
  184.8 4.6 %collective-permute-start.15 = (bf16[2048,256]{1,0:T(8,128)(2,1)S(1)}, bf16[2048,256]{1,0:T(8,128)(2,1)S(1)}, u32[]{:S(2)}, u32[]{:S(2)}) collective-permute-start(bf16[2048,256]{1,0:T(8,128)(2,1)S(1)} %convolution_convert_fusion.5), channel_id=1, source_target_pairs={{0,5},{1,6},{2,7},{3,0},{4,1},{5,2},{6,3},{7,4},{8,13},{9,14},{10,... | collective-permute-start | bytes 3145736 | tf_op jit(solution)/shard_map/ppermute | solution.py:185
  191.0 2.9 collective-permute-start.13
  193.9 2.0 collective-permute-start.12
  195.8 13.9 %collective-permute-done.10 = bf16[2048,256]{1,0:T(8,128)(2,1)S(1)} collective-permute-done((bf16[2048,256]{1,0:T(8,128)(2,1)S(1)}, bf16[2048,256]{1,0:T(8,128)(2,1)S(1)}, u32[]{:S(2)}, u32[]{:S(2)}) %collective-permute-start.10) | collective-permute-done | bytes 1048608 | tf_op jit(solution)/shard_map/ppermute | solution.py:184
  209.8 66.2 %collective-permute-start.11 = (bf16[2048,256]{1,0:T(8,128)(2,1)S(1)}, bf16[2048,256]{1,0:T(8,128)(2,1)S(1)}, u32[]{:S(2)}, u32[]{:S(2)}) collective-permute-start(bf16[2048,256]{1,0:T(8,128)(2,1)S(1)} %collective-permute-done.10), channel_id=1, source_target_pairs={{1,5},{3,7},{5,1},{7,3},{9,13},{11,15},{13,9},{15,11},{17,21},{19,... | collective-permute-start | bytes 3145736 | tf_op jit(solution)/shard_map/ppermute | solution.py:187
  276.0 1.7 shard_map.30.rest_0_
  283.7 18.2 %collective-permute-done.14.block = bf16[2048,256]{1,0:T(8,128)(2,1)S(1)} collective-permute-done((bf16[2048,256]{1,0:T(8,128)(2,1)S(1)}, bf16[2048,256]{1,0:T(8,128)(2,1)S(1)}, u32[]{:S(2)}, u32[]{:S(2)}) %collective-permute-start.14) | collective-permute-done | bytes 1048608 | tf_op jit(solution)/shard_map/ppermute | solution.py:185
  302.9 20.6 %collective-permute-done.13.block = bf16[2048,256]{1,0:T(8,128)(2,1)S(1)} collective-permute-done((bf16[2048,256]{1,0:T(8,128)(2,1)S(1)}, bf16[2048,256]{1,0:T(8,128)(2,1)S(1)}, u32[]{:S(2)}, u32[]{:S(2)}) %collective-permute-start.13) | collective-permute-done | bytes 1048608 | tf_op jit(solution)/shard_map/ppermute | solution.py:185
  (49 shorter events, 25.1 us)
Async XLA Ops:
  0.0 7.8 %copy-start.4 = (s32[2,8]{1,0:T(2,128)S(1)}, s32[2,8]{1,0:T(2,128)}, u32[]{:S(2)}) copy-start(s32[2,8]{1,0:T(2,128)} %param.3) | copy-start | bytes 196
  4.8 1.4 collective-permute-start
  6.2 5.6 %collective-permute-start.1 = (bf16[256,256]{1,0:T(8,128)(2,1)S(1)}, bf16[256,256]{1,0:T(8,128)(2,1)S(1)}, u32[]{:S(2)}, u32[]{:S(2)}) collective-permute-start(bf16[256,256]{1,0:T(8,128)(2,1)S(1)} %add_convert_fusion.1.mine), channel_id=1, source_target_pairs={{0,16},{8,24},{16,0},{24,8},{1,17},{9,25},{17,1},{25,9},{2,18},{10... | collective-permute-start | bytes 393224 | tf_op jit(solution)/shard_map/ppermute | solution.py:149
  20.4 26.7 %collective-permute-start.2 = (bf16[2048,256]{1,0:T(8,128)(2,1)}, bf16[2048,256]{1,0:T(8,128)(2,1)}, u32[]{:S(2)}, u32[]{:S(2)}) collective-permute-start(bf16[2048,256]{1,0:T(8,128)(2,1)} %fusion.4), channel_id=1, source_target_pairs={{0,1},{2,3},{4,5},{6,7},{8,9},{10,11},{12,13},{14,15},{16,17},{18,... | collective-permute-start | bytes 3145736 | tf_op jit(solution)/shard_map/ppermute | solution.py:184
  21.7 147.3 %collective-permute-start.4 = (bf16[2048,256]{1,0:T(8,128)(2,1)}, bf16[2048,256]{1,0:T(8,128)(2,1)S(1)}, u32[]{:S(2)}, u32[]{:S(2)}) collective-permute-start(bf16[2048,256]{1,0:T(8,128)(2,1)} %fusion.4), channel_id=1, source_target_pairs={{1,6},{3,0},{5,2},{7,4},{9,14},{11,8},{13,10},{15,12},{17,22},{19,... | collective-permute-start | bytes 3145736 | tf_op jit(solution)/shard_map/ppermute | solution.py:186
  32.6 92.0 %collective-permute-start.6 = (bf16[2048,256]{1,0:T(8,128)(2,1)S(1)}, bf16[2048,256]{1,0:T(8,128)(2,1)S(1)}, u32[]{:S(2)}, u32[]{:S(2)}) collective-permute-start(bf16[2048,256]{1,0:T(8,128)(2,1)S(1)} %fusion.6), channel_id=1, source_target_pairs={{0,5},{1,6},{2,7},{3,0},{4,1},{5,2},{6,3},{7,4},{8,13},{9,14},{10,... | collective-permute-start | bytes 3145736 | tf_op jit(solution)/shard_map/ppermute | solution.py:185
  34.9 111.2 %collective-permute-start.7 = (bf16[2048,256]{1,0:T(8,128)(2,1)S(1)}, bf16[2048,256]{1,0:T(8,128)(2,1)S(1)}, u32[]{:S(2)}, u32[]{:S(2)}) collective-permute-start(bf16[2048,256]{1,0:T(8,128)(2,1)S(1)} %fusion.7), channel_id=1, source_target_pairs={{0,5},{1,6},{2,7},{3,0},{4,1},{5,2},{6,3},{7,4},{8,13},{9,14},{10,... | collective-permute-start | bytes 3145736 | tf_op jit(solution)/shard_map/ppermute | solution.py:185
  39.0 129.5 %collective-permute-start.5 = (bf16[2048,256]{1,0:T(8,128)(2,1)S(1)}, bf16[2048,256]{1,0:T(8,128)(2,1)S(1)}, u32[]{:S(2)}, u32[]{:S(2)}) collective-permute-start(bf16[2048,256]{1,0:T(8,128)(2,1)S(1)} %fusion.5), channel_id=1, source_target_pairs={{0,5},{1,6},{2,7},{3,0},{4,1},{5,2},{6,3},{7,4},{8,13},{9,14},{10,... | collective-permute-start | bytes 3145736 | tf_op jit(solution)/shard_map/ppermute | solution.py:185
  47.0 122.0 %collective-permute-start.3 = (bf16[2048,256]{1,0:T(8,128)(2,1)}, bf16[2048,256]{1,0:T(8,128)(2,1)S(1)}, u32[]{:S(2)}, u32[]{:S(2)}) collective-permute-start(bf16[2048,256]{1,0:T(8,128)(2,1)} %collective-permute-done.2), channel_id=1, source_target_pairs={{1,5},{3,7},{5,1},{7,3},{9,13},{11,15},{13,9},{15,11},{17,21},{19,... | collective-permute-start | bytes 3145736 | tf_op jit(solution)/shard_map/ppermute | solution.py:187
  124.6 44.6 %copy-start = (bf16[8192,256]{1,0:T(8,128)(2,1)}, bf16[8192,256]{1,0:T(8,128)(2,1)S(1)}, u32[]{:S(2)}) copy-start(bf16[8192,256]{1,0:T(8,128)(2,1)S(1)} %fusion.kept) | copy-start | bytes 12582916
  168.5 1.1 copy-start.2
  169.6 1.4 collective-permute-start.8
  171.1 5.6 %collective-permute-start.9 = (bf16[256,256]{1,0:T(8,128)(2,1)S(1)}, bf16[256,256]{1,0:T(8,128)(2,1)S(1)}, u32[]{:S(2)}, u32[]{:S(2)}) collective-permute-start(bf16[256,256]{1,0:T(8,128)(2,1)S(1)} %add_convert_fusion.mine), channel_id=1, source_target_pairs={{0,16},{8,24},{16,0},{24,8},{1,17},{9,25},{17,1},{25,9},{2,18},{10... | collective-permute-start | bytes 393224 | tf_op jit(solution)/shard_map/ppermute | solution.py:149
  181.9 2.2 copy-start.3
  182.6 27.1 %collective-permute-start.10 = (bf16[2048,256]{1,0:T(8,128)(2,1)S(1)}, bf16[2048,256]{1,0:T(8,128)(2,1)S(1)}, u32[]{:S(2)}, u32[]{:S(2)}) collective-permute-start(bf16[2048,256]{1,0:T(8,128)(2,1)S(1)} %convolution_convert_fusion.8), channel_id=1, source_target_pairs={{0,1},{2,3},{4,5},{6,7},{8,9},{10,11},{12,13},{14,15},{16,17},{18,... | collective-permute-start | bytes 3145736 | tf_op jit(solution)/shard_map/ppermute | solution.py:184
  184.8 97.9 %collective-permute-start.15 = (bf16[2048,256]{1,0:T(8,128)(2,1)S(1)}, bf16[2048,256]{1,0:T(8,128)(2,1)S(1)}, u32[]{:S(2)}, u32[]{:S(2)}) collective-permute-start(bf16[2048,256]{1,0:T(8,128)(2,1)S(1)} %convolution_convert_fusion.5), channel_id=1, source_target_pairs={{0,5},{1,6},{2,7},{3,0},{4,1},{5,2},{6,3},{7,4},{8,13},{9,14},{10,... | collective-permute-start | bytes 3145736 | tf_op jit(solution)/shard_map/ppermute | solution.py:185
  189.5 86.5 %copy-start.1 = (bf16[8192,256]{1,0:T(8,128)(2,1)S(1)}, bf16[8192,256]{1,0:T(8,128)(2,1)}, u32[]{:S(2)}) copy-start(bf16[8192,256]{1,0:T(8,128)(2,1)} %copy-done) | copy-start | bytes 12582916
  190.2 111.7 %collective-permute-start.14 = (bf16[2048,256]{1,0:T(8,128)(2,1)S(1)}, bf16[2048,256]{1,0:T(8,128)(2,1)S(1)}, u32[]{:S(2)}, u32[]{:S(2)}) collective-permute-start(bf16[2048,256]{1,0:T(8,128)(2,1)S(1)} %convolution_convert_fusion.6), channel_id=1, source_target_pairs={{0,5},{1,6},{2,7},{3,0},{4,1},{5,2},{6,3},{7,4},{8,13},{9,14},{10,... | collective-permute-start | bytes 3145736 | tf_op jit(solution)/shard_map/ppermute | solution.py:185
  191.0 132.5 %collective-permute-start.13 = (bf16[2048,256]{1,0:T(8,128)(2,1)S(1)}, bf16[2048,256]{1,0:T(8,128)(2,1)S(1)}, u32[]{:S(2)}, u32[]{:S(2)}) collective-permute-start(bf16[2048,256]{1,0:T(8,128)(2,1)S(1)} %convolution_convert_fusion.7), channel_id=1, source_target_pairs={{0,5},{1,6},{2,7},{3,0},{4,1},{5,2},{6,3},{7,4},{8,13},{9,14},{10,... | collective-permute-start | bytes 3145736 | tf_op jit(solution)/shard_map/ppermute | solution.py:185
  193.9 130.6 %collective-permute-start.12 = (bf16[2048,256]{1,0:T(8,128)(2,1)S(1)}, bf16[2048,256]{1,0:T(8,128)(2,1)S(1)}, u32[]{:S(2)}, u32[]{:S(2)}) collective-permute-start(bf16[2048,256]{1,0:T(8,128)(2,1)S(1)} %convolution_convert_fusion.8), channel_id=1, source_target_pairs={{1,6},{3,0},{5,2},{7,4},{9,14},{11,8},{13,10},{15,12},{17,22},{19,... | collective-permute-start | bytes 3145736 | tf_op jit(solution)/shard_map/ppermute | solution.py:186
  209.8 114.7 %collective-permute-start.11 = (bf16[2048,256]{1,0:T(8,128)(2,1)S(1)}, bf16[2048,256]{1,0:T(8,128)(2,1)S(1)}, u32[]{:S(2)}, u32[]{:S(2)}) collective-permute-start(bf16[2048,256]{1,0:T(8,128)(2,1)S(1)} %collective-permute-done.10), channel_id=1, source_target_pairs={{1,5},{3,7},{5,1},{7,3},{9,13},{11,15},{13,9},{15,11},{17,21},{19,... | collective-permute-start | bytes 3145736 | tf_op jit(solution)/shard_map/ppermute | solution.py:187

commit v3 on v2

v3 whole, which is shorter than its diff:
```python
import functools

import jax
import jax.numpy as jnp
from jax import lax
from jax.experimental import pallas as pl
from jax.experimental.pallas import tpu as pltpu
from jax.sharding import PartitionSpec as P

POLAR_STEPS = 5
TILE = 1024
VMEM_LIMIT = 48 * 1024 * 1024


coupling = 2.0
start_scale = 6.0

IN_VMEM = pl.BlockSpec(memory_space=pltpu.VMEM)
IN_SMEM = pl.BlockSpec(memory_space=pltpu.SMEM)
ANYWHERE = pl.BlockSpec(memory_space=pl.ANY)
IN_HBM = pl.BlockSpec(memory_space=pltpu.MemorySpace.HBM)


def reads_of(t, sources, starts, tile, block, arrivals):
    rows = pl.multiple_of(t * tile, tile)
    copies, at = [], 0
    for s, (source, start) in enumerate(zip(sources, starts)):
        span = source.shape[1]
        copies.append(
            pltpu.make_async_copy(
                source.at[pl.ds(pl.multiple_of(start + rows, tile), tile)],
                block.at[pl.ds(rows, tile), pl.ds(at, span)],
                arrivals.at[s, t],
            )
        )
        at += span
    return copies


def start_reads(sources, starts, tiles, tile, block, arrivals):
    def start(t, carry):
        for copy in reads_of(t, sources, starts, tile, block, arrivals):
            copy.start()
        return carry

    lax.fori_loop(0, tiles, start, 0)


def write_rotated(sources, starts, tiles, tile, block, arrivals, columns, rotated, out, first_row, departures):
    def write_of(t):
        rows = pl.multiple_of(t * tile, tile)
        return pltpu.make_async_copy(
            rotated.at[pl.ds(rows, tile)],
            out.at[pl.ds(pl.multiple_of(first_row + rows, tile), tile), pl.ds(0, rotated.shape[1])],
            departures.at[t],
        )

    def rotate(t, carry):
        for copy in reads_of(t, sources, starts, tile, block, arrivals):
            copy.wait()
        here = pl.ds(pl.multiple_of(t * tile, tile), tile)
        rotated[here, :] = jnp.dot(
            block[here, :], columns[...], preferred_element_type=jnp.float32
        ).astype(rotated.dtype)
        write_of(t).start()
        return carry

    def finish(t, carry):
        write_of(t).wait()
        return carry

    lax.fori_loop(0, tiles, rotate, 0)
    lax.fori_loop(0, tiles, finish, 0)


def polar_columns(selector, mine, other, moving, keeping, iterate):
    width = mine.shape[0]
    gram = mine[...].astype(jnp.float32) + other[...].astype(jnp.float32)
    frobenius = jnp.sqrt(jnp.sum(gram * gram, keepdims=True) + 1e-06)
    coupled = coupling * gram / frobenius
    row = lax.broadcasted_iota(jnp.int32, (width, width), 0)
    column = lax.broadcasted_iota(jnp.int32, (width, width), 1)
    diagonal = (row == column).astype(jnp.float32) / start_scale
    iterate[:width, :width] = diagonal
    iterate[width:, width:] = diagonal
    iterate[:width, width:] = -coupled / start_scale
    iterate[width:, :width] = coupled.T / start_scale

    def step(_, carry):
        current = iterate[...]
        rounded = current.astype(jnp.bfloat16)
        square = lax.dot_general(
            rounded, rounded, (((0,), (0,)), ((), ())), preferred_element_type=jnp.float32
        ).astype(jnp.bfloat16)
        iterate[...] = 1.5 * current - 0.5 * jnp.dot(
            rounded, square, preferred_element_type=jnp.float32
        )
        return carry

    lax.fori_loop(0, POLAR_STEPS, step, 0)
    first = iterate[:, :width].astype(jnp.bfloat16)
    second = iterate[:, width:].astype(jnp.bfloat16)
    second_stays = selector[0] == 1

    @pl.when(second_stays)
    def _():
        moving[...] = first
        keeping[...] = second

    @pl.when(jnp.logical_not(second_stays))
    def _():
        moving[...] = second
        keeping[...] = first


def rotation_kernel(tile, starts_of, *refs):
    selector, mine, other = refs[:3]
    counts = [len(starts) for starts in starts_of]
    parts = len(counts)
    tail = refs[3 + sum(counts) :]
    moving, keeping = tail[:2]
    outs, iterate, block, rotated = tail[2 : 2 + parts], tail[2 + parts], tail[3 + parts], tail[4 + parts]
    arrivals, departures = tail[5 + parts :]
    rows = outs[0].shape[0]
    tiles = rows // tile
    at, pieces = 3, []
    for k, count in enumerate(counts):
        here = pl.ds(k * rows, rows)
        pieces.append(
            (refs[at : at + count], starts_of[k], tiles, tile, block.at[here], arrivals.at[k])
        )
        at += count
    for piece in pieces:
        start_reads(*piece)
    polar_columns(selector, mine, other, moving, keeping, iterate)
    for k, (sources, starts, _, _, rows_of, arrived) in enumerate(pieces):
        write_rotated(
            sources, starts, tiles, tile, rows_of, arrived, moving,
            rotated.at[pl.ds(k * rows, rows)], outs[k], 0, departures.at[k],
        )


def rotation_of(selector, terms, parts, starts_of, rows, where):
    width = terms[0].shape[0]
    tile = min(TILE, rows)
    counts = [len(part) for part in parts]
    columns = jax.ShapeDtypeStruct((2 * width, width), jnp.bfloat16)
    moved = jax.ShapeDtypeStruct((rows, width), jnp.bfloat16)
    return pl.pallas_call(
        functools.partial(rotation_kernel, tile, starts_of),
        out_shape=[columns, columns] + [moved] * len(parts),
        in_specs=[IN_SMEM, IN_VMEM, IN_VMEM] + where,
        out_specs=[IN_VMEM, IN_VMEM] + [IN_HBM] * len(parts),
        scratch_shapes=[
            pltpu.VMEM((2 * width, 2 * width), jnp.float32),
            pltpu.VMEM((len(parts) * rows, 2 * width), jnp.bfloat16),
            pltpu.VMEM((len(parts) * rows, width), jnp.bfloat16),
            pltpu.SemaphoreType.DMA((len(parts), max(counts), rows // tile)),
            pltpu.SemaphoreType.DMA((len(parts), rows // tile)),
        ],
        compiler_params=pltpu.CompilerParams(vmem_limit_bytes=VMEM_LIMIT),
        cost_estimate=pl.CostEstimate(
            flops=2 * 2 * POLAR_STEPS * (2 * width) ** 3 + 4 * len(parts) * rows * width**2,
            bytes_accessed=10 * width**2 + 6 * len(parts) * rows * width,
            transcendentals=0,
        ),
    )(selector, *terms, *[source for part in parts for source in part])


def rotated_kernel(starts, tile, rows, first_row, *refs):
    columns, sources = refs[0], refs[1 : 1 + len(starts)]
    out, block, rotated, arrivals, departures = refs[-5:]
    tiles = rows // tile
    start_reads(sources, starts, tiles, tile, block, arrivals)
    write_rotated(
        sources, starts, tiles, tile, block, arrivals, columns, rotated, out, first_row, departures
    )


def rotated_rows(sources, starts, rows, columns, where, shape=None, out=None, first_row=0):
    width = columns.shape[1]
    tile = min(TILE, rows)
    before = [] if out is None else [out]
    return pl.pallas_call(
        functools.partial(rotated_kernel, starts, tile, rows, first_row),
        out_shape=jax.ShapeDtypeStruct(shape or (rows, width), columns.dtype),
        in_specs=[IN_VMEM] + where + [IN_HBM] * len(before),
        out_specs=IN_HBM,
        input_output_aliases={1 + len(sources): 0} if before else {},
        scratch_shapes=[
            pltpu.VMEM((rows, 2 * width), jnp.bfloat16),
            pltpu.VMEM((rows, width), jnp.bfloat16),
            pltpu.SemaphoreType.DMA((len(sources), rows // tile)),
            pltpu.SemaphoreType.DMA((rows // tile,)),
        ],
        compiler_params=pltpu.CompilerParams(vmem_limit_bytes=VMEM_LIMIT),
        cost_estimate=pl.CostEstimate(
            flops=4 * rows * width**2, bytes_accessed=6 * rows * width, transcendentals=0
        ),
    )(columns, *sources, *before)


def place_kernel(tile, first_row, wanted, source, _, *refs):
    out, block, arrivals, departures = refs[-4:]
    rows, width = source.shape

    @pl.when(wanted[0] == 1)
    def _():
        reads = [
            pltpu.make_async_copy(
                source.at[pl.ds(t * tile, tile)], block.at[pl.ds(t * tile, tile)], arrivals.at[t]
            )
            for t in range(rows // tile)
        ]
        writes = [
            pltpu.make_async_copy(
                block.at[pl.ds(t * tile, tile)],
                out.at[pl.ds(first_row + t * tile, tile), pl.ds(width, width)],
                departures.at[t],
            )
            for t in range(rows // tile)
        ]
        for read in reads:
            read.start()
        for read, write in zip(reads, writes):
            read.wait()
            write.start()
        for write in writes:
            write.wait()


def place(wanted, source, out, first_row, after=()):
    rows, width = source.shape
    tile = min(TILE, rows)
    return pl.pallas_call(
        functools.partial(place_kernel, tile, first_row),
        out_shape=jax.ShapeDtypeStruct(out.shape, out.dtype),
        in_specs=[IN_SMEM, ANYWHERE, IN_HBM] + [ANYWHERE] * len(after),
        out_specs=IN_HBM,
        input_output_aliases={2: 0},
        scratch_shapes=[
            pltpu.VMEM((rows, width), jnp.bfloat16),
            pltpu.SemaphoreType.DMA((rows // tile,)),
            pltpu.SemaphoreType.DMA((rows // tile,)),
        ],
        compiler_params=pltpu.CompilerParams(vmem_limit_bytes=VMEM_LIMIT),
        cost_estimate=pl.CostEstimate(flops=0, bytes_accessed=4 * rows * width, transcendentals=0),
    )(wanted, source, out, *after)


def summed(value, positions):
    length, cycle_size = lax.axis_size("samp"), lax.axis_size("pair")
    total = value.astype(jnp.bfloat16)
    if length & (length - 1):
        return lax.psum(total, "samp"), jnp.zeros_like(total)
    other = jnp.zeros_like(total)
    step = 1
    while step < length:
        if step > 1:
            total = (total.astype(jnp.float32) + other.astype(jnp.float32)).astype(jnp.bfloat16)
        pairs = [(i * cycle_size + p, (i ^ step) * cycle_size + p) for i in range(length) for p in positions]
        other = lax.ppermute(total, ("samp", "pair"), pairs)
        step *= 2
    return total, other


def cross(first, second):
    return lax.dot_general(
        first, second, (((0,), (0,)), ((), ())), preferred_element_type=jnp.float32
    )


def shards(matrix, tournament):
    cycle_size = lax.axis_size("pair")
    half_cycle = cycle_size // 2
    position = lax.axis_index("pair")
    rows, width = matrix.shape[0], matrix.shape[1] // 2
    half = rows // 2

    def target(p):
        return (p + half_cycle + 1) % cycle_size

    def among(positions):
        found = sum((position == p).astype(jnp.int32) for p in positions)
        return found.reshape((1,))

    def passed(value, pairs):
        return lax.ppermute(value, "pair", pairs)

    def selector(tourney):
        slot_index = (position + half_cycle * (tourney % 2)) % cycle_size
        return lax.dynamic_slice(tournament[tourney], (slot_index,), (1,))

    def sends(positions):
        return [(p, target(p)) for p in positions]

    whole = list(range(cycle_size))
    late = [half_cycle - 1, cycle_size - 1]
    to_late = [p for p in whole if target(p) in late]
    others = [p for p in whole if p not in to_late]
    prompt = [p for p in whole if p not in late]
    late_ways = [
        (cycle_size - 2, half_cycle, cycle_size - 1, half_cycle - 1),
        (half_cycle - 2, half_cycle - 2, half_cycle - 1, cycle_size - 1),
    ]
    ways = [(0, half_cycle - 1, target(0)), (cycle_size - 2, half_cycle + 1, half_cycle - 1)]
    detoured = [source for source, _, _ in ways]
    straight = [p for p in prompt if p not in detoured]
    is_late = among(late)[0] == 1
    after_late = among([target(p) for p in late])
    after_detoured = among([target(p) for p in detoured])

    gram = cross(matrix[:, :width], matrix[:, width:])
    _, keeping, first, last = rotation_of(
        selector(0), summed(gram, whole), [[matrix], [matrix]], [[0], [half]], half, [IN_HBM] * 2
    )
    got_first = passed(first, sends(others))
    got_last = passed(last, sends(others))
    first = passed(first, [(source, by) for source, by, _, _ in late_ways])
    last = passed(last, [(source, by) for source, _, by, _ in late_ways])
    kept = rotated_rows([matrix], [0], rows, keeping, [IN_HBM])
    got_first, got_last, first, last = lax.optimization_barrier((got_first, got_last, first, last))
    late_first = passed(first, [(by, end) for _, by, _, end in late_ways])
    late_last = passed(last, [(by, end) for _, _, by, end in late_ways])

    both = [IN_HBM, ANYWHERE]

    def terms_of(first_half, last_half, positions):
        gram = cross(kept[:half], first_half) + cross(kept[half:], last_half)
        return summed(gram, positions)

    def slot_moved(first_half, last_half, terms):
        return rotation_of(
            selector(1),
            terms,
            [[kept, first_half], [kept, last_half]],
            [[0, 0], [half, 0]],
            half,
            both * 2,
        )

    _, prompt_keeping, first, last = slot_moved(got_first, got_last, terms_of(got_first, got_last, prompt))
    first, last, late_first, late_last = lax.optimization_barrier((first, last, late_first, late_last))
    token = passed(
        lax.slice(late_last, (0, 0), (16, 128)), [(half_cycle - 2, 0), (half_cycle - 1, 1)]
    )
    first, last, late_first, late_last, token = lax.optimization_barrier(
        (first, last, late_first, late_last, token)
    )
    from_first = passed(first, sends(prompt))
    beside = passed(last, [(source, by) for source, by, _ in ways])
    from_last = passed(last, sends(straight))
    from_far = passed(beside, [(by, end) for _, by, end in ways])

    terms = lax.cond(
        is_late,
        lambda: terms_of(late_first, late_last, late),
        lambda: (jnp.zeros((width, width), matrix.dtype),) * 2,
    )
    _, late_keeping, first, last = slot_moved(late_first, late_last, terms)
    from_late_first = passed(first, sends(late))
    from_late_last = passed(last, sends(late))

    keeping = jnp.where(is_late, late_keeping, prompt_keeping)
    got_first = jnp.where(is_late, late_first, got_first)
    got_last = jnp.where(is_late, late_last, got_last)
    out = rotated_rows([kept, got_first], [0, 0], half, keeping, both, matrix.shape)
    out = rotated_rows([kept, got_last], [half, 0], half, keeping, both, matrix.shape, out, half)
    out = place(1 - after_late, from_first, out, 0, [token])
    out = place((1 - after_late) * (1 - after_detoured), from_last, out, half)
    out = place(after_late, from_late_first, out, 0)
    out = place(after_late, from_late_last, out, half)
    return place(after_detoured, from_far, out, half)


def solution(mesh):
    placed = (P("samp", "pair"), P())
    return jax.shard_map(
        shards, mesh=mesh, in_specs=placed, out_specs=P("samp", "pair"), check_vma=False
    )
```

time: 326 us -> 314 us (0.963)
  starting transfers between devices: 164 us -> 34.4 us
  waiting for transfers between devices: 111 us -> 215 us
  Pallas kernels: 21.2 us -> 48.2 us
  matrix products: 25.4 us -> 6.26 us
    ppermute x16 -> x17, starting transfers between devices: 164 us -> 34.4 us  [the longest x13 27.4 us: passed(): return lax.ppermute(value, 'pair', pairs)]
    ppermute x16 -> x17, waiting for transfers between devices: 111 us -> 215 us  [the longest x13 206 us: passed(): return lax.ppermute(value, 'pair', pairs)]
    pallas_call x10 -> x11, Pallas kernels: 21.2 us -> 48.2 us  [the longest x3 32.7 us: rotation_of(): pl.pallas_call(functools.partial(rotation_kernel, tile, starts_of), out_s...]
    dot_general x9 -> x0, matrix products: 18.7 us -> none  [times(): jnp.dot(part, columns, preferred_element_type=jnp.float32)]
    dot_general x5 -> x3, matrix products: 6.68 us -> 6.26 us  [cross(): lax.dot_general(first, second, (((0,), (0,)), ((), ())), preferred_elemen...]
  transfers between devices with their start and end apart: 16 -> 17, of which waited for: 10 -> 8; matrix products, arithmetic and copies ran while one was open for 6% -> 2% of each run, Pallas kernels for 3% -> 12%
where the time goes in v3:
time: 314 us; the launch traced here: 313 us
  waiting for transfers between devices  215 us (68%)
  Pallas kernels  48.2 us (15%)
  starting transfers between devices  34.4 us (11%)
  matrix products  6.26 us (2%)
  local copies, waits for them, and re-layouts  5.8 us (2%)
    ppermute x13, waiting for transfers between devices, passed(): return lax.ppermute(value, 'pair', pairs)  206 us
    pallas_call x3, Pallas kernels, rotation_of(): pl.pallas_call(functools.partial(rotation_kernel, tile, starts_of), out_s...  32.7 us
    ppermute x13, starting transfers between devices, passed(): return lax.ppermute(value, 'pair', pairs)  27.4 us
    pallas_call x3, Pallas kernels, rotated_rows(): pl.pallas_call(functools.partial(rotated_kernel, starts, tile, rows, firs...  11.2 us
    ppermute x4, waiting for transfers between devices, summed(): other = lax.ppermute(total, ('samp', 'pair'), pairs)  9.48 us
    ppermute x4, starting transfers between devices, summed(): other = lax.ppermute(total, ('samp', 'pair'), pairs)  6.94 us
  transfers between devices with their start and end apart: 17, of which 8 were waited for; matrix products, arithmetic and copies ran while one was open for 2% of the time, Pallas kernels for 12%

profile of v3, /device:TPU:4, one launch (start us, length us, event | category | flops | bytes accessed | tf_op | source)
XLA Modules:
  0.0 313.2 jit_solution(4043113757762364222)
XLA Ops:
  0.0 4.8 %fusion.23 = bf16[256,256]{1,0:T(8,128)(2,1)S(1)} fusion(bf16[8192,512]{1,0:T(8,128)(2,1)} %refs_1_.1), kind=kOutput, calls=%fused_computation.18 | convolution fusion | flops 1073807360 | bytes 8519680 | tf_op jit(solution)/shard_map/dot_general | solution.py:268
  8.4 3.4 %collective-permute-done.3.refs_2_ = bf16[256,256]{1,0:T(8,128)(2,1)S(1)} collective-permute-done((bf16[256,256]{1,0:T(8,128)(2,1)S(1)}, bf16[256,256]{1,0:T(8,128)(2,1)S(1)}, u32[]{:S(2)}, u32[]{:S(2)}) %collective-permute-start.3) | collective-permute-done | bytes 131104 | tf_op jit(solution)/shard_map/ppermute | solution.py:262
  11.8 10.0 %shard_map.28 = (bf16[512,256]{1,0:T(8,128)(2,1)}, bf16[512,256]{1,0:T(8,128)(2,1)S(1)}, bf16[4096,256]{1,0:T(8,128)(2,1)S(1)}, bf16[4096,256]{1,0:T(8,128)(2,1)S(1)}) custom-call(s32[1]{0:T(128)} %bitcast.2.refs_0_, bf16[256,256]{1,0:T(8,128)(2,1)S(1)} %add_convert_fusion.2.refs_1_, bf16[256,256]{1,0:T(8,128)(2,1)S(1)} %collective-permute-done.3.refs_2_, ...), custom_call_target="tpu_custom_call" | custom-call | flops 4831838208 | bytes 13238272 | tf_op jit(solution)/shard_map/pallas_call | solution.py:149
  21.8 5.4 %collective-permute-start.4 = (bf16[4096,256]{1,0:T(8,128)(2,1)S(1)}, bf16[4096,256]{1,0:T(8,128)(2,1)S(1)}, u32[]{:S(2)}, u32[]{:S(2)}) collective-permute-start(bf16[4096,256]{1,0:T(8,128)(2,1)S(1)} %get-tuple-element.39), channel_id=1, source_target_pairs={{0,5},{1,6},{3,0},{4,1},{5,2},{7,4},{8,13},{9,14},{11,8},{12,9},{1... | collective-permute-start | bytes 6291464 | tf_op jit(solution)/shard_map/ppermute | solution.py:288
  29.2 2.0 collective-permute-start.6
  31.2 2.0 collective-permute-start.7
  33.2 40.9 %collective-permute-done.4.refs_4_ = bf16[4096,256]{1,0:T(8,128)(2,1)S(1)} collective-permute-done((bf16[4096,256]{1,0:T(8,128)(2,1)S(1)}, bf16[4096,256]{1,0:T(8,128)(2,1)S(1)}, u32[]{:S(2)}, u32[]{:S(2)}) %collective-permute-start.4) | collective-permute-done | bytes 2097184 | tf_op jit(solution)/shard_map/ppermute | solution.py:288
  74.1 43.2 %collective-permute-done.5.refs_6_ = bf16[4096,256]{1,0:T(8,128)(2,1)S(1)} collective-permute-done((bf16[4096,256]{1,0:T(8,128)(2,1)S(1)}, bf16[4096,256]{1,0:T(8,128)(2,1)S(1)}, u32[]{:S(2)}, u32[]{:S(2)}) %collective-permute-start.5) | collective-permute-done | bytes 2097184 | tf_op jit(solution)/shard_map/ppermute | solution.py:288
  117.3 2.0 collective-permute-start.10
  120.1 5.3 %shard_map.29.refs_3_.refs_5_.refs_1_ = bf16[8192,256]{1,0:T(8,128)(2,1)S(1)} custom-call(bf16[512,256]{1,0:T(8,128)(2,1)S(1)} %get-tuple-element.38.refs_0_, bf16[8192,512]{1,0:T(8,128)(2,1)} %refs_1_.1), custom_call_target="tpu_custom_call" | custom-call | flops 2147483648 | bytes 12582912 | tf_op jit(solution)/shard_map/pallas_call | solution.py:184
  131.5 3.4 %collective-permute-start.9 = (bf16[256,256]{1,0:T(8,128)(2,1)S(1)}, bf16[256,256]{1,0:T(8,128)(2,1)S(1)}, u32[]{:S(2)}, u32[]{:S(2)}) collective-permute-start(bf16[256,256]{1,0:T(8,128)(2,1)S(1)} %add_convert_fusion.1.refs_1_), channel_id=1, source_target_pairs={{0,16},{1,17},{2,18},{4,20},{5,21},{6,22},{8,24},{9,25},{10,26},{1... | collective-permute-start | bytes 393224 | tf_op jit(solution)/shard_map/ppermute | solution.py:262
  135.5 3.4 %collective-permute-done.9.refs_2_ = bf16[256,256]{1,0:T(8,128)(2,1)S(1)} collective-permute-done((bf16[256,256]{1,0:T(8,128)(2,1)S(1)}, bf16[256,256]{1,0:T(8,128)(2,1)S(1)}, u32[]{:S(2)}, u32[]{:S(2)}) %collective-permute-start.9) | collective-permute-done | bytes 131104 | tf_op jit(solution)/shard_map/ppermute | solution.py:262
  138.9 10.7 %shard_map.30 = (bf16[512,256]{1,0:T(8,128)(2,1)}, bf16[512,256]{1,0:T(8,128)(2,1)S(1)}, bf16[4096,256]{1,0:T(8,128)(2,1)S(1)}, bf16[4096,256]{1,0:T(8,128)(2,1)}) custom-call(s32[1]{0:T(128)} %bitcast.1.refs_0_, bf16[256,256]{1,0:T(8,128)(2,1)S(1)} %add_convert_fusion.1.refs_1_, bf16[256,256]{1,0:T(8,128)(2,1)S(1)} %collective-permute-done.9.refs_2_, ...), custom_call_target="tpu_custom_call" | custom-call | flops 4831838208 | bytes 13238272 | tf_op jit(solution)/shard_map/pallas_call | solution.py:149
  152.3 16.2 %collective-permute-done.12.refs_0_ = bf16[16,128]{1,0:T(8,128)(2,1)S(1)} collective-permute-done((bf16[16,128]{1,0:T(8,128)(2,1)S(1)}, bf16[16,128]{1,0:T(8,128)(2,1)S(1)}, u32[]{:S(2)}, u32[]{:S(2)}) %collective-permute-start.12) | collective-permute-done | bytes 4128 | tf_op jit(solution)/shard_map/ppermute | solution.py:288
  168.5 2.0 collective-permute-start.13
  175.7 12.1 %shard_map.31 = (bf16[512,256]{1,0:T(8,128)(2,1)}, bf16[512,256]{1,0:T(8,128)(2,1)S(1)}, bf16[4096,256]{1,0:T(8,128)(2,1)}, bf16[4096,256]{1,0:T(8,128)(2,1)}) custom-call(s32[1]{0:T(128)} %bitcast.1.refs_0_, bf16[256,256]{1,0:T(8,128)(2,1)} %get-tuple-element.54.refs_1_, bf16[256,256]{1,0:T(8,128)(2,1)} %get-tuple-element.55.refs_2_, ...), custom_call_target="tpu_custom_call" | custom-call | flops 4831838208 | bytes 13238272 | tf_op jit(solution)/shard_map/pallas_call | solution.py:149
  187.8 2.0 collective-permute-start.16
  189.8 2.1 collective-permute-start.15
  191.9 2.0 collective-permute-start.14
  193.9 2.8 broadcast_select_fusion
  197.4 3.0 shard_map.32.refs_3_
  200.4 3.0 shard_map.33._
  203.4 105.5 %collective-permute-done.18.source = bf16[4096,256]{1,0:T(8,128)(2,1)S(1)} collective-permute-done((bf16[4096,256]{1,0:T(8,128)(2,1)}, bf16[4096,256]{1,0:T(8,128)(2,1)S(1)}, u32[]{:S(2)}, u32[]{:S(2)}) %collective-permute-start.18) | collective-permute-done | bytes 2097184 | tf_op jit(solution)/shard_map/ppermute | solution.py:288
  310.4 2.4 shard_map.35._
  (49 shorter events, 24.5 us)
Async XLA Ops:
  0.0 7.8 %copy-start.7 = (s32[2,8]{1,0:T(2,128)S(1)}, s32[2,8]{1,0:T(2,128)}, u32[]{:S(2)}) copy-start(s32[2,8]{1,0:T(2,128)} %param.5) | copy-start | bytes 196
  4.8 1.4 collective-permute-start.2
  6.2 5.6 %collective-permute-start.3 = (bf16[256,256]{1,0:T(8,128)(2,1)S(1)}, bf16[256,256]{1,0:T(8,128)(2,1)S(1)}, u32[]{:S(2)}, u32[]{:S(2)}) collective-permute-start(bf16[256,256]{1,0:T(8,128)(2,1)S(1)} %add_convert_fusion.2.refs_1_), channel_id=1, source_target_pairs={{0,16},{1,17},{2,18},{3,19},{4,20},{5,21},{6,22},{7,23},{8,24},{9,... | collective-permute-start | bytes 393224 | tf_op jit(solution)/shard_map/ppermute | solution.py:262
  21.8 52.3 %collective-permute-start.4 = (bf16[4096,256]{1,0:T(8,128)(2,1)S(1)}, bf16[4096,256]{1,0:T(8,128)(2,1)S(1)}, u32[]{:S(2)}, u32[]{:S(2)}) collective-permute-start(bf16[4096,256]{1,0:T(8,128)(2,1)S(1)} %get-tuple-element.39), channel_id=1, source_target_pairs={{0,5},{1,6},{3,0},{4,1},{5,2},{7,4},{8,13},{9,14},{11,8},{12,9},{1... | collective-permute-start | bytes 6291464 | tf_op jit(solution)/shard_map/ppermute | solution.py:288
  27.3 90.0 %collective-permute-start.5 = (bf16[4096,256]{1,0:T(8,128)(2,1)S(1)}, bf16[4096,256]{1,0:T(8,128)(2,1)S(1)}, u32[]{:S(2)}, u32[]{:S(2)}) collective-permute-start(bf16[4096,256]{1,0:T(8,128)(2,1)S(1)} %get-tuple-element.40), channel_id=1, source_target_pairs={{0,5},{1,6},{3,0},{4,1},{5,2},{7,4},{8,13},{9,14},{11,8},{12,9},{1... | collective-permute-start | bytes 6291464 | tf_op jit(solution)/shard_map/ppermute | solution.py:288
  29.2 88.1 %collective-permute-start.6 = (bf16[4096,256]{1,0:T(8,128)(2,1)S(1)}, bf16[4096,256]{1,0:T(8,128)(2,1)}, u32[]{:S(2)}, u32[]{:S(2)}) collective-permute-start(bf16[4096,256]{1,0:T(8,128)(2,1)S(1)} %get-tuple-element.39), channel_id=1, source_target_pairs={{6,4},{2,2},{14,12},{10,10},{22,20},{18,18},{30,28},{26,26}} | collective-permute-start | bytes 6291464 | tf_op jit(solution)/shard_map/ppermute | solution.py:288
  31.2 86.1 %collective-permute-start.7 = (bf16[4096,256]{1,0:T(8,128)(2,1)S(1)}, bf16[4096,256]{1,0:T(8,128)(2,1)}, u32[]{:S(2)}, u32[]{:S(2)}) collective-permute-start(bf16[4096,256]{1,0:T(8,128)(2,1)S(1)} %get-tuple-element.40), channel_id=1, source_target_pairs={{6,7},{2,3},{14,15},{10,11},{22,23},{18,19},{30,31},{26,27}} | collective-permute-start | bytes 6291464 | tf_op jit(solution)/shard_map/ppermute | solution.py:288
  74.1 52.1 %copy-start.5 = (bf16[4096,256]{1,0:T(8,128)(2,1)}, bf16[4096,256]{1,0:T(8,128)(2,1)S(1)}, u32[]{:S(2)}) copy-start(bf16[4096,256]{1,0:T(8,128)(2,1)S(1)} %collective-permute-done.4.refs_4_) | copy-start | bytes 6291460
  117.3 8.1 %copy-start.6 = (bf16[4096,256]{1,0:T(8,128)(2,1)}, bf16[4096,256]{1,0:T(8,128)(2,1)S(1)}, u32[]{:S(2)}) copy-start(bf16[4096,256]{1,0:T(8,128)(2,1)S(1)} %collective-permute-done.5.refs_6_) | copy-start | bytes 6291460
  117.3 33.6 %collective-permute-start.10 = (bf16[4096,256]{1,0:T(8,128)(2,1)}, bf16[4096,256]{1,0:T(8,128)(2,1)}, u32[]{:S(2)}, u32[]{:S(2)}) collective-permute-start(bf16[4096,256]{1,0:T(8,128)(2,1)} %collective-permute-done.6), channel_id=1, source_target_pairs={{4,3},{2,7},{12,11},{10,15},{20,19},{18,23},{28,27},{26,31}} | collective-permute-start | bytes 6291464 | tf_op jit(solution)/shard_map/ppermute | solution.py:288
  119.3 31.6 %collective-permute-start.11 = (bf16[4096,256]{1,0:T(8,128)(2,1)}, bf16[4096,256]{1,0:T(8,128)(2,1)S(1)}, u32[]{:S(2)}, u32[]{:S(2)}) collective-permute-start(bf16[4096,256]{1,0:T(8,128)(2,1)} %collective-permute-done.7), channel_id=1, source_target_pairs={{7,3},{3,7},{15,11},{11,15},{23,19},{19,23},{31,27},{27,31}} | collective-permute-start | bytes 6291464 | tf_op jit(solution)/shard_map/ppermute | solution.py:288
  125.4 2.0 copy-start.1
  128.2 3.2 %collective-permute-start.8 = (bf16[256,256]{1,0:T(8,128)(2,1)S(1)}, bf16[256,256]{1,0:T(8,128)(2,1)S(1)}, u32[]{:S(2)}, u32[]{:S(2)}) collective-permute-start(bf16[256,256]{1,0:T(8,128)(2,1)S(1)} %fusion.20), channel_id=1, source_target_pairs={{0,8},{1,9},{2,10},{4,12},{5,13},{6,14},{8,0},{9,1},{10,2},{12,4},... | collective-permute-start | bytes 393224 | tf_op jit(solution)/shard_map/ppermute | solution.py:262
  131.5 7.4 %collective-permute-start.9 = (bf16[256,256]{1,0:T(8,128)(2,1)S(1)}, bf16[256,256]{1,0:T(8,128)(2,1)S(1)}, u32[]{:S(2)}, u32[]{:S(2)}) collective-permute-start(bf16[256,256]{1,0:T(8,128)(2,1)S(1)} %add_convert_fusion.1.refs_1_), channel_id=1, source_target_pairs={{0,16},{1,17},{2,18},{4,20},{5,21},{6,22},{8,24},{9,25},{10,26},{1... | collective-permute-start | bytes 393224 | tf_op jit(solution)/shard_map/ppermute | solution.py:262
  149.6 1.4 copy-start
  151.0 19.5 %copy-start.4 = (bf16[4096,256]{1,0:T(8,128)(2,1)}, bf16[4096,256]{1,0:T(8,128)(2,1)S(1)}, u32[]{:S(2)}) copy-start(bf16[4096,256]{1,0:T(8,128)(2,1)S(1)} %collective-permute-done.11.refs_6_) | copy-start | bytes 6291460
  151.0 17.5 %collective-permute-start.12 = (bf16[16,128]{1,0:T(8,128)(2,1)S(1)}, bf16[16,128]{1,0:T(8,128)(2,1)S(1)}, u32[]{:S(2)}, u32[]{:S(2)}) collective-permute-start(bf16[16,128]{1,0:T(8,128)(2,1)S(1)} %slice.34), channel_id=1, source_target_pairs={{2,0},{3,1},{10,8},{11,9},{18,16},{19,17},{26,24},{27,25}} | collective-permute-start | bytes 12296 | tf_op jit(solution)/shard_map/ppermute | solution.py:288
  168.5 23.4 %collective-permute-start.13 = (bf16[4096,256]{1,0:T(8,128)(2,1)}, bf16[4096,256]{1,0:T(8,128)(2,1)}, u32[]{:S(2)}, u32[]{:S(2)}) collective-permute-start(bf16[4096,256]{1,0:T(8,128)(2,1)} %get-tuple-element.51), channel_id=1, source_target_pairs={{0,3},{6,5},{8,11},{14,13},{16,19},{22,21},{24,27},{30,29}} | collective-permute-start | bytes 6291464 | tf_op jit(solution)/shard_map/ppermute | solution.py:288
  170.5 139.9 %collective-permute-start.17 = (bf16[4096,256]{1,0:T(8,128)(2,1)}, bf16[4096,256]{1,0:T(8,128)(2,1)}, u32[]{:S(2)}, u32[]{:S(2)}) collective-permute-start(bf16[4096,256]{1,0:T(8,128)(2,1)} %get-tuple-element.51), channel_id=1, source_target_pairs={{1,6},{2,7},{4,1},{5,2},{9,14},{10,15},{12,9},{13,10},{17,22},{18,... | collective-permute-start | bytes 6291464 | tf_op jit(solution)/shard_map/ppermute | solution.py:288
  172.4 136.4 %collective-permute-start.18 = (bf16[4096,256]{1,0:T(8,128)(2,1)}, bf16[4096,256]{1,0:T(8,128)(2,1)S(1)}, u32[]{:S(2)}, u32[]{:S(2)}) collective-permute-start(bf16[4096,256]{1,0:T(8,128)(2,1)} %copy-done), channel_id=1, source_target_pairs={{0,5},{1,6},{2,7},{4,1},{5,2},{6,3},{8,13},{9,14},{10,15},{12,9},{... | collective-permute-start | bytes 6291464 | tf_op jit(solution)/shard_map/ppermute | solution.py:288
  187.8 125.1 %collective-permute-start.16 = (bf16[4096,256]{1,0:T(8,128)(2,1)}, bf16[4096,256]{1,0:T(8,128)(2,1)}, u32[]{:S(2)}, u32[]{:S(2)}) collective-permute-start(bf16[4096,256]{1,0:T(8,128)(2,1)} %get-tuple-element.57), channel_id=1, source_target_pairs={{3,0},{7,4},{11,8},{15,12},{19,16},{23,20},{27,24},{31,28}} | collective-permute-start | bytes 6291464 | tf_op jit(solution)/shard_map/ppermute | solution.py:288
  189.8 123.2 %collective-permute-start.15 = (bf16[4096,256]{1,0:T(8,128)(2,1)}, bf16[4096,256]{1,0:T(8,128)(2,1)}, u32[]{:S(2)}, u32[]{:S(2)}) collective-permute-start(bf16[4096,256]{1,0:T(8,128)(2,1)} %get-tuple-element.56), channel_id=1, source_target_pairs={{3,0},{7,4},{11,8},{15,12},{19,16},{23,20},{27,24},{31,28}} | collective-permute-start | bytes 6291464 | tf_op jit(solution)/shard_map/ppermute | solution.py:288
  191.9 121.2 %collective-permute-start.14 = (bf16[4096,256]{1,0:T(8,128)(2,1)}, bf16[4096,256]{1,0:T(8,128)(2,1)}, u32[]{:S(2)}, u32[]{:S(2)}) collective-permute-start(bf16[4096,256]{1,0:T(8,128)(2,1)} %collective-permute-done.13), channel_id=1, source_target_pairs={{3,5},{5,3},{11,13},{13,11},{19,21},{21,19},{27,29},{29,27}} | collective-permute-start | bytes 6291464 | tf_op jit(solution)/shard_map/ppermute | solution.py:288
  193.9 3.5 %copy-start.2 = (bf16[8192,256]{1,0:T(8,128)(2,1)S(1)}, bf16[8192,256]{1,0:T(8,128)(2,1)}, u32[]{:S(2)}) copy-start(bf16[8192,256]{1,0:T(8,128)(2,1)} %copy-done.1) | copy-start | bytes 12582916

commit v4 on v3

--- a/solution.py
+++ b/solution.py
@@ -8,7 +8,7 @@
 from jax.sharding import PartitionSpec as P
 
 POLAR_STEPS = 5
-TILE = 1024
+TILE = 2048
 VMEM_LIMIT = 48 * 1024 * 1024
 
 
@@ -314,14 +314,13 @@
     _, keeping, first, last = rotation_of(
         selector(0), summed(gram, whole), [[matrix], [matrix]], [[0], [half]], half, [IN_HBM] * 2
     )
-    got_first = passed(first, sends(others))
+    got_first = passed(first, sends(others) + [(source, by) for source, _, by, _ in late_ways])
     got_last = passed(last, sends(others))
-    first = passed(first, [(source, by) for source, by, _, _ in late_ways])
-    last = passed(last, [(source, by) for source, _, by, _ in late_ways])
+    relayed = passed(last, [(source, by) for source, by, _, _ in late_ways])
     kept = rotated_rows([matrix], [0], rows, keeping, [IN_HBM])
-    got_first, got_last, first, last = lax.optimization_barrier((got_first, got_last, first, last))
-    late_first = passed(first, [(by, end) for _, by, _, end in late_ways])
-    late_last = passed(last, [(by, end) for _, _, by, end in late_ways])
+    got_first, got_last, relayed = lax.optimization_barrier((got_first, got_last, relayed))
+    late_first = passed(got_first, [(by, end) for _, _, by, end in late_ways])
+    late_last = passed(relayed, [(by, end) for _, by, _, end in late_ways])
 
     both = [IN_HBM, ANYWHERE]
 
@@ -340,17 +339,16 @@
         )
 
     _, prompt_keeping, first, last = slot_moved(got_first, got_last, terms_of(got_first, got_last, prompt))
-    first, last, late_first, late_last = lax.optimization_barrier((first, last, late_first, late_last))
-    token = passed(
-        lax.slice(late_last, (0, 0), (16, 128)), [(half_cycle - 2, 0), (half_cycle - 1, 1)]
-    )
+    first, last, late_first, late_last, token = lax.optimization_barrier(
+        (first, last, late_first, late_last, jnp.zeros((16, 128), matrix.dtype))
+    )
+    token = passed(token, [(half_cycle - 2, 0), (cycle_size - 1, cycle_size - 2)])
     first, last, late_first, late_last, token = lax.optimization_barrier(
         (first, last, late_first, late_last, token)
     )
     from_first = passed(first, sends(prompt))
-    beside = passed(last, [(source, by) for source, by, _ in ways])
-    from_last = passed(last, sends(straight))
-    from_far = passed(beside, [(by, end) for _, by, end in ways])
+    from_last = passed(last, sends(straight) + [(source, by) for source, by, _ in ways])
+    from_far = passed(from_last, [(by, end) for _, by, end in ways])
 
     terms = lax.cond(
         is_late,
@@ -366,8 +364,8 @@
     got_last = jnp.where(is_late, late_last, got_last)
     out = rotated_rows([kept, got_first], [0, 0], half, keeping, both, matrix.shape)
     out = rotated_rows([kept, got_last], [half, 0], half, keeping, both, matrix.shape, out, half)
-    out = place(1 - after_late, from_first, out, 0, [token])
-    out = place((1 - after_late) * (1 - after_detoured), from_last, out, half)
+    out = place((1 - after_late) * (1 - after_detoured), from_last, out, half, [token])
+    out = place(1 - after_late, from_first, out, 0)
     out = place(after_late, from_late_first, out, 0)
     out = place(after_late, from_late_last, out, half)
     return place(after_detoured, from_far, out, half)

time: 314 us -> 307 us (0.978)
  the two profiles are of different devices: /device:TPU:4 before, /device:TPU:23 now
where the time goes in v4:
time: 307 us
  waiting for transfers between devices  202 us (66%)
  Pallas kernels  46.8 us (15%)
  starting transfers between devices  40.9 us (13%)
  matrix products  7.86 us (3%)
  local copies, waits for them, and re-layouts  5.84 us (2%)
    ppermute x11, waiting for transfers between devices, passed(): return lax.ppermute(value, 'pair', pairs)  192 us
    ppermute x11, starting transfers between devices, passed(): return lax.ppermute(value, 'pair', pairs)  33.6 us
    pallas_call x3, Pallas kernels, rotation_of(): pl.pallas_call(functools.partial(rotation_kernel, tile, starts_of), out_s...  31.1 us
    pallas_call x3, Pallas kernels, rotated_rows(): pl.pallas_call(functools.partial(rotated_kernel, starts, tile, rows, firs...  10.4 us
    ppermute x4, waiting for transfers between devices, summed(): other = lax.ppermute(total, ('samp', 'pair'), pairs)  9.59 us
    dot_general x3, matrix products, cross(): lax.dot_general(first, second, (((0,), (0,)), ((), ())), preferred_elemen...  7.86 us
    ppermute x4, starting transfers between devices, summed(): other = lax.ppermute(total, ('samp', 'pair'), pairs)  7.25 us
  transfers between devices with their start and end apart: 15, of which 9 were waited for; matrix products, arithmetic and copies ran while one was open for 3% of the time, Pallas kernels for 11%

profile of v4, /device:TPU:23, one launch (start us, length us, event | category | flops | bytes accessed | tf_op | source)
XLA Modules:
  0.0 306.5 jit_solution(9695236504668651124)
XLA Ops:
  0.0 4.8 %fusion.23 = bf16[256,256]{1,0:T(8,128)(2,1)S(1)} fusion(bf16[8192,512]{1,0:T(8,128)(2,1)} %refs_1_.1), kind=kOutput, calls=%fused_computation.18 | convolution fusion | flops 1073807360 | bytes 8519680 | tf_op jit(solution)/shard_map/dot_general | solution.py:268
  7.5 3.9 %collective-permute-done.3.refs_2_ = bf16[256,256]{1,0:T(8,128)(2,1)S(1)} collective-permute-done((bf16[256,256]{1,0:T(8,128)(2,1)S(1)}, bf16[256,256]{1,0:T(8,128)(2,1)S(1)}, u32[]{:S(2)}, u32[]{:S(2)}) %collective-permute-start.3) | collective-permute-done | bytes 131104 | tf_op jit(solution)/shard_map/ppermute | solution.py:262
  11.3 9.2 %shard_map.28 = (bf16[512,256]{1,0:T(8,128)(2,1)}, bf16[512,256]{1,0:T(8,128)(2,1)S(1)}, bf16[4096,256]{1,0:T(8,128)(2,1)S(1)}, bf16[4096,256]{1,0:T(8,128)(2,1)S(1)}) custom-call(s32[1]{0:T(128)} %bitcast.2.refs_0_, bf16[256,256]{1,0:T(8,128)(2,1)S(1)} %add_convert_fusion.2.refs_1_, bf16[256,256]{1,0:T(8,128)(2,1)S(1)} %collective-permute-done.3.refs_2_, ...), custom_call_target="tpu_custom_call" | custom-call | flops 4831838208 | bytes 13238272 | tf_op jit(solution)/shard_map/pallas_call | solution.py:149
  20.7 3.1 %collective-permute-start.5 = (bf16[4096,256]{1,0:T(8,128)(2,1)S(1)}, bf16[4096,256]{1,0:T(8,128)(2,1)S(1)}, u32[]{:S(2)}, u32[]{:S(2)}) collective-permute-start(bf16[4096,256]{1,0:T(8,128)(2,1)S(1)} %get-tuple-element.40), channel_id=1, source_target_pairs={{0,5},{1,6},{3,0},{4,1},{5,2},{7,4},{8,13},{9,14},{11,8},{12,9},{1... | collective-permute-start | bytes 6291464 | tf_op jit(solution)/shard_map/ppermute | solution.py:288
  25.8 42.6 %collective-permute-done.4.refs_4_ = bf16[4096,256]{1,0:T(8,128)(2,1)} collective-permute-done((bf16[4096,256]{1,0:T(8,128)(2,1)S(1)}, bf16[4096,256]{1,0:T(8,128)(2,1)}, u32[]{:S(2)}, u32[]{:S(2)}) %collective-permute-start.4) | collective-permute-done | bytes 2097184 | tf_op jit(solution)/shard_map/ppermute | solution.py:288
  68.4 44.8 %collective-permute-done.5.refs_6_ = bf16[4096,256]{1,0:T(8,128)(2,1)S(1)} collective-permute-done((bf16[4096,256]{1,0:T(8,128)(2,1)S(1)}, bf16[4096,256]{1,0:T(8,128)(2,1)S(1)}, u32[]{:S(2)}, u32[]{:S(2)}) %collective-permute-start.5) | collective-permute-done | bytes 2097184 | tf_op jit(solution)/shard_map/ppermute | solution.py:288
  113.3 2.1 collective-permute-start.10
  117.3 4.8 %shard_map.29.refs_3_.refs_5_.refs_1_ = bf16[8192,256]{1,0:T(8,128)(2,1)S(1)} custom-call(bf16[512,256]{1,0:T(8,128)(2,1)S(1)} %get-tuple-element.38.refs_0_, bf16[8192,512]{1,0:T(8,128)(2,1)} %refs_1_.1), custom_call_target="tpu_custom_call" | custom-call | flops 2147483648 | bytes 12582912 | tf_op jit(solution)/shard_map/pallas_call | solution.py:184
  124.2 2.3 fusion.20
  126.6 4.0 %collective-permute-start.7 = (bf16[256,256]{1,0:T(8,128)(2,1)S(1)}, bf16[256,256]{1,0:T(8,128)(2,1)S(1)}, u32[]{:S(2)}, u32[]{:S(2)}) collective-permute-start(bf16[256,256]{1,0:T(8,128)(2,1)S(1)} %fusion.20), channel_id=1, source_target_pairs={{0,8},{1,9},{2,10},{4,12},{5,13},{6,14},{8,0},{9,1},{10,2},{12,4},... | collective-permute-start | bytes 393224 | tf_op jit(solution)/shard_map/ppermute | solution.py:262
  131.6 2.2 collective-permute-start.8
  134.4 3.8 %collective-permute-done.8.refs_2_ = bf16[256,256]{1,0:T(8,128)(2,1)S(1)} collective-permute-done((bf16[256,256]{1,0:T(8,128)(2,1)S(1)}, bf16[256,256]{1,0:T(8,128)(2,1)S(1)}, u32[]{:S(2)}, u32[]{:S(2)}) %collective-permute-start.8) | collective-permute-done | bytes 131104 | tf_op jit(solution)/shard_map/ppermute | solution.py:262
  138.2 10.0 %shard_map.30 = (bf16[512,256]{1,0:T(8,128)(2,1)}, bf16[512,256]{1,0:T(8,128)(2,1)S(1)}, bf16[4096,256]{1,0:T(8,128)(2,1)S(1)}, bf16[4096,256]{1,0:T(8,128)(2,1)}) custom-call(s32[1]{0:T(128)} %bitcast.1.refs_0_, bf16[256,256]{1,0:T(8,128)(2,1)S(1)} %add_convert_fusion.1.refs_1_, bf16[256,256]{1,0:T(8,128)(2,1)S(1)} %collective-permute-done.8.refs_2_, ...), custom_call_target="tpu_custom_call" | custom-call | flops 4831838208 | bytes 13238272 | tf_op jit(solution)/shard_map/pallas_call | solution.py:149
  150.3 11.4 %collective-permute-start.12 = (bf16[4096,256]{1,0:T(8,128)(2,1)}, bf16[4096,256]{1,0:T(8,128)(2,1)S(1)}, u32[]{:S(2)}, u32[]{:S(2)}) collective-permute-start(bf16[4096,256]{1,0:T(8,128)(2,1)} %get-tuple-element.51), channel_id=1, source_target_pairs={{1,6},{2,7},{4,1},{5,2},{0,3},{6,5},{9,14},{10,15},{12,9},{13,10},... | collective-permute-start | bytes 6291464 | tf_op jit(solution)/shard_map/ppermute | solution.py:288
  161.7 6.3 %collective-permute-start.16 = (bf16[4096,256]{1,0:T(8,128)(2,1)}, bf16[4096,256]{1,0:T(8,128)(2,1)}, u32[]{:S(2)}, u32[]{:S(2)}) collective-permute-start(bf16[4096,256]{1,0:T(8,128)(2,1)} %copy-done), channel_id=1, source_target_pairs={{0,5},{1,6},{2,7},{4,1},{5,2},{6,3},{8,13},{9,14},{10,15},{12,9},{... | collective-permute-start | bytes 6291464 | tf_op jit(solution)/shard_map/ppermute | solution.py:288
  169.4 11.9 %shard_map.31 = (bf16[512,256]{1,0:T(8,128)(2,1)}, bf16[512,256]{1,0:T(8,128)(2,1)S(1)}, bf16[4096,256]{1,0:T(8,128)(2,1)}, bf16[4096,256]{1,0:T(8,128)(2,1)}) custom-call(s32[1]{0:T(128)} %bitcast.1.refs_0_, bf16[256,256]{1,0:T(8,128)(2,1)} %get-tuple-element.54.refs_1_, bf16[256,256]{1,0:T(8,128)(2,1)} %get-tuple-element.55.refs_2_, ...), custom_call_target="tpu_custom_call" | custom-call | flops 4831838208 | bytes 13238272 | tf_op jit(solution)/shard_map/pallas_call | solution.py:149
  185.3 22.5 %collective-permute-done.12.source = bf16[4096,256]{1,0:T(8,128)(2,1)S(1)} collective-permute-done((bf16[4096,256]{1,0:T(8,128)(2,1)}, bf16[4096,256]{1,0:T(8,128)(2,1)S(1)}, u32[]{:S(2)}, u32[]{:S(2)}) %collective-permute-start.12) | collective-permute-done | bytes 2097184 | tf_op jit(solution)/shard_map/ppermute | solution.py:288
  209.7 2.8 broadcast_select_fusion
  213.2 2.8 shard_map.32.refs_3_
  216.0 2.8 shard_map.33._
  218.8 34.6 %collective-permute-done.16.source = bf16[4096,256]{1,0:T(8,128)(2,1)} collective-permute-done((bf16[4096,256]{1,0:T(8,128)(2,1)}, bf16[4096,256]{1,0:T(8,128)(2,1)}, u32[]{:S(2)}, u32[]{:S(2)}) %collective-permute-start.16) | collective-permute-done | bytes 2097184 | tf_op jit(solution)/shard_map/ppermute | solution.py:288
  253.5 2.6 shard_map.35._
  256.2 47.6 %collective-permute-done.13.source = bf16[4096,256]{1,0:T(8,128)(2,1)} collective-permute-done((bf16[4096,256]{1,0:T(8,128)(2,1)S(1)}, bf16[4096,256]{1,0:T(8,128)(2,1)}, u32[]{:S(2)}, u32[]{:S(2)}) %collective-permute-start.13) | collective-permute-done | bytes 2097184 | tf_op jit(solution)/shard_map/ppermute | solution.py:288
  303.8 2.6 shard_map.38
  (41 shorter events, 21.9 us)
Async XLA Ops:
  0.0 6.9 %copy-start.5 = (s32[2,8]{1,0:T(2,128)S(1)}, s32[2,8]{1,0:T(2,128)}, u32[]{:S(2)}) copy-start(s32[2,8]{1,0:T(2,128)} %param.5) | copy-start | bytes 196
  4.8 1.7 collective-permute-start.2
  6.5 4.8 %collective-permute-start.3 = (bf16[256,256]{1,0:T(8,128)(2,1)S(1)}, bf16[256,256]{1,0:T(8,128)(2,1)S(1)}, u32[]{:S(2)}, u32[]{:S(2)}) collective-permute-start(bf16[256,256]{1,0:T(8,128)(2,1)S(1)} %add_convert_fusion.2.refs_1_), channel_id=1, source_target_pairs={{0,16},{1,17},{2,18},{3,19},{4,20},{5,21},{6,22},{7,23},{8,24},{9,... | collective-permute-start | bytes 393224 | tf_op jit(solution)/shard_map/ppermute | solution.py:262
  20.5 47.9 %collective-permute-start.4 = (bf16[4096,256]{1,0:T(8,128)(2,1)S(1)}, bf16[4096,256]{1,0:T(8,128)(2,1)}, u32[]{:S(2)}, u32[]{:S(2)}) collective-permute-start(bf16[4096,256]{1,0:T(8,128)(2,1)S(1)} %get-tuple-element.39), channel_id=1, source_target_pairs={{0,5},{1,6},{3,0},{4,1},{5,2},{7,4},{6,7},{2,3},{8,13},{9,14},{11,... | collective-permute-start | bytes 6291464 | tf_op jit(solution)/shard_map/ppermute | solution.py:288
  20.7 92.6 %collective-permute-start.5 = (bf16[4096,256]{1,0:T(8,128)(2,1)S(1)}, bf16[4096,256]{1,0:T(8,128)(2,1)S(1)}, u32[]{:S(2)}, u32[]{:S(2)}) collective-permute-start(bf16[4096,256]{1,0:T(8,128)(2,1)S(1)} %get-tuple-element.40), channel_id=1, source_target_pairs={{0,5},{1,6},{3,0},{4,1},{5,2},{7,4},{8,13},{9,14},{11,8},{12,9},{1... | collective-permute-start | bytes 6291464 | tf_op jit(solution)/shard_map/ppermute | solution.py:288
  23.8 89.4 %collective-permute-start.6 = (bf16[4096,256]{1,0:T(8,128)(2,1)S(1)}, bf16[4096,256]{1,0:T(8,128)(2,1)}, u32[]{:S(2)}, u32[]{:S(2)}) collective-permute-start(bf16[4096,256]{1,0:T(8,128)(2,1)S(1)} %get-tuple-element.40), channel_id=1, source_target_pairs={{6,4},{2,2},{14,12},{10,10},{22,20},{18,18},{30,28},{26,26}} | collective-permute-start | bytes 6291464 | tf_op jit(solution)/shard_map/ppermute | solution.py:288
  113.2 8.9 %copy-start.4 = (bf16[4096,256]{1,0:T(8,128)(2,1)}, bf16[4096,256]{1,0:T(8,128)(2,1)S(1)}, u32[]{:S(2)}) copy-start(bf16[4096,256]{1,0:T(8,128)(2,1)S(1)} %collective-permute-done.5.refs_6_) | copy-start | bytes 6291460
  113.3 36.4 %collective-permute-start.10 = (bf16[4096,256]{1,0:T(8,128)(2,1)}, bf16[4096,256]{1,0:T(8,128)(2,1)}, u32[]{:S(2)}, u32[]{:S(2)}) collective-permute-start(bf16[4096,256]{1,0:T(8,128)(2,1)} %collective-permute-done.6), channel_id=1, source_target_pairs={{4,3},{2,7},{12,11},{10,15},{20,19},{18,23},{28,27},{26,31}} | collective-permute-start | bytes 6291464 | tf_op jit(solution)/shard_map/ppermute | solution.py:288
  115.3 34.3 %collective-permute-start.9 = (bf16[4096,256]{1,0:T(8,128)(2,1)}, bf16[4096,256]{1,0:T(8,128)(2,1)}, u32[]{:S(2)}, u32[]{:S(2)}) collective-permute-start(bf16[4096,256]{1,0:T(8,128)(2,1)} %collective-permute-done.4.refs_4_), channel_id=1, source_target_pairs={{7,3},{3,7},{15,11},{11,15},{23,19},{19,23},{31,27},{27,31}} | collective-permute-start | bytes 6291464 | tf_op jit(solution)/shard_map/ppermute | solution.py:288
  122.2 2.0 copy-start.1
  126.6 5.0 %collective-permute-start.7 = (bf16[256,256]{1,0:T(8,128)(2,1)S(1)}, bf16[256,256]{1,0:T(8,128)(2,1)S(1)}, u32[]{:S(2)}, u32[]{:S(2)}) collective-permute-start(bf16[256,256]{1,0:T(8,128)(2,1)S(1)} %fusion.20), channel_id=1, source_target_pairs={{0,8},{1,9},{2,10},{4,12},{5,13},{6,14},{8,0},{9,1},{10,2},{12,4},... | collective-permute-start | bytes 393224 | tf_op jit(solution)/shard_map/ppermute | solution.py:262
  131.6 6.6 %collective-permute-start.8 = (bf16[256,256]{1,0:T(8,128)(2,1)S(1)}, bf16[256,256]{1,0:T(8,128)(2,1)S(1)}, u32[]{:S(2)}, u32[]{:S(2)}) collective-permute-start(bf16[256,256]{1,0:T(8,128)(2,1)S(1)} %add_convert_fusion.1.refs_1_), channel_id=1, source_target_pairs={{0,16},{1,17},{2,18},{4,20},{5,21},{6,22},{8,24},{9,25},{10,26},{1... | collective-permute-start | bytes 393224 | tf_op jit(solution)/shard_map/ppermute | solution.py:262
  148.2 1.4 copy-start
  149.6 0.7 collective-permute-start.11
  150.3 57.5 %collective-permute-start.12 = (bf16[4096,256]{1,0:T(8,128)(2,1)}, bf16[4096,256]{1,0:T(8,128)(2,1)S(1)}, u32[]{:S(2)}, u32[]{:S(2)}) collective-permute-start(bf16[4096,256]{1,0:T(8,128)(2,1)} %get-tuple-element.51), channel_id=1, source_target_pairs={{1,6},{2,7},{4,1},{5,2},{0,3},{6,5},{9,14},{10,15},{12,9},{13,10},... | collective-permute-start | bytes 6291464 | tf_op jit(solution)/shard_map/ppermute | solution.py:288
  161.7 91.7 %collective-permute-start.16 = (bf16[4096,256]{1,0:T(8,128)(2,1)}, bf16[4096,256]{1,0:T(8,128)(2,1)}, u32[]{:S(2)}, u32[]{:S(2)}) collective-permute-start(bf16[4096,256]{1,0:T(8,128)(2,1)} %copy-done), channel_id=1, source_target_pairs={{0,5},{1,6},{2,7},{4,1},{5,2},{6,3},{8,13},{9,14},{10,15},{12,9},{... | collective-permute-start | bytes 6291464 | tf_op jit(solution)/shard_map/ppermute | solution.py:288
  181.3 74.7 %collective-permute-start.15 = (bf16[4096,256]{1,0:T(8,128)(2,1)}, bf16[4096,256]{1,0:T(8,128)(2,1)}, u32[]{:S(2)}, u32[]{:S(2)}) collective-permute-start(bf16[4096,256]{1,0:T(8,128)(2,1)} %get-tuple-element.57), channel_id=1, source_target_pairs={{3,0},{7,4},{11,8},{15,12},{19,16},{23,20},{27,24},{31,28}} | collective-permute-start | bytes 6291464 | tf_op jit(solution)/shard_map/ppermute | solution.py:288
  183.3 72.8 %collective-permute-start.14 = (bf16[4096,256]{1,0:T(8,128)(2,1)}, bf16[4096,256]{1,0:T(8,128)(2,1)}, u32[]{:S(2)}, u32[]{:S(2)}) collective-permute-start(bf16[4096,256]{1,0:T(8,128)(2,1)} %get-tuple-element.56), channel_id=1, source_target_pairs={{3,0},{7,4},{11,8},{15,12},{19,16},{23,20},{27,24},{31,28}} | collective-permute-start | bytes 6291464 | tf_op jit(solution)/shard_map/ppermute | solution.py:288
  207.8 96.0 %collective-permute-start.13 = (bf16[4096,256]{1,0:T(8,128)(2,1)S(1)}, bf16[4096,256]{1,0:T(8,128)(2,1)}, u32[]{:S(2)}, u32[]{:S(2)}) collective-permute-start(bf16[4096,256]{1,0:T(8,128)(2,1)S(1)} %collective-permute-done.12.source), channel_id=1, source_target_pairs={{3,5},{5,3},{11,13},{13,11},{19,21},{21,19},{27,29},{29,27}} | collective-permute-start | bytes 6291464 | tf_op jit(solution)/shard_map/ppermute | solution.py:288
  209.7 3.5 %copy-start.2 = (bf16[8192,256]{1,0:T(8,128)(2,1)S(1)}, bf16[8192,256]{1,0:T(8,128)(2,1)}, u32[]{:S(2)}) copy-start(bf16[8192,256]{1,0:T(8,128)(2,1)} %copy-done.1) | copy-start | bytes 12582916

commit v5 on v4

--- a/solution.py
+++ b/solution.py
@@ -97,7 +97,7 @@
         )
         return carry
 
-    lax.fori_loop(0, POLAR_STEPS, step, 0)
+    lax.fori_loop(0, POLAR_STEPS, step, 0, unroll=True)
     first = iterate[:, :width].astype(jnp.bfloat16)
     second = iterate[:, width:].astype(jnp.bfloat16)
     second_stays = selector[0] == 1
@@ -264,6 +264,49 @@
     return total, other
 
 
+def whole_gram_kernel(tile, matrix, gram, block, total, arrivals):
+    rows, width = matrix.shape[0], matrix.shape[1] // 2
+
+    def read_of(t):
+        here = pl.ds(pl.multiple_of(t * tile, tile), tile)
+        return pltpu.make_async_copy(matrix.at[here], block.at[here], arrivals.at[t])
+
+    def start(t, carry):
+        read_of(t).start()
+        return carry
+
+    def add(t, carry):
+        read_of(t).wait()
+        here = pl.ds(pl.multiple_of(t * tile, tile), tile)
+        total[...] += cross(block[here, :width], block[here, width:])
+        return carry
+
+    lax.fori_loop(0, rows // tile, start, 0)
+    total[...] = jnp.zeros_like(total)
+    lax.fori_loop(0, rows // tile, add, 0)
+    gram[...] = total[...].astype(gram.dtype)
+
+
+def whole_gram(matrix):
+    rows, width = matrix.shape[0], matrix.shape[1] // 2
+    tile = min(1024, rows)
+    return pl.pallas_call(
+        functools.partial(whole_gram_kernel, tile),
+        out_shape=jax.ShapeDtypeStruct((width, width), matrix.dtype),
+        in_specs=[IN_HBM],
+        out_specs=IN_VMEM,
+        scratch_shapes=[
+            pltpu.VMEM(matrix.shape, matrix.dtype),
+            pltpu.VMEM((width, width), jnp.float32),
+            pltpu.SemaphoreType.DMA((rows // tile,)),
+        ],
+        compiler_params=pltpu.CompilerParams(vmem_limit_bytes=VMEM_LIMIT),
+        cost_estimate=pl.CostEstimate(
+            flops=2 * rows * width**2, bytes_accessed=4 * rows * width, transcendentals=0
+        ),
+    )(matrix)
+
+
 def cross(first, second):
     return lax.dot_general(
         first, second, (((0,), (0,)), ((), ())), preferred_element_type=jnp.float32
@@ -310,7 +353,7 @@
     after_late = among([target(p) for p in late])
     after_detoured = among([target(p) for p in detoured])
 
-    gram = cross(matrix[:, :width], matrix[:, width:])
+    gram = whole_gram(matrix)
     _, keeping, first, last = rotation_of(
         selector(0), summed(gram, whole), [[matrix], [matrix]], [[0], [half]], half, [IN_HBM] * 2
     )
@@ -342,7 +385,7 @@
     first, last, late_first, late_last, token = lax.optimization_barrier(
         (first, last, late_first, late_last, jnp.zeros((16, 128), matrix.dtype))
     )
-    token = passed(token, [(half_cycle - 2, 0), (cycle_size - 1, cycle_size - 2)])
+    token = passed(token, [(half_cycle - 2, cycle_size - 2)])
     first, last, late_first, late_last, token = lax.optimization_barrier(
         (first, last, late_first, late_last, token)
     )

time: 307 us -> 304 us (level)
  the two profiles are of different devices: /device:TPU:23 before, /device:TPU:4 now
where the time goes in v5:
time: 304 us; the launch traced here: 299 us
  waiting for transfers between devices  192 us (63%)
  Pallas kernels  48.1 us (16%)
  starting transfers between devices  47 us (15%)
  local copies, waits for them, and re-layouts  5.85 us (2%)
  matrix products  3.08 us (1%)
    ppermute x11, waiting for transfers between devices, passed(): return lax.ppermute(value, 'pair', pairs)  182 us
    ppermute x11, starting transfers between devices, passed(): return lax.ppermute(value, 'pair', pairs)  40 us
    pallas_call x3, Pallas kernels, rotation_of(): pl.pallas_call(functools.partial(rotation_kernel, tile, starts_of), out_s...  29.3 us
    pallas_call x3, Pallas kernels, rotated_rows(): pl.pallas_call(functools.partial(rotated_kernel, starts, tile, rows, firs...  10.4 us
    ppermute x4, waiting for transfers between devices, summed(): other = lax.ppermute(total, ('samp', 'pair'), pairs)  9.46 us
    ppermute x4, starting transfers between devices, summed(): other = lax.ppermute(total, ('samp', 'pair'), pairs)  6.95 us
  transfers between devices with their start and end apart: 15, of which 8 were waited for; matrix products, arithmetic and copies ran while one was open for 3% of the time, Pallas kernels for 12%

profile of v5, /device:TPU:4, one launch (start us, length us, event | category | flops | bytes accessed | tf_op | source)
XLA Modules:
  0.0 299.1 jit_solution(13792934831024539031)
XLA Ops:
  0.0 4.1 %shard_map.28 = bf16[256,256]{1,0:T(8,128)(2,1)S(1)} custom-call(bf16[8192,512]{1,0:T(8,128)(2,1)} %refs_1_.1), custom_call_target="tpu_custom_call" | custom-call | flops 1073741824 | bytes 8388608 | tf_op jit(solution)/shard_map/pallas_call | solution.py:293
  7.8 3.4 %collective-permute-done.3.refs_2_ = bf16[256,256]{1,0:T(8,128)(2,1)S(1)} collective-permute-done((bf16[256,256]{1,0:T(8,128)(2,1)S(1)}, bf16[256,256]{1,0:T(8,128)(2,1)S(1)}, u32[]{:S(2)}, u32[]{:S(2)}) %collective-permute-start.3) | collective-permute-done | bytes 131104 | tf_op jit(solution)/shard_map/ppermute | solution.py:262
  11.2 8.6 %shard_map.29 = (bf16[512,256]{1,0:T(8,128)(2,1)}, bf16[512,256]{1,0:T(8,128)(2,1)S(1)}, bf16[4096,256]{1,0:T(8,128)(2,1)S(1)}, bf16[4096,256]{1,0:T(8,128)(2,1)S(1)}) custom-call(s32[1]{0:T(128)} %bitcast.2.refs_0_, bf16[256,256]{1,0:T(8,128)(2,1)S(1)} %add_convert_fusion.2.refs_1_, bf16[256,256]{1,0:T(8,128)(2,1)S(1)} %collective-permute-done.3.refs_2_, ...), custom_call_target="tpu_custom_call" | custom-call | flops 4831838208 | bytes 13238272 | tf_op jit(solution)/shard_map/pallas_call | solution.py:149
  19.8 3.6 %collective-permute-start.4 = (bf16[4096,256]{1,0:T(8,128)(2,1)S(1)}, bf16[4096,256]{1,0:T(8,128)(2,1)}, u32[]{:S(2)}, u32[]{:S(2)}) collective-permute-start(bf16[4096,256]{1,0:T(8,128)(2,1)S(1)} %get-tuple-element.39), channel_id=1, source_target_pairs={{0,5},{1,6},{3,0},{4,1},{5,2},{7,4},{6,7},{2,3},{8,13},{9,14},{11,... | collective-permute-start | bytes 6291464 | tf_op jit(solution)/shard_map/ppermute | solution.py:331
  23.4 3.4 %collective-permute-start.5 = (bf16[4096,256]{1,0:T(8,128)(2,1)S(1)}, bf16[4096,256]{1,0:T(8,128)(2,1)S(1)}, u32[]{:S(2)}, u32[]{:S(2)}) collective-permute-start(bf16[4096,256]{1,0:T(8,128)(2,1)S(1)} %get-tuple-element.40), channel_id=1, source_target_pairs={{0,5},{1,6},{3,0},{4,1},{5,2},{7,4},{8,13},{9,14},{11,8},{12,9},{1... | collective-permute-start | bytes 6291464 | tf_op jit(solution)/shard_map/ppermute | solution.py:331
  26.9 2.0 collective-permute-start.6
  28.9 41.5 %collective-permute-done.4.refs_4_ = bf16[4096,256]{1,0:T(8,128)(2,1)} collective-permute-done((bf16[4096,256]{1,0:T(8,128)(2,1)S(1)}, bf16[4096,256]{1,0:T(8,128)(2,1)}, u32[]{:S(2)}, u32[]{:S(2)}) %collective-permute-start.4) | collective-permute-done | bytes 2097184 | tf_op jit(solution)/shard_map/ppermute | solution.py:331
  70.4 43.1 %collective-permute-done.5.refs_6_ = bf16[4096,256]{1,0:T(8,128)(2,1)S(1)} collective-permute-done((bf16[4096,256]{1,0:T(8,128)(2,1)S(1)}, bf16[4096,256]{1,0:T(8,128)(2,1)S(1)}, u32[]{:S(2)}, u32[]{:S(2)}) %collective-permute-start.5) | collective-permute-done | bytes 2097184 | tf_op jit(solution)/shard_map/ppermute | solution.py:331
  113.5 2.1 collective-permute-start.10
  115.6 2.0 collective-permute-start.9
  117.6 4.8 %shard_map.30.refs_3_.refs_5_.refs_1_ = bf16[8192,256]{1,0:T(8,128)(2,1)S(1)} custom-call(bf16[512,256]{1,0:T(8,128)(2,1)S(1)} %get-tuple-element.38.refs_0_, bf16[8192,512]{1,0:T(8,128)(2,1)} %refs_1_.1), custom_call_target="tpu_custom_call" | custom-call | flops 2147483648 | bytes 12582912 | tf_op jit(solution)/shard_map/pallas_call | solution.py:184
  124.5 2.3 fusion.17
  130.1 3.4 %collective-permute-start.8 = (bf16[256,256]{1,0:T(8,128)(2,1)S(1)}, bf16[256,256]{1,0:T(8,128)(2,1)S(1)}, u32[]{:S(2)}, u32[]{:S(2)}) collective-permute-start(bf16[256,256]{1,0:T(8,128)(2,1)S(1)} %add_convert_fusion.1.refs_1_), channel_id=1, source_target_pairs={{0,16},{1,17},{2,18},{4,20},{5,21},{6,22},{8,24},{9,25},{10,26},{1... | collective-permute-start | bytes 393224 | tf_op jit(solution)/shard_map/ppermute | solution.py:262
  134.1 3.4 %collective-permute-done.8.refs_2_ = bf16[256,256]{1,0:T(8,128)(2,1)S(1)} collective-permute-done((bf16[256,256]{1,0:T(8,128)(2,1)S(1)}, bf16[256,256]{1,0:T(8,128)(2,1)S(1)}, u32[]{:S(2)}, u32[]{:S(2)}) %collective-permute-start.8) | collective-permute-done | bytes 131104 | tf_op jit(solution)/shard_map/ppermute | solution.py:262
  137.5 9.5 %shard_map.31 = (bf16[512,256]{1,0:T(8,128)(2,1)}, bf16[512,256]{1,0:T(8,128)(2,1)S(1)}, bf16[4096,256]{1,0:T(8,128)(2,1)S(1)}, bf16[4096,256]{1,0:T(8,128)(2,1)}) custom-call(s32[1]{0:T(128)} %bitcast.1.refs_0_, bf16[256,256]{1,0:T(8,128)(2,1)S(1)} %add_convert_fusion.1.refs_1_, bf16[256,256]{1,0:T(8,128)(2,1)S(1)} %collective-permute-done.8.refs_2_, ...), custom_call_target="tpu_custom_call" | custom-call | flops 4831838208 | bytes 13238272 | tf_op jit(solution)/shard_map/pallas_call | solution.py:149
  149.1 18.4 %collective-permute-start.12 = (bf16[4096,256]{1,0:T(8,128)(2,1)}, bf16[4096,256]{1,0:T(8,128)(2,1)S(1)}, u32[]{:S(2)}, u32[]{:S(2)}) collective-permute-start(bf16[4096,256]{1,0:T(8,128)(2,1)} %get-tuple-element.51), channel_id=1, source_target_pairs={{1,6},{2,7},{4,1},{5,2},{0,3},{6,5},{9,14},{10,15},{12,9},{13,10},... | collective-permute-start | bytes 6291464 | tf_op jit(solution)/shard_map/ppermute | solution.py:331
  170.8 11.2 %shard_map.32 = (bf16[512,256]{1,0:T(8,128)(2,1)}, bf16[512,256]{1,0:T(8,128)(2,1)S(1)}, bf16[4096,256]{1,0:T(8,128)(2,1)}, bf16[4096,256]{1,0:T(8,128)(2,1)}) custom-call(s32[1]{0:T(128)} %bitcast.1.refs_0_, bf16[256,256]{1,0:T(8,128)(2,1)} %get-tuple-element.54.refs_1_, bf16[256,256]{1,0:T(8,128)(2,1)} %get-tuple-element.55.refs_2_, ...), custom_call_target="tpu_custom_call" | custom-call | flops 4831838208 | bytes 13238272 | tf_op jit(solution)/shard_map/pallas_call | solution.py:149
  182.0 2.0 collective-permute-start.15
  186.0 27.9 %collective-permute-done.12.source = bf16[4096,256]{1,0:T(8,128)(2,1)S(1)} collective-permute-done((bf16[4096,256]{1,0:T(8,128)(2,1)}, bf16[4096,256]{1,0:T(8,128)(2,1)S(1)}, u32[]{:S(2)}, u32[]{:S(2)}) %collective-permute-start.12) | collective-permute-done | bytes 2097184 | tf_op jit(solution)/shard_map/ppermute | solution.py:331
  215.9 2.8 broadcast_select_fusion
  219.3 2.8 shard_map.33.refs_3_
  222.1 2.8 shard_map.34._
  226.4 69.7 %collective-permute-done.16.source = bf16[4096,256]{1,0:T(8,128)(2,1)} collective-permute-done((bf16[4096,256]{1,0:T(8,128)(2,1)}, bf16[4096,256]{1,0:T(8,128)(2,1)}, u32[]{:S(2)}, u32[]{:S(2)}) %collective-permute-start.16) | collective-permute-done | bytes 2097184 | tf_op jit(solution)/shard_map/ppermute | solution.py:331
  296.1 2.6 shard_map.36._
  (41 shorter events, 22.4 us)
Async XLA Ops:
  0.0 7.1 %copy-start.5 = (s32[2,8]{1,0:T(2,128)S(1)}, s32[2,8]{1,0:T(2,128)}, u32[]{:S(2)}) copy-start(s32[2,8]{1,0:T(2,128)} %param.5) | copy-start | bytes 196
  4.1 1.4 collective-permute-start.2
  5.6 5.6 %collective-permute-start.3 = (bf16[256,256]{1,0:T(8,128)(2,1)S(1)}, bf16[256,256]{1,0:T(8,128)(2,1)S(1)}, u32[]{:S(2)}, u32[]{:S(2)}) collective-permute-start(bf16[256,256]{1,0:T(8,128)(2,1)S(1)} %add_convert_fusion.2.refs_1_), channel_id=1, source_target_pairs={{0,16},{1,17},{2,18},{3,19},{4,20},{5,21},{6,22},{7,23},{8,24},{9,... | collective-permute-start | bytes 393224 | tf_op jit(solution)/shard_map/ppermute | solution.py:262
  19.8 50.5 %collective-permute-start.4 = (bf16[4096,256]{1,0:T(8,128)(2,1)S(1)}, bf16[4096,256]{1,0:T(8,128)(2,1)}, u32[]{:S(2)}, u32[]{:S(2)}) collective-permute-start(bf16[4096,256]{1,0:T(8,128)(2,1)S(1)} %get-tuple-element.39), channel_id=1, source_target_pairs={{0,5},{1,6},{3,0},{4,1},{5,2},{7,4},{6,7},{2,3},{8,13},{9,14},{11,... | collective-permute-start | bytes 6291464 | tf_op jit(solution)/shard_map/ppermute | solution.py:331
  23.4 90.0 %collective-permute-start.5 = (bf16[4096,256]{1,0:T(8,128)(2,1)S(1)}, bf16[4096,256]{1,0:T(8,128)(2,1)S(1)}, u32[]{:S(2)}, u32[]{:S(2)}) collective-permute-start(bf16[4096,256]{1,0:T(8,128)(2,1)S(1)} %get-tuple-element.40), channel_id=1, source_target_pairs={{0,5},{1,6},{3,0},{4,1},{5,2},{7,4},{8,13},{9,14},{11,8},{12,9},{1... | collective-permute-start | bytes 6291464 | tf_op jit(solution)/shard_map/ppermute | solution.py:331
  26.9 86.6 %collective-permute-start.6 = (bf16[4096,256]{1,0:T(8,128)(2,1)S(1)}, bf16[4096,256]{1,0:T(8,128)(2,1)}, u32[]{:S(2)}, u32[]{:S(2)}) collective-permute-start(bf16[4096,256]{1,0:T(8,128)(2,1)S(1)} %get-tuple-element.40), channel_id=1, source_target_pairs={{6,4},{2,2},{14,12},{10,10},{22,20},{18,18},{30,28},{26,26}} | collective-permute-start | bytes 6291464 | tf_op jit(solution)/shard_map/ppermute | solution.py:331
  113.5 8.9 %copy-start.4 = (bf16[4096,256]{1,0:T(8,128)(2,1)}, bf16[4096,256]{1,0:T(8,128)(2,1)S(1)}, u32[]{:S(2)}) copy-start(bf16[4096,256]{1,0:T(8,128)(2,1)S(1)} %collective-permute-done.5.refs_6_) | copy-start | bytes 6291460
  113.5 34.9 %collective-permute-start.10 = (bf16[4096,256]{1,0:T(8,128)(2,1)}, bf16[4096,256]{1,0:T(8,128)(2,1)}, u32[]{:S(2)}, u32[]{:S(2)}) collective-permute-start(bf16[4096,256]{1,0:T(8,128)(2,1)} %collective-permute-done.6), channel_id=1, source_target_pairs={{4,3},{2,7},{12,11},{10,15},{20,19},{18,23},{28,27},{26,31}} | collective-permute-start | bytes 6291464 | tf_op jit(solution)/shard_map/ppermute | solution.py:331
  115.6 32.8 %collective-permute-start.9 = (bf16[4096,256]{1,0:T(8,128)(2,1)}, bf16[4096,256]{1,0:T(8,128)(2,1)}, u32[]{:S(2)}, u32[]{:S(2)}) collective-permute-start(bf16[4096,256]{1,0:T(8,128)(2,1)} %collective-permute-done.4.refs_4_), channel_id=1, source_target_pairs={{7,3},{3,7},{15,11},{11,15},{23,19},{19,23},{31,27},{27,31}} | collective-permute-start | bytes 6291464 | tf_op jit(solution)/shard_map/ppermute | solution.py:331
  122.4 2.0 copy-start.1
  126.8 3.2 %collective-permute-start.7 = (bf16[256,256]{1,0:T(8,128)(2,1)S(1)}, bf16[256,256]{1,0:T(8,128)(2,1)S(1)}, u32[]{:S(2)}, u32[]{:S(2)}) collective-permute-start(bf16[256,256]{1,0:T(8,128)(2,1)S(1)} %fusion.17), channel_id=1, source_target_pairs={{0,8},{1,9},{2,10},{4,12},{5,13},{6,14},{8,0},{9,1},{10,2},{12,4},... | collective-permute-start | bytes 393224 | tf_op jit(solution)/shard_map/ppermute | solution.py:262
  130.1 7.4 %collective-permute-start.8 = (bf16[256,256]{1,0:T(8,128)(2,1)S(1)}, bf16[256,256]{1,0:T(8,128)(2,1)S(1)}, u32[]{:S(2)}, u32[]{:S(2)}) collective-permute-start(bf16[256,256]{1,0:T(8,128)(2,1)S(1)} %add_convert_fusion.1.refs_1_), channel_id=1, source_target_pairs={{0,16},{1,17},{2,18},{4,20},{5,21},{6,22},{8,24},{9,25},{10,26},{1... | collective-permute-start | bytes 393224 | tf_op jit(solution)/shard_map/ppermute | solution.py:262
  147.0 1.4 copy-start
  148.4 0.7 collective-permute-start.11
  149.1 64.8 %collective-permute-start.12 = (bf16[4096,256]{1,0:T(8,128)(2,1)}, bf16[4096,256]{1,0:T(8,128)(2,1)S(1)}, u32[]{:S(2)}, u32[]{:S(2)}) collective-permute-start(bf16[4096,256]{1,0:T(8,128)(2,1)} %get-tuple-element.51), channel_id=1, source_target_pairs={{1,6},{2,7},{4,1},{5,2},{0,3},{6,5},{9,14},{10,15},{12,9},{13,10},... | collective-permute-start | bytes 6291464 | tf_op jit(solution)/shard_map/ppermute | solution.py:331
  167.5 128.6 %collective-permute-start.16 = (bf16[4096,256]{1,0:T(8,128)(2,1)}, bf16[4096,256]{1,0:T(8,128)(2,1)}, u32[]{:S(2)}, u32[]{:S(2)}) collective-permute-start(bf16[4096,256]{1,0:T(8,128)(2,1)} %copy-done), channel_id=1, source_target_pairs={{0,5},{1,6},{2,7},{4,1},{5,2},{6,3},{8,13},{9,14},{10,15},{12,9},{... | collective-permute-start | bytes 6291464 | tf_op jit(solution)/shard_map/ppermute | solution.py:331
  182.0 116.7 %collective-permute-start.15 = (bf16[4096,256]{1,0:T(8,128)(2,1)}, bf16[4096,256]{1,0:T(8,128)(2,1)}, u32[]{:S(2)}, u32[]{:S(2)}) collective-permute-start(bf16[4096,256]{1,0:T(8,128)(2,1)} %get-tuple-element.57), channel_id=1, source_target_pairs={{3,0},{7,4},{11,8},{15,12},{19,16},{23,20},{27,24},{31,28}} | collective-permute-start | bytes 6291464 | tf_op jit(solution)/shard_map/ppermute | solution.py:331
  184.0 114.8 %collective-permute-start.14 = (bf16[4096,256]{1,0:T(8,128)(2,1)}, bf16[4096,256]{1,0:T(8,128)(2,1)}, u32[]{:S(2)}, u32[]{:S(2)}) collective-permute-start(bf16[4096,256]{1,0:T(8,128)(2,1)} %get-tuple-element.56), channel_id=1, source_target_pairs={{3,0},{7,4},{11,8},{15,12},{19,16},{23,20},{27,24},{31,28}} | collective-permute-start | bytes 6291464 | tf_op jit(solution)/shard_map/ppermute | solution.py:331
  213.9 84.9 %collective-permute-start.13 = (bf16[4096,256]{1,0:T(8,128)(2,1)S(1)}, bf16[4096,256]{1,0:T(8,128)(2,1)}, u32[]{:S(2)}, u32[]{:S(2)}) collective-permute-start(bf16[4096,256]{1,0:T(8,128)(2,1)S(1)} %collective-permute-done.12.source), channel_id=1, source_target_pairs={{3,5},{5,3},{11,13},{13,11},{19,21},{21,19},{27,29},{29,27}} | collective-permute-start | bytes 6291464 | tf_op jit(solution)/shard_map/ppermute | solution.py:331
  215.9 3.5 %copy-start.2 = (bf16[8192,256]{1,0:T(8,128)(2,1)S(1)}, bf16[8192,256]{1,0:T(8,128)(2,1)}, u32[]{:S(2)}) copy-start(bf16[8192,256]{1,0:T(8,128)(2,1)} %copy-done.1) | copy-start | bytes 12582916

commit v6 on v5

--- a/solution.py
+++ b/solution.py
@@ -59,18 +59,18 @@
         for copy in reads_of(t, sources, starts, tile, block, arrivals):
             copy.wait()
         here = pl.ds(pl.multiple_of(t * tile, tile), tile)
-        rotated[here, :] = jnp.dot(
-            block[here, :], columns[...], preferred_element_type=jnp.float32
+        rotated[here, :] = lax.dot_general(
+            block[here, :], columns[...], (((1,), (1,)), ((), ())), preferred_element_type=jnp.float32
         ).astype(rotated.dtype)
         write_of(t).start()
         return carry
 
-    def finish(t, carry):
+    def wait(t, carry):
         write_of(t).wait()
         return carry
 
     lax.fori_loop(0, tiles, rotate, 0)
-    lax.fori_loop(0, tiles, finish, 0)
+    return lambda: lax.fori_loop(0, tiles, wait, 0)
 
 
 def polar_columns(selector, mine, other, moving, keeping, iterate):
@@ -83,23 +83,23 @@
     diagonal = (row == column).astype(jnp.float32) / start_scale
     iterate[:width, :width] = diagonal
     iterate[width:, width:] = diagonal
-    iterate[:width, width:] = -coupled / start_scale
-    iterate[width:, :width] = coupled.T / start_scale
+    iterate[:width, width:] = coupled / start_scale
+    iterate[width:, :width] = -coupled.T / start_scale
 
     def step(_, carry):
         current = iterate[...]
         rounded = current.astype(jnp.bfloat16)
         square = lax.dot_general(
-            rounded, rounded, (((0,), (0,)), ((), ())), preferred_element_type=jnp.float32
+            rounded, rounded, (((1,), (1,)), ((), ())), preferred_element_type=jnp.float32
         ).astype(jnp.bfloat16)
         iterate[...] = 1.5 * current - 0.5 * jnp.dot(
-            rounded, square, preferred_element_type=jnp.float32
+            square, rounded, preferred_element_type=jnp.float32
         )
         return carry
 
     lax.fori_loop(0, POLAR_STEPS, step, 0, unroll=True)
-    first = iterate[:, :width].astype(jnp.bfloat16)
-    second = iterate[:, width:].astype(jnp.bfloat16)
+    first = iterate[:width, :].astype(jnp.bfloat16)
+    second = iterate[width:, :].astype(jnp.bfloat16)
     second_stays = selector[0] == 1
 
     @pl.when(second_stays)
@@ -118,9 +118,8 @@
     counts = [len(starts) for starts in starts_of]
     parts = len(counts)
     tail = refs[3 + sum(counts) :]
-    moving, keeping = tail[:2]
-    outs, iterate, block, rotated = tail[2 : 2 + parts], tail[2 + parts], tail[3 + parts], tail[4 + parts]
-    arrivals, departures = tail[5 + parts :]
+    kept_columns, outs = tail[0], tail[1 : 1 + parts]
+    iterate, moving, keeping, block, rotated, arrivals, departures, departure = tail[1 + parts :]
     rows = outs[0].shape[0]
     tiles = rows // tile
     at, pieces = 3, []
@@ -133,30 +132,39 @@
     for piece in pieces:
         start_reads(*piece)
     polar_columns(selector, mine, other, moving, keeping, iterate)
-    for k, (sources, starts, _, _, rows_of, arrived) in enumerate(pieces):
+    waits = [
         write_rotated(
-            sources, starts, tiles, tile, rows_of, arrived, moving,
-            rotated.at[pl.ds(k * rows, rows)], outs[k], 0, departures.at[k],
-        )
+            *piece, moving, rotated.at[pl.ds(k * rows, rows)], outs[k], 0, departures.at[k]
+        )
+        for k, piece in enumerate(pieces)
+    ]
+    write = pltpu.make_async_copy(keeping, kept_columns, departure)
+    write.start()
+    for wait in waits:
+        wait()
+    write.wait()
 
 
 def rotation_of(selector, terms, parts, starts_of, rows, where):
     width = terms[0].shape[0]
     tile = min(TILE, rows)
     counts = [len(part) for part in parts]
-    columns = jax.ShapeDtypeStruct((2 * width, width), jnp.bfloat16)
+    columns = (width, 2 * width)
     moved = jax.ShapeDtypeStruct((rows, width), jnp.bfloat16)
     return pl.pallas_call(
         functools.partial(rotation_kernel, tile, starts_of),
-        out_shape=[columns, columns] + [moved] * len(parts),
+        out_shape=[jax.ShapeDtypeStruct(columns, jnp.bfloat16)] + [moved] * len(parts),
         in_specs=[IN_SMEM, IN_VMEM, IN_VMEM] + where,
-        out_specs=[IN_VMEM, IN_VMEM] + [IN_HBM] * len(parts),
+        out_specs=[IN_HBM] * (1 + len(parts)),
         scratch_shapes=[
             pltpu.VMEM((2 * width, 2 * width), jnp.float32),
+            pltpu.VMEM(columns, jnp.bfloat16),
+            pltpu.VMEM(columns, jnp.bfloat16),
             pltpu.VMEM((len(parts) * rows, 2 * width), jnp.bfloat16),
             pltpu.VMEM((len(parts) * rows, width), jnp.bfloat16),
             pltpu.SemaphoreType.DMA((len(parts), max(counts), rows // tile)),
             pltpu.SemaphoreType.DMA((len(parts), rows // tile)),
+            pltpu.SemaphoreType.DMA(()),
         ],
         compiler_params=pltpu.CompilerParams(vmem_limit_bytes=VMEM_LIMIT),
         cost_estimate=pl.CostEstimate(
@@ -174,11 +182,11 @@
     start_reads(sources, starts, tiles, tile, block, arrivals)
     write_rotated(
         sources, starts, tiles, tile, block, arrivals, columns, rotated, out, first_row, departures
-    )
+    )()
 
 
 def rotated_rows(sources, starts, rows, columns, where, shape=None, out=None, first_row=0):
-    width = columns.shape[1]
+    width = columns.shape[0]
     tile = min(TILE, rows)
     before = [] if out is None else [out]
     return pl.pallas_call(
@@ -354,7 +362,7 @@
     after_detoured = among([target(p) for p in detoured])
 
     gram = whole_gram(matrix)
-    _, keeping, first, last = rotation_of(
+    keeping, first, last = rotation_of(
         selector(0), summed(gram, whole), [[matrix], [matrix]], [[0], [half]], half, [IN_HBM] * 2
     )
     got_first = passed(first, sends(others) + [(source, by) for source, _, by, _ in late_ways])
@@ -381,7 +389,7 @@
             both * 2,
         )
 
-    _, prompt_keeping, first, last = slot_moved(got_first, got_last, terms_of(got_first, got_last, prompt))
+    prompt_keeping, first, last = slot_moved(got_first, got_last, terms_of(got_first, got_last, prompt))
     first, last, late_first, late_last, token = lax.optimization_barrier(
         (first, last, late_first, late_last, jnp.zeros((16, 128), matrix.dtype))
     )
@@ -398,7 +406,7 @@
         lambda: terms_of(late_first, late_last, late),
         lambda: (jnp.zeros((width, width), matrix.dtype),) * 2,
     )
-    _, late_keeping, first, last = slot_moved(late_first, late_last, terms)
+    late_keeping, first, last = slot_moved(late_first, late_last, terms)
     from_late_first = passed(first, sends(late))
     from_late_last = passed(last, sends(late))
 

time: 304 us -> 302 us (level)
  Pallas kernels: 48.1 us -> 44 us
    pallas_call x3, Pallas kernels: 29.3 us -> 25 us  [rotation_of(): pl.pallas_call(functools.partial(rotation_kernel, tile, starts_of), out_s...]
  transfers between devices with their start and end apart: 15 -> 15, of which waited for: 8 -> 8; matrix products, arithmetic and copies ran while one was open for 3% -> 3% of each run, Pallas kernels for 12% -> 11%
where the time goes in v6:
time: 302 us; the launch traced here: 298 us
  waiting for transfers between devices  194 us (64%)
  starting transfers between devices  47.9 us (16%)
  Pallas kernels  44 us (15%)
  local copies, waits for them, and re-layouts  5.79 us (2%)
  matrix products  3.08 us (1%)
    ppermute x11, waiting for transfers between devices, passed(): return lax.ppermute(value, 'pair', pairs)  184 us
    ppermute x11, starting transfers between devices, passed(): return lax.ppermute(value, 'pair', pairs)  41 us
    pallas_call x3, Pallas kernels, rotation_of(): pl.pallas_call(functools.partial(rotation_kernel, tile, starts_of), out_s...  25 us
    pallas_call x3, Pallas kernels, rotated_rows(): pl.pallas_call(functools.partial(rotated_kernel, starts, tile, rows, firs...  10.7 us
    ppermute x4, waiting for transfers between devices, summed(): other = lax.ppermute(total, ('samp', 'pair'), pairs)  9.53 us
    ppermute x4, starting transfers between devices, summed(): other = lax.ppermute(total, ('samp', 'pair'), pairs)  6.94 us
  transfers between devices with their start and end apart: 15, of which 8 were waited for; matrix products, arithmetic and copies ran while one was open for 3% of the time, Pallas kernels for 11%

profile of v6, /device:TPU:4, one launch (start us, length us, event | category | flops | bytes accessed | tf_op | source)
XLA Modules:
  0.0 297.9 jit_solution(2876335259975036147)
XLA Ops:
  0.0 4.1 %shard_map.28 = bf16[256,256]{1,0:T(8,128)(2,1)S(1)} custom-call(bf16[8192,512]{1,0:T(8,128)(2,1)} %refs_1_.1), custom_call_target="tpu_custom_call" | custom-call | flops 1073741824 | bytes 8388608 | tf_op jit(solution)/shard_map/pallas_call | solution.py:301
  7.7 3.5 %collective-permute-done.3.refs_2_ = bf16[256,256]{1,0:T(8,128)(2,1)S(1)} collective-permute-done((bf16[256,256]{1,0:T(8,128)(2,1)S(1)}, bf16[256,256]{1,0:T(8,128)(2,1)S(1)}, u32[]{:S(2)}, u32[]{:S(2)}) %collective-permute-start.3) | collective-permute-done | bytes 131104 | tf_op jit(solution)/shard_map/ppermute | solution.py:270
  11.2 7.5 %shard_map.29 = (bf16[256,512]{1,0:T(8,128)(2,1)S(1)}, bf16[4096,256]{1,0:T(8,128)(2,1)S(1)}, bf16[4096,256]{1,0:T(8,128)(2,1)S(1)}) custom-call(s32[1]{0:T(128)} %bitcast.2.refs_0_, bf16[256,256]{1,0:T(8,128)(2,1)S(1)} %add_convert_fusion.2.refs_1_, bf16[256,256]{1,0:T(8,128)(2,1)S(1)} %collective-permute-done.3.refs_2_, bf16[8192,512]{1,0:T(8,128)(2,1)} %refs_1_.1, ...), custom_call_target="tpu_custom_call" | custom-call | flops 4831838208 | bytes 13238272 | tf_op jit(solution)/shard_map/pallas_call | solution.py:154
  18.7 3.6 %collective-permute-start.4 = (bf16[4096,256]{1,0:T(8,128)(2,1)S(1)}, bf16[4096,256]{1,0:T(8,128)(2,1)}, u32[]{:S(2)}, u32[]{:S(2)}) collective-permute-start(bf16[4096,256]{1,0:T(8,128)(2,1)S(1)} %get-tuple-element.39), channel_id=1, source_target_pairs={{0,5},{1,6},{3,0},{4,1},{5,2},{7,4},{6,7},{2,3},{8,13},{9,14},{11,... | collective-permute-start | bytes 6291464 | tf_op jit(solution)/shard_map/ppermute | solution.py:339
  22.3 3.4 %collective-permute-start.5 = (bf16[4096,256]{1,0:T(8,128)(2,1)S(1)}, bf16[4096,256]{1,0:T(8,128)(2,1)S(1)}, u32[]{:S(2)}, u32[]{:S(2)}) collective-permute-start(bf16[4096,256]{1,0:T(8,128)(2,1)S(1)} %get-tuple-element.40), channel_id=1, source_target_pairs={{0,5},{1,6},{3,0},{4,1},{5,2},{7,4},{8,13},{9,14},{11,8},{12,9},{1... | collective-permute-start | bytes 6291464 | tf_op jit(solution)/shard_map/ppermute | solution.py:339
  25.7 2.0 collective-permute-start.6
  27.7 41.5 %collective-permute-done.4.refs_4_ = bf16[4096,256]{1,0:T(8,128)(2,1)} collective-permute-done((bf16[4096,256]{1,0:T(8,128)(2,1)S(1)}, bf16[4096,256]{1,0:T(8,128)(2,1)}, u32[]{:S(2)}, u32[]{:S(2)}) %collective-permute-start.4) | collective-permute-done | bytes 2097184 | tf_op jit(solution)/shard_map/ppermute | solution.py:339
  69.2 43.1 %collective-permute-done.5.refs_6_ = bf16[4096,256]{1,0:T(8,128)(2,1)S(1)} collective-permute-done((bf16[4096,256]{1,0:T(8,128)(2,1)S(1)}, bf16[4096,256]{1,0:T(8,128)(2,1)S(1)}, u32[]{:S(2)}, u32[]{:S(2)}) %collective-permute-start.5) | collective-permute-done | bytes 2097184 | tf_op jit(solution)/shard_map/ppermute | solution.py:339
  112.3 2.1 collective-permute-start.10
  114.4 2.0 collective-permute-start.9
  116.4 5.0 %shard_map.30.refs_3_.refs_5_.refs_1_ = bf16[8192,256]{1,0:T(8,128)(2,1)S(1)} custom-call(bf16[256,512]{1,0:T(8,128)(2,1)S(1)} %get-tuple-element.38.refs_0_, bf16[8192,512]{1,0:T(8,128)(2,1)} %refs_1_.1), custom_call_target="tpu_custom_call" | custom-call | flops 2147483648 | bytes 12582912 | tf_op jit(solution)/shard_map/pallas_call | solution.py:192
  123.4 2.3 fusion.17
  129.0 3.4 %collective-permute-start.8 = (bf16[256,256]{1,0:T(8,128)(2,1)S(1)}, bf16[256,256]{1,0:T(8,128)(2,1)S(1)}, u32[]{:S(2)}, u32[]{:S(2)}) collective-permute-start(bf16[256,256]{1,0:T(8,128)(2,1)S(1)} %add_convert_fusion.1.refs_1_), channel_id=1, source_target_pairs={{0,16},{1,17},{2,18},{4,20},{5,21},{6,22},{8,24},{9,25},{10,26},{1... | collective-permute-start | bytes 393224 | tf_op jit(solution)/shard_map/ppermute | solution.py:270
  133.1 3.4 %collective-permute-done.8.refs_2_ = bf16[256,256]{1,0:T(8,128)(2,1)S(1)} collective-permute-done((bf16[256,256]{1,0:T(8,128)(2,1)S(1)}, bf16[256,256]{1,0:T(8,128)(2,1)S(1)}, u32[]{:S(2)}, u32[]{:S(2)}) %collective-permute-start.8) | collective-permute-done | bytes 131104 | tf_op jit(solution)/shard_map/ppermute | solution.py:270
  136.5 8.4 %shard_map.31 = (bf16[256,512]{1,0:T(8,128)(2,1)S(1)}, bf16[4096,256]{1,0:T(8,128)(2,1)S(1)}, bf16[4096,256]{1,0:T(8,128)(2,1)}) custom-call(s32[1]{0:T(128)} %bitcast.1.refs_0_, bf16[256,256]{1,0:T(8,128)(2,1)S(1)} %add_convert_fusion.1.refs_1_, bf16[256,256]{1,0:T(8,128)(2,1)S(1)} %collective-permute-done.8.refs_2_, bf16[8192,256]{1,0:T(8,128)(2,1)} %copy-done.1, ...), custom_call_target="tpu_custom_call" | custom-call | flops 4831838208 | bytes 13238272 | tf_op jit(solution)/shard_map/pallas_call | solution.py:154
  147.0 19.3 %collective-permute-start.12 = (bf16[4096,256]{1,0:T(8,128)(2,1)}, bf16[4096,256]{1,0:T(8,128)(2,1)S(1)}, u32[]{:S(2)}, u32[]{:S(2)}) collective-permute-start(bf16[4096,256]{1,0:T(8,128)(2,1)} %get-tuple-element.51), channel_id=1, source_target_pairs={{1,6},{2,7},{4,1},{5,2},{0,3},{6,5},{9,14},{10,15},{12,9},{13,10},... | collective-permute-start | bytes 6291464 | tf_op jit(solution)/shard_map/ppermute | solution.py:339
  169.6 9.1 %shard_map.32 = (bf16[256,512]{1,0:T(8,128)(2,1)S(1)}, bf16[4096,256]{1,0:T(8,128)(2,1)}, bf16[4096,256]{1,0:T(8,128)(2,1)}) custom-call(s32[1]{0:T(128)} %bitcast.1.refs_0_, bf16[256,256]{1,0:T(8,128)(2,1)} %get-tuple-element.54.refs_1_, bf16[256,256]{1,0:T(8,128)(2,1)} %get-tuple-element.55.refs_2_, bf16[8192,256]{1,0:T(8,128)(2,1)} %copy-done.1, ...), custom_call_target="tpu_custom_call" | custom-call | flops 4831838208 | bytes 13238272 | tf_op jit(solution)/shard_map/pallas_call | solution.py:154
  178.7 2.0 collective-permute-start.15
  182.7 30.1 %collective-permute-done.12.source = bf16[4096,256]{1,0:T(8,128)(2,1)S(1)} collective-permute-done((bf16[4096,256]{1,0:T(8,128)(2,1)}, bf16[4096,256]{1,0:T(8,128)(2,1)S(1)}, u32[]{:S(2)}, u32[]{:S(2)}) %collective-permute-start.12) | collective-permute-done | bytes 2097184 | tf_op jit(solution)/shard_map/ppermute | solution.py:339
  214.7 2.8 broadcast_select_fusion
  218.2 2.8 shard_map.33.refs_3_
  221.0 2.9 shard_map.34._
  225.4 69.6 %collective-permute-done.16.source = bf16[4096,256]{1,0:T(8,128)(2,1)} collective-permute-done((bf16[4096,256]{1,0:T(8,128)(2,1)}, bf16[4096,256]{1,0:T(8,128)(2,1)}, u32[]{:S(2)}, u32[]{:S(2)}) %collective-permute-start.16) | collective-permute-done | bytes 2097184 | tf_op jit(solution)/shard_map/ppermute | solution.py:339
  295.0 2.6 shard_map.36._
  (41 shorter events, 22.3 us)
Async XLA Ops:
  0.0 7.1 %copy-start.5 = (s32[2,8]{1,0:T(2,128)S(1)}, s32[2,8]{1,0:T(2,128)}, u32[]{:S(2)}) copy-start(s32[2,8]{1,0:T(2,128)} %param.5) | copy-start | bytes 196
  4.1 1.4 collective-permute-start.2
  5.6 5.6 %collective-permute-start.3 = (bf16[256,256]{1,0:T(8,128)(2,1)S(1)}, bf16[256,256]{1,0:T(8,128)(2,1)S(1)}, u32[]{:S(2)}, u32[]{:S(2)}) collective-permute-start(bf16[256,256]{1,0:T(8,128)(2,1)S(1)} %add_convert_fusion.2.refs_1_), channel_id=1, source_target_pairs={{0,16},{1,17},{2,18},{3,19},{4,20},{5,21},{6,22},{7,23},{8,24},{9,... | collective-permute-start | bytes 393224 | tf_op jit(solution)/shard_map/ppermute | solution.py:270
  18.7 50.5 %collective-permute-start.4 = (bf16[4096,256]{1,0:T(8,128)(2,1)S(1)}, bf16[4096,256]{1,0:T(8,128)(2,1)}, u32[]{:S(2)}, u32[]{:S(2)}) collective-permute-start(bf16[4096,256]{1,0:T(8,128)(2,1)S(1)} %get-tuple-element.39), channel_id=1, source_target_pairs={{0,5},{1,6},{3,0},{4,1},{5,2},{7,4},{6,7},{2,3},{8,13},{9,14},{11,... | collective-permute-start | bytes 6291464 | tf_op jit(solution)/shard_map/ppermute | solution.py:339
  22.3 90.0 %collective-permute-start.5 = (bf16[4096,256]{1,0:T(8,128)(2,1)S(1)}, bf16[4096,256]{1,0:T(8,128)(2,1)S(1)}, u32[]{:S(2)}, u32[]{:S(2)}) collective-permute-start(bf16[4096,256]{1,0:T(8,128)(2,1)S(1)} %get-tuple-element.40), channel_id=1, source_target_pairs={{0,5},{1,6},{3,0},{4,1},{5,2},{7,4},{8,13},{9,14},{11,8},{12,9},{1... | collective-permute-start | bytes 6291464 | tf_op jit(solution)/shard_map/ppermute | solution.py:339
  25.7 86.6 %collective-permute-start.6 = (bf16[4096,256]{1,0:T(8,128)(2,1)S(1)}, bf16[4096,256]{1,0:T(8,128)(2,1)}, u32[]{:S(2)}, u32[]{:S(2)}) collective-permute-start(bf16[4096,256]{1,0:T(8,128)(2,1)S(1)} %get-tuple-element.40), channel_id=1, source_target_pairs={{6,4},{2,2},{14,12},{10,10},{22,20},{18,18},{30,28},{26,26}} | collective-permute-start | bytes 6291464 | tf_op jit(solution)/shard_map/ppermute | solution.py:339
  112.3 9.1 %copy-start.4 = (bf16[4096,256]{1,0:T(8,128)(2,1)}, bf16[4096,256]{1,0:T(8,128)(2,1)S(1)}, u32[]{:S(2)}) copy-start(bf16[4096,256]{1,0:T(8,128)(2,1)S(1)} %collective-permute-done.5.refs_6_) | copy-start | bytes 6291460
  112.3 34.0 %collective-permute-start.10 = (bf16[4096,256]{1,0:T(8,128)(2,1)}, bf16[4096,256]{1,0:T(8,128)(2,1)}, u32[]{:S(2)}, u32[]{:S(2)}) collective-permute-start(bf16[4096,256]{1,0:T(8,128)(2,1)} %collective-permute-done.6), channel_id=1, source_target_pairs={{4,3},{2,7},{12,11},{10,15},{20,19},{18,23},{28,27},{26,31}} | collective-permute-start | bytes 6291464 | tf_op jit(solution)/shard_map/ppermute | solution.py:339
  114.4 31.9 %collective-permute-start.9 = (bf16[4096,256]{1,0:T(8,128)(2,1)}, bf16[4096,256]{1,0:T(8,128)(2,1)}, u32[]{:S(2)}, u32[]{:S(2)}) collective-permute-start(bf16[4096,256]{1,0:T(8,128)(2,1)} %collective-permute-done.4.refs_4_), channel_id=1, source_target_pairs={{7,3},{3,7},{15,11},{11,15},{23,19},{19,23},{31,27},{27,31}} | collective-permute-start | bytes 6291464 | tf_op jit(solution)/shard_map/ppermute | solution.py:339
  121.4 2.0 copy-start.1
  125.8 3.2 %collective-permute-start.7 = (bf16[256,256]{1,0:T(8,128)(2,1)S(1)}, bf16[256,256]{1,0:T(8,128)(2,1)S(1)}, u32[]{:S(2)}, u32[]{:S(2)}) collective-permute-start(bf16[256,256]{1,0:T(8,128)(2,1)S(1)} %fusion.17), channel_id=1, source_target_pairs={{0,8},{1,9},{2,10},{4,12},{5,13},{6,14},{8,0},{9,1},{10,2},{12,4},... | collective-permute-start | bytes 393224 | tf_op jit(solution)/shard_map/ppermute | solution.py:270
  129.0 7.4 %collective-permute-start.8 = (bf16[256,256]{1,0:T(8,128)(2,1)S(1)}, bf16[256,256]{1,0:T(8,128)(2,1)S(1)}, u32[]{:S(2)}, u32[]{:S(2)}) collective-permute-start(bf16[256,256]{1,0:T(8,128)(2,1)S(1)} %add_convert_fusion.1.refs_1_), channel_id=1, source_target_pairs={{0,16},{1,17},{2,18},{4,20},{5,21},{6,22},{8,24},{9,25},{10,26},{1... | collective-permute-start | bytes 393224 | tf_op jit(solution)/shard_map/ppermute | solution.py:270
  144.9 1.4 copy-start
  146.3 0.7 collective-permute-start.11
  147.0 65.7 %collective-permute-start.12 = (bf16[4096,256]{1,0:T(8,128)(2,1)}, bf16[4096,256]{1,0:T(8,128)(2,1)S(1)}, u32[]{:S(2)}, u32[]{:S(2)}) collective-permute-start(bf16[4096,256]{1,0:T(8,128)(2,1)} %get-tuple-element.51), channel_id=1, source_target_pairs={{1,6},{2,7},{4,1},{5,2},{0,3},{6,5},{9,14},{10,15},{12,9},{13,10},... | collective-permute-start | bytes 6291464 | tf_op jit(solution)/shard_map/ppermute | solution.py:339
  166.3 128.6 %collective-permute-start.16 = (bf16[4096,256]{1,0:T(8,128)(2,1)}, bf16[4096,256]{1,0:T(8,128)(2,1)}, u32[]{:S(2)}, u32[]{:S(2)}) collective-permute-start(bf16[4096,256]{1,0:T(8,128)(2,1)} %copy-done), channel_id=1, source_target_pairs={{0,5},{1,6},{2,7},{4,1},{5,2},{6,3},{8,13},{9,14},{10,15},{12,9},{... | collective-permute-start | bytes 6291464 | tf_op jit(solution)/shard_map/ppermute | solution.py:339
  178.7 118.9 %collective-permute-start.15 = (bf16[4096,256]{1,0:T(8,128)(2,1)}, bf16[4096,256]{1,0:T(8,128)(2,1)}, u32[]{:S(2)}, u32[]{:S(2)}) collective-permute-start(bf16[4096,256]{1,0:T(8,128)(2,1)} %get-tuple-element.57), channel_id=1, source_target_pairs={{3,0},{7,4},{11,8},{15,12},{19,16},{23,20},{27,24},{31,28}} | collective-permute-start | bytes 6291464 | tf_op jit(solution)/shard_map/ppermute | solution.py:339
  180.7 116.9 %collective-permute-start.14 = (bf16[4096,256]{1,0:T(8,128)(2,1)}, bf16[4096,256]{1,0:T(8,128)(2,1)}, u32[]{:S(2)}, u32[]{:S(2)}) collective-permute-start(bf16[4096,256]{1,0:T(8,128)(2,1)} %get-tuple-element.56), channel_id=1, source_target_pairs={{3,0},{7,4},{11,8},{15,12},{19,16},{23,20},{27,24},{31,28}} | collective-permute-start | bytes 6291464 | tf_op jit(solution)/shard_map/ppermute | solution.py:339
  212.7 84.9 %collective-permute-start.13 = (bf16[4096,256]{1,0:T(8,128)(2,1)S(1)}, bf16[4096,256]{1,0:T(8,128)(2,1)}, u32[]{:S(2)}, u32[]{:S(2)}) collective-permute-start(bf16[4096,256]{1,0:T(8,128)(2,1)S(1)} %collective-permute-done.12.source), channel_id=1, source_target_pairs={{3,5},{5,3},{11,13},{13,11},{19,21},{21,19},{27,29},{29,27}} | collective-permute-start | bytes 6291464 | tf_op jit(solution)/shard_map/ppermute | solution.py:339
  214.7 3.5 %copy-start.2 = (bf16[8192,256]{1,0:T(8,128)(2,1)S(1)}, bf16[8192,256]{1,0:T(8,128)(2,1)}, u32[]{:S(2)}) copy-start(bf16[8192,256]{1,0:T(8,128)(2,1)} %copy-done.1) | copy-start | bytes 12582916

commit v7 on v6

--- a/solution.py
+++ b/solution.py
@@ -239,7 +239,7 @@
 
 def place(wanted, source, out, first_row, after=()):
     rows, width = source.shape
-    tile = min(TILE, rows)
+    tile = min(TILE // 4, rows)
     return pl.pallas_call(
         functools.partial(place_kernel, tile, first_row),
         out_shape=jax.ShapeDtypeStruct(out.shape, out.dtype),
@@ -397,9 +397,10 @@
     first, last, late_first, late_last, token = lax.optimization_barrier(
         (first, last, late_first, late_last, token)
     )
-    from_first = passed(first, sends(prompt))
+    from_first = [passed(first[at : at + half // 2], sends(prompt)) for at in (0, half // 2)]
     from_last = passed(last, sends(straight) + [(source, by) for source, by, _ in ways])
-    from_far = passed(from_last, [(by, end) for _, by, end in ways])
+    relays = [(by, end) for _, by, end in ways]
+    from_far = [passed(from_last[at : at + half // 2], relays) for at in (0, half // 2)]
 
     terms = lax.cond(
         is_late,
@@ -416,10 +417,12 @@
     out = rotated_rows([kept, got_first], [0, 0], half, keeping, both, matrix.shape)
     out = rotated_rows([kept, got_last], [half, 0], half, keeping, both, matrix.shape, out, half)
     out = place((1 - after_late) * (1 - after_detoured), from_last, out, half, [token])
-    out = place(1 - after_late, from_first, out, 0)
+    for at, block in zip((0, half // 2), from_first):
+        out = place(1 - after_late, block, out, at)
     out = place(after_late, from_late_first, out, 0)
     out = place(after_late, from_late_last, out, half)
-    return place(after_detoured, from_far, out, half)
+    out = place(after_detoured, from_far[0], out, half)
+    return place(after_detoured, from_far[1], out, half + half // 2)
 
 
 def solution(mesh):

time: 302 us -> 301 us (level)
  waiting for transfers between devices: 194 us -> 188 us
  local copies, waits for them, and re-layouts: 5.79 us -> 9.74 us
    ppermute x11 -> x13, waiting for transfers between devices: 184 us -> 179 us  [passed(): return lax.ppermute(value, 'pair', pairs)]
    slice x0 -> x2, local copies, waits for them, and re-layouts: none -> 4.65 us  [the longest x1 3.14 us: shards(): first[at:at + half // 2]]
    ppermute x11 -> x13, starting transfers between devices: 41 us -> 39.9 us  [passed(): return lax.ppermute(value, 'pair', pairs)]
  transfers between devices with their start and end apart: 15 -> 17, of which waited for: 8 -> 9; matrix products, arithmetic and copies ran while one was open for 3% -> 4% of each run, Pallas kernels for 11% -> 12%
where the time goes in v7:
time: 301 us; the launch traced here: 297 us
  waiting for transfers between devices  188 us (62%)
  starting transfers between devices  46.9 us (16%)
  Pallas kernels  46.1 us (15%)
  local copies, waits for them, and re-layouts  9.74 us (3%)
  matrix products  3.08 us (1%)
    ppermute x13, waiting for transfers between devices, passed(): return lax.ppermute(value, 'pair', pairs)  179 us
    ppermute x13, starting transfers between devices, passed(): return lax.ppermute(value, 'pair', pairs)  39.9 us
    pallas_call x3, Pallas kernels, rotation_of(): pl.pallas_call(functools.partial(rotation_kernel, tile, starts_of), out_s...  24.3 us
    pallas_call x3, Pallas kernels, rotated_rows(): pl.pallas_call(functools.partial(rotated_kernel, starts, tile, rows, firs...  12.5 us
    ppermute x4, waiting for transfers between devices, summed(): other = lax.ppermute(total, ('samp', 'pair'), pairs)  9.44 us
    ppermute x4, starting transfers between devices, summed(): other = lax.ppermute(total, ('samp', 'pair'), pairs)  6.96 us
  transfers between devices with their start and end apart: 17, of which 9 were waited for; matrix products, arithmetic and copies ran while one was open for 4% of the time, Pallas kernels for 12%

profile of v7, /device:TPU:4, one launch (start us, length us, event | category | flops | bytes accessed | tf_op | source)
XLA Modules:
  0.0 296.7 jit_solution(3064447913374358190)
XLA Ops:
  0.0 4.1 %shard_map.28 = bf16[256,256]{1,0:T(8,128)(2,1)S(1)} custom-call(bf16[8192,512]{1,0:T(8,128)(2,1)} %refs_1_.1), custom_call_target="tpu_custom_call" | custom-call | flops 1073741824 | bytes 8388608 | tf_op jit(solution)/shard_map/pallas_call | solution.py:301
  7.7 3.5 %collective-permute-done.3.refs_2_ = bf16[256,256]{1,0:T(8,128)(2,1)S(1)} collective-permute-done((bf16[256,256]{1,0:T(8,128)(2,1)S(1)}, bf16[256,256]{1,0:T(8,128)(2,1)S(1)}, u32[]{:S(2)}, u32[]{:S(2)}) %collective-permute-start.3) | collective-permute-done | bytes 131104 | tf_op jit(solution)/shard_map/ppermute | solution.py:270
  11.2 7.5 %shard_map.29 = (bf16[256,512]{1,0:T(8,128)(2,1)S(1)}, bf16[4096,256]{1,0:T(8,128)(2,1)S(1)}, bf16[4096,256]{1,0:T(8,128)(2,1)S(1)}) custom-call(s32[1]{0:T(128)} %bitcast.2.refs_0_, bf16[256,256]{1,0:T(8,128)(2,1)S(1)} %add_convert_fusion.2.refs_1_, bf16[256,256]{1,0:T(8,128)(2,1)S(1)} %collective-permute-done.3.refs_2_, bf16[8192,512]{1,0:T(8,128)(2,1)} %refs_1_.1, ...), custom_call_target="tpu_custom_call" | custom-call | flops 4831838208 | bytes 13238272 | tf_op jit(solution)/shard_map/pallas_call | solution.py:154
  18.7 3.6 %collective-permute-start.4 = (bf16[4096,256]{1,0:T(8,128)(2,1)S(1)}, bf16[4096,256]{1,0:T(8,128)(2,1)}, u32[]{:S(2)}, u32[]{:S(2)}) collective-permute-start(bf16[4096,256]{1,0:T(8,128)(2,1)S(1)} %get-tuple-element.39), channel_id=1, source_target_pairs={{0,5},{1,6},{3,0},{4,1},{5,2},{7,4},{6,7},{2,3},{8,13},{9,14},{11,... | collective-permute-start | bytes 6291464 | tf_op jit(solution)/shard_map/ppermute | solution.py:339
  22.3 3.4 %collective-permute-start.5 = (bf16[4096,256]{1,0:T(8,128)(2,1)S(1)}, bf16[4096,256]{1,0:T(8,128)(2,1)S(1)}, u32[]{:S(2)}, u32[]{:S(2)}) collective-permute-start(bf16[4096,256]{1,0:T(8,128)(2,1)S(1)} %get-tuple-element.40), channel_id=1, source_target_pairs={{0,5},{1,6},{3,0},{4,1},{5,2},{7,4},{8,13},{9,14},{11,8},{12,9},{1... | collective-permute-start | bytes 6291464 | tf_op jit(solution)/shard_map/ppermute | solution.py:339
  27.7 41.5 %collective-permute-done.4.refs_4_ = bf16[4096,256]{1,0:T(8,128)(2,1)} collective-permute-done((bf16[4096,256]{1,0:T(8,128)(2,1)S(1)}, bf16[4096,256]{1,0:T(8,128)(2,1)}, u32[]{:S(2)}, u32[]{:S(2)}) %collective-permute-start.4) | collective-permute-done | bytes 2097184 | tf_op jit(solution)/shard_map/ppermute | solution.py:339
  69.2 43.1 %collective-permute-done.5.refs_6_ = bf16[4096,256]{1,0:T(8,128)(2,1)S(1)} collective-permute-done((bf16[4096,256]{1,0:T(8,128)(2,1)S(1)}, bf16[4096,256]{1,0:T(8,128)(2,1)S(1)}, u32[]{:S(2)}, u32[]{:S(2)}) %collective-permute-start.5) | collective-permute-done | bytes 2097184 | tf_op jit(solution)/shard_map/ppermute | solution.py:339
  112.3 2.1 collective-permute-start.10
  114.4 2.1 collective-permute-start.9
  116.4 5.0 %shard_map.30.refs_3_.refs_5_.refs_1_ = bf16[8192,256]{1,0:T(8,128)(2,1)S(1)} custom-call(bf16[256,512]{1,0:T(8,128)(2,1)S(1)} %get-tuple-element.38.refs_0_, bf16[8192,512]{1,0:T(8,128)(2,1)} %refs_1_.1), custom_call_target="tpu_custom_call" | custom-call | flops 2147483648 | bytes 12582912 | tf_op jit(solution)/shard_map/pallas_call | solution.py:192
  123.4 2.3 fusion.17
  129.0 3.4 %collective-permute-start.8 = (bf16[256,256]{1,0:T(8,128)(2,1)S(1)}, bf16[256,256]{1,0:T(8,128)(2,1)S(1)}, u32[]{:S(2)}, u32[]{:S(2)}) collective-permute-start(bf16[256,256]{1,0:T(8,128)(2,1)S(1)} %add_convert_fusion.1.refs_1_), channel_id=1, source_target_pairs={{0,16},{1,17},{2,18},{4,20},{5,21},{6,22},{8,24},{9,25},{10,26},{1... | collective-permute-start | bytes 393224 | tf_op jit(solution)/shard_map/ppermute | solution.py:270
  133.1 3.3 %collective-permute-done.8.refs_2_ = bf16[256,256]{1,0:T(8,128)(2,1)S(1)} collective-permute-done((bf16[256,256]{1,0:T(8,128)(2,1)S(1)}, bf16[256,256]{1,0:T(8,128)(2,1)S(1)}, u32[]{:S(2)}, u32[]{:S(2)}) %collective-permute-start.8) | collective-permute-done | bytes 131104 | tf_op jit(solution)/shard_map/ppermute | solution.py:270
  136.5 8.5 %shard_map.31 = (bf16[256,512]{1,0:T(8,128)(2,1)S(1)}, bf16[4096,256]{1,0:T(8,128)(2,1)S(1)}, bf16[4096,256]{1,0:T(8,128)(2,1)}) custom-call(s32[1]{0:T(128)} %bitcast.1.refs_0_, bf16[256,256]{1,0:T(8,128)(2,1)S(1)} %add_convert_fusion.1.refs_1_, bf16[256,256]{1,0:T(8,128)(2,1)S(1)} %collective-permute-done.8.refs_2_, bf16[8192,256]{1,0:T(8,128)(2,1)} %copy-done.1, ...), custom_call_target="tpu_custom_call" | custom-call | flops 4831838208 | bytes 13238272 | tf_op jit(solution)/shard_map/pallas_call | solution.py:154
  147.0 19.3 %collective-permute-start.12 = (bf16[4096,256]{1,0:T(8,128)(2,1)}, bf16[4096,256]{1,0:T(8,128)(2,1)S(1)}, u32[]{:S(2)}, u32[]{:S(2)}) collective-permute-start(bf16[4096,256]{1,0:T(8,128)(2,1)} %get-tuple-element.51), channel_id=1, source_target_pairs={{1,6},{2,7},{4,1},{5,2},{0,3},{6,5},{9,14},{10,15},{12,9},{13,10},... | collective-permute-start | bytes 6291464 | tf_op jit(solution)/shard_map/ppermute | solution.py:339
  166.4 3.1 %fusion.20 = (bf16[2048,256]{1,0:T(8,128)(2,1)}, bf16[2048,256]{1,0:T(8,128)(2,1)}) fusion(bf16[4096,256]{1,0:T(8,128)(2,1)} %copy-done), kind=kLoop, calls=%fused_computation.20 | loop fusion | bytes 4194304 | tf_op jit(solution)/shard_map/slice | solution.py:400
  174.7 8.3 %shard_map.32 = (bf16[256,512]{1,0:T(8,128)(2,1)S(1)}, bf16[4096,256]{1,0:T(8,128)(2,1)}, bf16[4096,256]{1,0:T(8,128)(2,1)S(1)}) custom-call(s32[1]{0:T(128)} %bitcast.1.refs_0_, bf16[256,256]{1,0:T(8,128)(2,1)} %get-tuple-element.54.refs_1_, bf16[256,256]{1,0:T(8,128)(2,1)} %get-tuple-element.55.refs_2_, bf16[8192,256]{1,0:T(8,128)(2,1)} %copy-done.1, ...), custom_call_target="tpu_custom_call" | custom-call | flops 4831838208 | bytes 13238272 | tf_op jit(solution)/shard_map/pallas_call | solution.py:154
  184.7 28.0 %collective-permute-done.12.source = bf16[4096,256]{1,0:T(8,128)(2,1)S(1)} collective-permute-done((bf16[4096,256]{1,0:T(8,128)(2,1)}, bf16[4096,256]{1,0:T(8,128)(2,1)S(1)}, u32[]{:S(2)}, u32[]{:S(2)}) %collective-permute-start.12) | collective-permute-done | bytes 2097184 | tf_op jit(solution)/shard_map/ppermute | solution.py:339
  215.0 60.5 %collective-permute-done.18.source = bf16[2048,256]{1,0:T(8,128)(2,1)} collective-permute-done((bf16[2048,256]{1,0:T(8,128)(2,1)}, bf16[2048,256]{1,0:T(8,128)(2,1)}, u32[]{:S(2)}, u32[]{:S(2)}) %collective-permute-start.18) | collective-permute-done | bytes 1048608 | tf_op jit(solution)/shard_map/ppermute | solution.py:339
  276.2 2.0 broadcast_select_fusion
  278.2 3.7 %shard_map.33.refs_3_ = bf16[8192,512]{1,0:T(8,128)(2,1)} custom-call(bf16[256,512]{1,0:T(8,128)(2,1)S(1)} %broadcast_select_fusion.2.refs_0_, bf16[8192,256]{1,0:T(8,128)(2,1)} %copy-done.1, bf16[4096,256]{1,0:T(8,128)(2,1)S(1)} %get-tuple-element.68.refs_2_), custom_call_target="tpu_custom_call" | custom-call | flops 1073741824 | bytes 6291456 | tf_op jit(solution)/shard_map/pallas_call | solution.py:192
  282.0 3.7 %shard_map.34._ = bf16[8192,512]{1,0:T(8,128)(2,1)} custom-call(bf16[256,512]{1,0:T(8,128)(2,1)S(1)} %broadcast_select_fusion.2.refs_0_, bf16[8192,256]{1,0:T(8,128)(2,1)} %copy-done.1, bf16[4096,256]{1,0:T(8,128)(2,1)S(1)} %get-tuple-element.69.refs_2_, bf16[8192,512]{1,0:T(8,128)(2,1)} %shard_map.33.refs_3_), custom_call_target="tpu_custom_call", output_to_operand_aliasing={{}: (3, {})} | custom-call | flops 1073741824 | bytes 6291456 | tf_op jit(solution)/shard_map/pallas_call | solution.py:192
  287.4 2.0 shard_map.36._
  289.4 5.5 %collective-permute-done.17.source = bf16[2048,256]{1,0:T(8,128)(2,1)S(1)} collective-permute-done((bf16[2048,256]{1,0:T(8,128)(2,1)}, bf16[2048,256]{1,0:T(8,128)(2,1)S(1)}, u32[]{:S(2)}, u32[]{:S(2)}) %collective-permute-start.17) | collective-permute-done | bytes 1048608 | tf_op jit(solution)/shard_map/ppermute | solution.py:339
  (51 shorter events, 27.6 us)
Async XLA Ops:
  0.0 7.1 %copy-start.5 = (s32[2,8]{1,0:T(2,128)S(1)}, s32[2,8]{1,0:T(2,128)}, u32[]{:S(2)}) copy-start(s32[2,8]{1,0:T(2,128)} %param.5) | copy-start | bytes 196
  4.1 1.4 collective-permute-start.2
  5.6 5.6 %collective-permute-start.3 = (bf16[256,256]{1,0:T(8,128)(2,1)S(1)}, bf16[256,256]{1,0:T(8,128)(2,1)S(1)}, u32[]{:S(2)}, u32[]{:S(2)}) collective-permute-start(bf16[256,256]{1,0:T(8,128)(2,1)S(1)} %add_convert_fusion.2.refs_1_), channel_id=1, source_target_pairs={{0,16},{1,17},{2,18},{3,19},{4,20},{5,21},{6,22},{7,23},{8,24},{9,... | collective-permute-start | bytes 393224 | tf_op jit(solution)/shard_map/ppermute | solution.py:270
  18.7 50.5 %collective-permute-start.4 = (bf16[4096,256]{1,0:T(8,128)(2,1)S(1)}, bf16[4096,256]{1,0:T(8,128)(2,1)}, u32[]{:S(2)}, u32[]{:S(2)}) collective-permute-start(bf16[4096,256]{1,0:T(8,128)(2,1)S(1)} %get-tuple-element.39), channel_id=1, source_target_pairs={{0,5},{1,6},{3,0},{4,1},{5,2},{7,4},{6,7},{2,3},{8,13},{9,14},{11,... | collective-permute-start | bytes 6291464 | tf_op jit(solution)/shard_map/ppermute | solution.py:339
  22.3 90.1 %collective-permute-start.5 = (bf16[4096,256]{1,0:T(8,128)(2,1)S(1)}, bf16[4096,256]{1,0:T(8,128)(2,1)S(1)}, u32[]{:S(2)}, u32[]{:S(2)}) collective-permute-start(bf16[4096,256]{1,0:T(8,128)(2,1)S(1)} %get-tuple-element.40), channel_id=1, source_target_pairs={{0,5},{1,6},{3,0},{4,1},{5,2},{7,4},{8,13},{9,14},{11,8},{12,9},{1... | collective-permute-start | bytes 6291464 | tf_op jit(solution)/shard_map/ppermute | solution.py:339
  25.7 86.6 %collective-permute-start.6 = (bf16[4096,256]{1,0:T(8,128)(2,1)S(1)}, bf16[4096,256]{1,0:T(8,128)(2,1)}, u32[]{:S(2)}, u32[]{:S(2)}) collective-permute-start(bf16[4096,256]{1,0:T(8,128)(2,1)S(1)} %get-tuple-element.40), channel_id=1, source_target_pairs={{6,4},{2,2},{14,12},{10,10},{22,20},{18,18},{30,28},{26,26}} | collective-permute-start | bytes 6291464 | tf_op jit(solution)/shard_map/ppermute | solution.py:339
  112.3 9.1 %copy-start.3 = (bf16[4096,256]{1,0:T(8,128)(2,1)}, bf16[4096,256]{1,0:T(8,128)(2,1)S(1)}, u32[]{:S(2)}) copy-start(bf16[4096,256]{1,0:T(8,128)(2,1)S(1)} %collective-permute-done.5.refs_6_) | copy-start | bytes 6291460
  112.3 34.0 %collective-permute-start.10 = (bf16[4096,256]{1,0:T(8,128)(2,1)}, bf16[4096,256]{1,0:T(8,128)(2,1)}, u32[]{:S(2)}, u32[]{:S(2)}) collective-permute-start(bf16[4096,256]{1,0:T(8,128)(2,1)} %collective-permute-done.6), channel_id=1, source_target_pairs={{4,3},{2,7},{12,11},{10,15},{20,19},{18,23},{28,27},{26,31}} | collective-permute-start | bytes 6291464 | tf_op jit(solution)/shard_map/ppermute | solution.py:339
  114.4 31.9 %collective-permute-start.9 = (bf16[4096,256]{1,0:T(8,128)(2,1)}, bf16[4096,256]{1,0:T(8,128)(2,1)}, u32[]{:S(2)}, u32[]{:S(2)}) collective-permute-start(bf16[4096,256]{1,0:T(8,128)(2,1)} %collective-permute-done.4.refs_4_), channel_id=1, source_target_pairs={{7,3},{3,7},{15,11},{11,15},{23,19},{19,23},{31,27},{27,31}} | collective-permute-start | bytes 6291464 | tf_op jit(solution)/shard_map/ppermute | solution.py:339
  121.4 2.0 copy-start.1
  125.7 3.2 %collective-permute-start.7 = (bf16[256,256]{1,0:T(8,128)(2,1)S(1)}, bf16[256,256]{1,0:T(8,128)(2,1)S(1)}, u32[]{:S(2)}, u32[]{:S(2)}) collective-permute-start(bf16[256,256]{1,0:T(8,128)(2,1)S(1)} %fusion.17), channel_id=1, source_target_pairs={{0,8},{1,9},{2,10},{4,12},{5,13},{6,14},{8,0},{9,1},{10,2},{12,4},... | collective-permute-start | bytes 393224 | tf_op jit(solution)/shard_map/ppermute | solution.py:270
  129.0 7.4 %collective-permute-start.8 = (bf16[256,256]{1,0:T(8,128)(2,1)S(1)}, bf16[256,256]{1,0:T(8,128)(2,1)S(1)}, u32[]{:S(2)}, u32[]{:S(2)}) collective-permute-start(bf16[256,256]{1,0:T(8,128)(2,1)S(1)} %add_convert_fusion.1.refs_1_), channel_id=1, source_target_pairs={{0,16},{1,17},{2,18},{4,20},{5,21},{6,22},{8,24},{9,25},{10,26},{1... | collective-permute-start | bytes 393224 | tf_op jit(solution)/shard_map/ppermute | solution.py:270
  145.0 1.3 copy-start
  146.3 0.7 collective-permute-start.11
  147.0 65.7 %collective-permute-start.12 = (bf16[4096,256]{1,0:T(8,128)(2,1)}, bf16[4096,256]{1,0:T(8,128)(2,1)S(1)}, u32[]{:S(2)}, u32[]{:S(2)}) collective-permute-start(bf16[4096,256]{1,0:T(8,128)(2,1)} %get-tuple-element.51), channel_id=1, source_target_pairs={{1,6},{2,7},{4,1},{5,2},{0,3},{6,5},{9,14},{10,15},{12,9},{13,10},... | collective-permute-start | bytes 6291464 | tf_op jit(solution)/shard_map/ppermute | solution.py:339
  166.3 7.0 %copy-start.2 = (bf16[8192,256]{1,0:T(8,128)(2,1)S(1)}, bf16[8192,256]{1,0:T(8,128)(2,1)}, u32[]{:S(2)}) copy-start(bf16[8192,256]{1,0:T(8,128)(2,1)} %copy-done.1) | copy-start | bytes 12582916
  169.5 106.0 %collective-permute-start.18 = (bf16[2048,256]{1,0:T(8,128)(2,1)}, bf16[2048,256]{1,0:T(8,128)(2,1)}, u32[]{:S(2)}, u32[]{:S(2)}) collective-permute-start(bf16[2048,256]{1,0:T(8,128)(2,1)} %get-tuple-element.62), channel_id=1, source_target_pairs={{0,5},{1,6},{2,7},{4,1},{5,2},{6,3},{8,13},{9,14},{10,15},{12,9},{... | collective-permute-start | bytes 3145736 | tf_op jit(solution)/shard_map/ppermute | solution.py:339
  171.4 123.4 %collective-permute-start.17 = (bf16[2048,256]{1,0:T(8,128)(2,1)}, bf16[2048,256]{1,0:T(8,128)(2,1)S(1)}, u32[]{:S(2)}, u32[]{:S(2)}) collective-permute-start(bf16[2048,256]{1,0:T(8,128)(2,1)} %get-tuple-element.63), channel_id=1, source_target_pairs={{0,5},{1,6},{2,7},{4,1},{5,2},{6,3},{8,13},{9,14},{10,15},{12,9},{... | collective-permute-start | bytes 3145736 | tf_op jit(solution)/shard_map/ppermute | solution.py:339
  183.0 112.9 %collective-permute-start.16 = (bf16[4096,256]{1,0:T(8,128)(2,1)}, bf16[4096,256]{1,0:T(8,128)(2,1)S(1)}, u32[]{:S(2)}, u32[]{:S(2)}) collective-permute-start(bf16[4096,256]{1,0:T(8,128)(2,1)} %get-tuple-element.57), channel_id=1, source_target_pairs={{3,0},{7,4},{11,8},{15,12},{19,16},{23,20},{27,24},{31,28}} | collective-permute-start | bytes 6291464 | tf_op jit(solution)/shard_map/ppermute | solution.py:339
  183.8 112.3 %collective-permute-start.15 = (bf16[4096,256]{1,0:T(8,128)(2,1)S(1)}, bf16[4096,256]{1,0:T(8,128)(2,1)S(1)}, u32[]{:S(2)}, u32[]{:S(2)}) collective-permute-start(bf16[4096,256]{1,0:T(8,128)(2,1)S(1)} %get-tuple-element.56), channel_id=1, source_target_pairs={{3,0},{7,4},{11,8},{15,12},{19,16},{23,20},{27,24},{31,28}} | collective-permute-start | bytes 6291464 | tf_op jit(solution)/shard_map/ppermute | solution.py:339
  184.7 91.5 %copy-start.4 = (bf16[4096,256]{1,0:T(8,128)(2,1)S(1)}, bf16[4096,256]{1,0:T(8,128)(2,1)}, u32[]{:S(2)}) copy-start(bf16[4096,256]{1,0:T(8,128)(2,1)} %copy-done.3) | copy-start | bytes 6291460
  214.2 82.1 %collective-permute-start.14 = (bf16[2048,256]{1,0:T(8,128)(2,1)}, bf16[2048,256]{1,0:T(8,128)(2,1)S(1)}, u32[]{:S(2)}, u32[]{:S(2)}) collective-permute-start(bf16[2048,256]{1,0:T(8,128)(2,1)} %get-tuple-element.64), channel_id=1, source_target_pairs={{3,5},{5,3},{11,13},{13,11},{19,21},{21,19},{27,29},{29,27}} | collective-permute-start | bytes 3145736 | tf_op jit(solution)/shard_map/ppermute | solution.py:339
  275.5 20.9 %collective-permute-start.13 = (bf16[2048,256]{1,0:T(8,128)(2,1)}, bf16[2048,256]{1,0:T(8,128)(2,1)S(1)}, u32[]{:S(2)}, u32[]{:S(2)}) collective-permute-start(bf16[2048,256]{1,0:T(8,128)(2,1)} %get-tuple-element.65), channel_id=1, source_target_pairs={{3,5},{5,3},{11,13},{13,11},{19,21},{21,19},{27,29},{29,27}} | collective-permute-start | bytes 3145736 | tf_op jit(solution)/shard_map/ppermute | solution.py:339

commit v8 on v7

--- a/solution.py
+++ b/solution.py
@@ -397,10 +397,11 @@
     first, last, late_first, late_last, token = lax.optimization_barrier(
         (first, last, late_first, late_last, token)
     )
-    from_first = [passed(first[at : at + half // 2], sends(prompt)) for at in (0, half // 2)]
+    from_first = [passed(first[: half // 2], sends(prompt)), passed(first[half // 2 :], sends(prompt))]
     from_last = passed(last, sends(straight) + [(source, by) for source, by, _ in ways])
     relays = [(by, end) for _, by, end in ways]
-    from_far = [passed(from_last[at : at + half // 2], relays) for at in (0, half // 2)]
+    cuts = ((0, half * 3 // 4), (half * 3 // 4, half))
+    from_far = [passed(from_last[a:b], relays) for a, b in cuts]
 
     terms = lax.cond(
         is_late,
@@ -422,7 +423,7 @@
     out = place(after_late, from_late_first, out, 0)
     out = place(after_late, from_late_last, out, half)
     out = place(after_detoured, from_far[0], out, half)
-    return place(after_detoured, from_far[1], out, half + half // 2)
+    return place(after_detoured, from_far[1], out, half + half * 3 // 4)
 
 
 def solution(mesh):

time: 301 us -> 301 us (level)
  starting transfers between devices: 46.9 us -> 52.8 us
    ppermute x13, starting transfers between devices: 39.9 us -> 45.8 us  [passed(): return lax.ppermute(value, 'pair', pairs)]
  transfers between devices with their start and end apart: 17 -> 17, of which waited for: 9 -> 9; matrix products, arithmetic and copies ran while one was open for 4% -> 2% of each run, Pallas kernels for 12% -> 11%
where the time goes in v8:
time: 301 us; the launch traced here: 297 us
  waiting for transfers between devices  189 us (63%)
  starting transfers between devices  52.8 us (18%)
  Pallas kernels  44 us (15%)
  local copies, waits for them, and re-layouts  8.96 us (3%)
    ppermute x13, waiting for transfers between devices, passed(): return lax.ppermute(value, 'pair', pairs)  179 us
    ppermute x13, starting transfers between devices, passed(): return lax.ppermute(value, 'pair', pairs)  45.8 us
    pallas_call x3, Pallas kernels, rotation_of(): pl.pallas_call(functools.partial(rotation_kernel, tile, starts_of), out_s...  24.8 us
    pallas_call x3, Pallas kernels, rotated_rows(): pl.pallas_call(functools.partial(rotated_kernel, starts, tile, rows, firs...  10.7 us
    ppermute x4, waiting for transfers between devices, summed(): other = lax.ppermute(total, ('samp', 'pair'), pairs)  9.52 us
    ppermute x4, starting transfers between devices, summed(): other = lax.ppermute(total, ('samp', 'pair'), pairs)  6.95 us
  transfers between devices with their start and end apart: 17, of which 9 were waited for; matrix products, arithmetic and copies ran while one was open for 2% of the time, Pallas kernels for 11%

profile of v8, /device:TPU:4, one launch (start us, length us, event | category | flops | bytes accessed | tf_op | source)
XLA Modules:
  0.0 296.9 jit_solution(18293877995405592903)
XLA Ops:
  0.0 4.1 %shard_map.28 = bf16[256,256]{1,0:T(8,128)(2,1)S(1)} custom-call(bf16[8192,512]{1,0:T(8,128)(2,1)} %refs_1_.1), custom_call_target="tpu_custom_call" | custom-call | flops 1073741824 | bytes 8388608 | tf_op jit(solution)/shard_map/pallas_call | solution.py:301
  7.7 3.5 %collective-permute-done.3.refs_2_ = bf16[256,256]{1,0:T(8,128)(2,1)S(1)} collective-permute-done((bf16[256,256]{1,0:T(8,128)(2,1)S(1)}, bf16[256,256]{1,0:T(8,128)(2,1)S(1)}, u32[]{:S(2)}, u32[]{:S(2)}) %collective-permute-start.3) | collective-permute-done | bytes 131104 | tf_op jit(solution)/shard_map/ppermute | solution.py:270
  11.2 7.5 %shard_map.29 = (bf16[256,512]{1,0:T(8,128)(2,1)S(1)}, bf16[4096,256]{1,0:T(8,128)(2,1)S(1)}, bf16[4096,256]{1,0:T(8,128)(2,1)S(1)}) custom-call(s32[1]{0:T(128)} %bitcast.2.refs_0_, bf16[256,256]{1,0:T(8,128)(2,1)S(1)} %add_convert_fusion.2.refs_1_, bf16[256,256]{1,0:T(8,128)(2,1)S(1)} %collective-permute-done.3.refs_2_, bf16[8192,512]{1,0:T(8,128)(2,1)} %refs_1_.1, ...), custom_call_target="tpu_custom_call" | custom-call | flops 4831838208 | bytes 13238272 | tf_op jit(solution)/shard_map/pallas_call | solution.py:154
  18.7 3.6 %collective-permute-start.4 = (bf16[4096,256]{1,0:T(8,128)(2,1)S(1)}, bf16[4096,256]{1,0:T(8,128)(2,1)S(1)}, u32[]{:S(2)}, u32[]{:S(2)}) collective-permute-start(bf16[4096,256]{1,0:T(8,128)(2,1)S(1)} %get-tuple-element.39), channel_id=1, source_target_pairs={{0,5},{1,6},{3,0},{4,1},{5,2},{7,4},{6,7},{2,3},{8,13},{9,14},{11,... | collective-permute-start | bytes 6291464 | tf_op jit(solution)/shard_map/ppermute | solution.py:339
  22.3 3.4 %collective-permute-start.5 = (bf16[4096,256]{1,0:T(8,128)(2,1)S(1)}, bf16[4096,256]{1,0:T(8,128)(2,1)S(1)}, u32[]{:S(2)}, u32[]{:S(2)}) collective-permute-start(bf16[4096,256]{1,0:T(8,128)(2,1)S(1)} %get-tuple-element.40), channel_id=1, source_target_pairs={{0,5},{1,6},{3,0},{4,1},{5,2},{7,4},{8,13},{9,14},{11,8},{12,9},{1... | collective-permute-start | bytes 6291464 | tf_op jit(solution)/shard_map/ppermute | solution.py:339
  25.7 2.0 collective-permute-start.6
  27.7 41.4 %collective-permute-done.4.refs_4_ = bf16[4096,256]{1,0:T(8,128)(2,1)S(1)} collective-permute-done((bf16[4096,256]{1,0:T(8,128)(2,1)S(1)}, bf16[4096,256]{1,0:T(8,128)(2,1)S(1)}, u32[]{:S(2)}, u32[]{:S(2)}) %collective-permute-start.4) | collective-permute-done | bytes 2097184 | tf_op jit(solution)/shard_map/ppermute | solution.py:339
  69.1 43.2 %collective-permute-done.5.refs_6_ = bf16[4096,256]{1,0:T(8,128)(2,1)S(1)} collective-permute-done((bf16[4096,256]{1,0:T(8,128)(2,1)S(1)}, bf16[4096,256]{1,0:T(8,128)(2,1)S(1)}, u32[]{:S(2)}, u32[]{:S(2)}) %collective-permute-start.5) | collective-permute-done | bytes 2097184 | tf_op jit(solution)/shard_map/ppermute | solution.py:339
  112.3 2.1 collective-permute-start.10
  114.4 2.0 collective-permute-start.9
  116.4 5.0 %shard_map.30.refs_3_.refs_5_.refs_1_ = bf16[8192,256]{1,0:T(8,128)(2,1)S(1)} custom-call(bf16[256,512]{1,0:T(8,128)(2,1)S(1)} %get-tuple-element.38.refs_0_, bf16[8192,512]{1,0:T(8,128)(2,1)} %refs_1_.1), custom_call_target="tpu_custom_call" | custom-call | flops 2147483648 | bytes 12582912 | tf_op jit(solution)/shard_map/pallas_call | solution.py:192
  127.5 3.4 %collective-permute-start.8 = (bf16[256,256]{1,0:T(8,128)(2,1)S(1)}, bf16[256,256]{1,0:T(8,128)(2,1)S(1)}, u32[]{:S(2)}, u32[]{:S(2)}) collective-permute-start(bf16[256,256]{1,0:T(8,128)(2,1)S(1)} %add_convert_fusion.1.refs_1_), channel_id=1, source_target_pairs={{0,16},{1,17},{2,18},{4,20},{5,21},{6,22},{8,24},{9,25},{10,26},{1... | collective-permute-start | bytes 393224 | tf_op jit(solution)/shard_map/ppermute | solution.py:270
  131.5 3.4 %collective-permute-done.8.refs_2_ = bf16[256,256]{1,0:T(8,128)(2,1)S(1)} collective-permute-done((bf16[256,256]{1,0:T(8,128)(2,1)S(1)}, bf16[256,256]{1,0:T(8,128)(2,1)S(1)}, u32[]{:S(2)}, u32[]{:S(2)}) %collective-permute-start.8) | collective-permute-done | bytes 131104 | tf_op jit(solution)/shard_map/ppermute | solution.py:270
  134.9 8.3 %shard_map.31 = (bf16[256,512]{1,0:T(8,128)(2,1)S(1)}, bf16[4096,256]{1,0:T(8,128)(2,1)S(1)}, bf16[4096,256]{1,0:T(8,128)(2,1)}) custom-call(s32[1]{0:T(128)} %bitcast.1.refs_0_, bf16[256,256]{1,0:T(8,128)(2,1)S(1)} %add_convert_fusion.1.refs_1_, bf16[256,256]{1,0:T(8,128)(2,1)S(1)} %collective-permute-done.8.refs_2_, bf16[8192,256]{1,0:T(8,128)(2,1)} %copy-done.2, ...), custom_call_target="tpu_custom_call" | custom-call | flops 4831838208 | bytes 13238272 | tf_op jit(solution)/shard_map/pallas_call | solution.py:154
  144.1 22.4 %collective-permute-start.12 = (bf16[4096,256]{1,0:T(8,128)(2,1)}, bf16[4096,256]{1,0:T(8,128)(2,1)S(1)}, u32[]{:S(2)}, u32[]{:S(2)}) collective-permute-start(bf16[4096,256]{1,0:T(8,128)(2,1)} %get-tuple-element.51), channel_id=1, source_target_pairs={{1,6},{2,7},{4,1},{5,2},{0,3},{6,5},{9,14},{10,15},{12,9},{13,10},... | collective-permute-start | bytes 6291464 | tf_op jit(solution)/shard_map/ppermute | solution.py:339
  171.2 9.1 %shard_map.32 = (bf16[256,512]{1,0:T(8,128)(2,1)S(1)}, bf16[4096,256]{1,0:T(8,128)(2,1)}, bf16[4096,256]{1,0:T(8,128)(2,1)}) custom-call(s32[1]{0:T(128)} %bitcast.1.refs_0_, bf16[256,256]{1,0:T(8,128)(2,1)} %get-tuple-element.54.refs_1_, bf16[256,256]{1,0:T(8,128)(2,1)} %get-tuple-element.55.refs_2_, bf16[8192,256]{1,0:T(8,128)(2,1)} %copy-done.2, ...), custom_call_target="tpu_custom_call" | custom-call | flops 4831838208 | bytes 13238272 | tf_op jit(solution)/shard_map/pallas_call | solution.py:154
  181.0 2.0 collective-permute-start.16
  183.0 2.0 collective-permute-start.15
  185.0 2.2 collective-permute-start.17
  187.2 25.7 %collective-permute-done.12.source = bf16[4096,256]{1,0:T(8,128)(2,1)S(1)} collective-permute-done((bf16[4096,256]{1,0:T(8,128)(2,1)}, bf16[4096,256]{1,0:T(8,128)(2,1)S(1)}, u32[]{:S(2)}, u32[]{:S(2)}) %collective-permute-start.12) | collective-permute-done | bytes 2097184 | tf_op jit(solution)/shard_map/ppermute | solution.py:339
  215.0 60.6 %collective-permute-done.18.source = bf16[2048,256]{1,0:T(8,128)(2,1)S(1)} collective-permute-done((bf16[2048,256]{1,0:T(8,128)(2,1)}, bf16[2048,256]{1,0:T(8,128)(2,1)S(1)}, u32[]{:S(2)}, u32[]{:S(2)}) %collective-permute-start.18) | collective-permute-done | bytes 1048608 | tf_op jit(solution)/shard_map/ppermute | solution.py:339
  278.5 2.8 shard_map.33.refs_3_
  281.3 2.9 shard_map.34._
  286.9 8.1 %collective-permute-done.17.source = bf16[2048,256]{1,0:T(8,128)(2,1)S(1)} collective-permute-done((bf16[2048,256]{1,0:T(8,128)(2,1)}, bf16[2048,256]{1,0:T(8,128)(2,1)S(1)}, u32[]{:S(2)}, u32[]{:S(2)}) %collective-permute-start.17) | collective-permute-done | bytes 1048608 | tf_op jit(solution)/shard_map/ppermute | solution.py:339
  (58 shorter events, 27.0 us)
Async XLA Ops:
  0.0 7.1 %copy-start.9 = (s32[2,8]{1,0:T(2,128)S(1)}, s32[2,8]{1,0:T(2,128)}, u32[]{:S(2)}) copy-start(s32[2,8]{1,0:T(2,128)} %param.5) | copy-start | bytes 196
  4.1 1.4 collective-permute-start.2
  5.6 5.6 %collective-permute-start.3 = (bf16[256,256]{1,0:T(8,128)(2,1)S(1)}, bf16[256,256]{1,0:T(8,128)(2,1)S(1)}, u32[]{:S(2)}, u32[]{:S(2)}) collective-permute-start(bf16[256,256]{1,0:T(8,128)(2,1)S(1)} %add_convert_fusion.2.refs_1_), channel_id=1, source_target_pairs={{0,16},{1,17},{2,18},{3,19},{4,20},{5,21},{6,22},{7,23},{8,24},{9,... | collective-permute-start | bytes 393224 | tf_op jit(solution)/shard_map/ppermute | solution.py:270
  18.7 50.4 %collective-permute-start.4 = (bf16[4096,256]{1,0:T(8,128)(2,1)S(1)}, bf16[4096,256]{1,0:T(8,128)(2,1)S(1)}, u32[]{:S(2)}, u32[]{:S(2)}) collective-permute-start(bf16[4096,256]{1,0:T(8,128)(2,1)S(1)} %get-tuple-element.39), channel_id=1, source_target_pairs={{0,5},{1,6},{3,0},{4,1},{5,2},{7,4},{6,7},{2,3},{8,13},{9,14},{11,... | collective-permute-start | bytes 6291464 | tf_op jit(solution)/shard_map/ppermute | solution.py:339
  22.3 90.0 %collective-permute-start.5 = (bf16[4096,256]{1,0:T(8,128)(2,1)S(1)}, bf16[4096,256]{1,0:T(8,128)(2,1)S(1)}, u32[]{:S(2)}, u32[]{:S(2)}) collective-permute-start(bf16[4096,256]{1,0:T(8,128)(2,1)S(1)} %get-tuple-element.40), channel_id=1, source_target_pairs={{0,5},{1,6},{3,0},{4,1},{5,2},{7,4},{8,13},{9,14},{11,8},{12,9},{1... | collective-permute-start | bytes 6291464 | tf_op jit(solution)/shard_map/ppermute | solution.py:339
  25.7 86.6 %collective-permute-start.6 = (bf16[4096,256]{1,0:T(8,128)(2,1)S(1)}, bf16[4096,256]{1,0:T(8,128)(2,1)}, u32[]{:S(2)}, u32[]{:S(2)}) collective-permute-start(bf16[4096,256]{1,0:T(8,128)(2,1)S(1)} %get-tuple-element.40), channel_id=1, source_target_pairs={{6,4},{2,2},{14,12},{10,10},{22,20},{18,18},{30,28},{26,26}} | collective-permute-start | bytes 6291464 | tf_op jit(solution)/shard_map/ppermute | solution.py:339
  69.1 53.1 %copy-start.5 = (bf16[4096,256]{1,0:T(8,128)(2,1)}, bf16[4096,256]{1,0:T(8,128)(2,1)S(1)}, u32[]{:S(2)}) copy-start(bf16[4096,256]{1,0:T(8,128)(2,1)S(1)} %collective-permute-done.4.refs_4_) | copy-start | bytes 6291460
  112.3 9.1 %copy-start.7 = (bf16[4096,256]{1,0:T(8,128)(2,1)}, bf16[4096,256]{1,0:T(8,128)(2,1)S(1)}, u32[]{:S(2)}) copy-start(bf16[4096,256]{1,0:T(8,128)(2,1)S(1)} %collective-permute-done.5.refs_6_) | copy-start | bytes 6291460
  112.3 30.9 %collective-permute-start.10 = (bf16[4096,256]{1,0:T(8,128)(2,1)}, bf16[4096,256]{1,0:T(8,128)(2,1)}, u32[]{:S(2)}, u32[]{:S(2)}) collective-permute-start(bf16[4096,256]{1,0:T(8,128)(2,1)} %collective-permute-done.6), channel_id=1, source_target_pairs={{4,3},{2,7},{12,11},{10,15},{20,19},{18,23},{28,27},{26,31}} | collective-permute-start | bytes 6291464 | tf_op jit(solution)/shard_map/ppermute | solution.py:339
  114.4 28.8 %collective-permute-start.9 = (bf16[4096,256]{1,0:T(8,128)(2,1)S(1)}, bf16[4096,256]{1,0:T(8,128)(2,1)}, u32[]{:S(2)}, u32[]{:S(2)}) collective-permute-start(bf16[4096,256]{1,0:T(8,128)(2,1)S(1)} %collective-permute-done.4.refs_4_), channel_id=1, source_target_pairs={{7,3},{3,7},{15,11},{11,15},{23,19},{19,23},{31,27},{27,31}} | collective-permute-start | bytes 6291464 | tf_op jit(solution)/shard_map/ppermute | solution.py:339
  124.2 3.2 %collective-permute-start.7 = (bf16[256,256]{1,0:T(8,128)(2,1)S(1)}, bf16[256,256]{1,0:T(8,128)(2,1)S(1)}, u32[]{:S(2)}, u32[]{:S(2)}) collective-permute-start(bf16[256,256]{1,0:T(8,128)(2,1)S(1)} %fusion.17), channel_id=1, source_target_pairs={{0,8},{1,9},{2,10},{4,12},{5,13},{6,14},{8,0},{9,1},{10,2},{12,4},... | collective-permute-start | bytes 393224 | tf_op jit(solution)/shard_map/ppermute | solution.py:270
  127.5 7.4 %collective-permute-start.8 = (bf16[256,256]{1,0:T(8,128)(2,1)S(1)}, bf16[256,256]{1,0:T(8,128)(2,1)S(1)}, u32[]{:S(2)}, u32[]{:S(2)}) collective-permute-start(bf16[256,256]{1,0:T(8,128)(2,1)S(1)} %add_convert_fusion.1.refs_1_), channel_id=1, source_target_pairs={{0,16},{1,17},{2,18},{4,20},{5,21},{6,22},{8,24},{9,25},{10,26},{1... | collective-permute-start | bytes 393224 | tf_op jit(solution)/shard_map/ppermute | solution.py:270
  143.3 0.9 collective-permute-start.11
  144.1 68.8 %collective-permute-start.12 = (bf16[4096,256]{1,0:T(8,128)(2,1)}, bf16[4096,256]{1,0:T(8,128)(2,1)S(1)}, u32[]{:S(2)}, u32[]{:S(2)}) collective-permute-start(bf16[4096,256]{1,0:T(8,128)(2,1)} %get-tuple-element.51), channel_id=1, source_target_pairs={{1,6},{2,7},{4,1},{5,2},{0,3},{6,5},{9,14},{10,15},{12,9},{13,10},... | collective-permute-start | bytes 6291464 | tf_op jit(solution)/shard_map/ppermute | solution.py:339
  168.0 107.6 %collective-permute-start.18 = (bf16[2048,256]{1,0:T(8,128)(2,1)}, bf16[2048,256]{1,0:T(8,128)(2,1)S(1)}, u32[]{:S(2)}, u32[]{:S(2)}) collective-permute-start(bf16[2048,256]{1,0:T(8,128)(2,1)} %get-tuple-element.62), channel_id=1, source_target_pairs={{0,5},{1,6},{2,7},{4,1},{5,2},{6,3},{8,13},{9,14},{10,15},{12,9},{... | collective-permute-start | bytes 3145736 | tf_op jit(solution)/shard_map/ppermute | solution.py:339
  181.0 115.1 %collective-permute-start.16 = (bf16[4096,256]{1,0:T(8,128)(2,1)}, bf16[4096,256]{1,0:T(8,128)(2,1)}, u32[]{:S(2)}, u32[]{:S(2)}) collective-permute-start(bf16[4096,256]{1,0:T(8,128)(2,1)} %get-tuple-element.57), channel_id=1, source_target_pairs={{3,0},{7,4},{11,8},{15,12},{19,16},{23,20},{27,24},{31,28}} | collective-permute-start | bytes 6291464 | tf_op jit(solution)/shard_map/ppermute | solution.py:339
  183.0 113.3 %collective-permute-start.15 = (bf16[4096,256]{1,0:T(8,128)(2,1)}, bf16[4096,256]{1,0:T(8,128)(2,1)}, u32[]{:S(2)}, u32[]{:S(2)}) collective-permute-start(bf16[4096,256]{1,0:T(8,128)(2,1)} %get-tuple-element.56), channel_id=1, source_target_pairs={{3,0},{7,4},{11,8},{15,12},{19,16},{23,20},{27,24},{31,28}} | collective-permute-start | bytes 6291464 | tf_op jit(solution)/shard_map/ppermute | solution.py:339
  185.0 91.3 %copy-start.6 = (bf16[4096,256]{1,0:T(8,128)(2,1)S(1)}, bf16[4096,256]{1,0:T(8,128)(2,1)}, u32[]{:S(2)}) copy-start(bf16[4096,256]{1,0:T(8,128)(2,1)} %copy-done.5) | copy-start | bytes 6291460
  185.0 91.3 %copy-start.8 = (bf16[4096,256]{1,0:T(8,128)(2,1)S(1)}, bf16[4096,256]{1,0:T(8,128)(2,1)}, u32[]{:S(2)}) copy-start(bf16[4096,256]{1,0:T(8,128)(2,1)} %copy-done.7) | copy-start | bytes 6291460
  185.0 110.1 %collective-permute-start.17 = (bf16[2048,256]{1,0:T(8,128)(2,1)}, bf16[2048,256]{1,0:T(8,128)(2,1)S(1)}, u32[]{:S(2)}, u32[]{:S(2)}) collective-permute-start(bf16[2048,256]{1,0:T(8,128)(2,1)} %get-tuple-element.63), channel_id=1, source_target_pairs={{0,5},{1,6},{2,7},{4,1},{5,2},{6,3},{8,13},{9,14},{10,15},{12,9},{... | collective-permute-start | bytes 3145736 | tf_op jit(solution)/shard_map/ppermute | solution.py:339
  214.2 82.4 %collective-permute-start.14 = (bf16[3072,256]{1,0:T(8,128)(2,1)}, bf16[3072,256]{1,0:T(8,128)(2,1)S(1)}, u32[]{:S(2)}, u32[]{:S(2)}) collective-permute-start(bf16[3072,256]{1,0:T(8,128)(2,1)} %slice.42), channel_id=1, source_target_pairs={{3,5},{5,3},{11,13},{13,11},{19,21},{21,19},{27,29},{29,27}} | collective-permute-start | bytes 4718600 | tf_op jit(solution)/shard_map/ppermute | solution.py:339
  215.0 61.7 %copy-start.1 = (bf16[256,512]{1,0:T(8,128)(2,1)S(1)}, bf16[256,512]{1,0:T(8,128)(2,1)}, u32[]{:S(2)}) copy-start(bf16[256,512]{1,0:T(8,128)(2,1)} %copy-done) | copy-start | bytes 786436
  275.6 21.1 %collective-permute-start.13 = (bf16[1024,256]{1,0:T(8,128)(2,1)S(1)}, bf16[1024,256]{1,0:T(8,128)(2,1)S(1)}, u32[]{:S(2)}, u32[]{:S(2)}) collective-permute-start(bf16[1024,256]{1,0:T(8,128)(2,1)S(1)} %slice.41), channel_id=1, source_target_pairs={{3,5},{5,3},{11,13},{13,11},{19,21},{21,19},{27,29},{29,27}} | collective-permute-start | bytes 1572872 | tf_op jit(solution)/shard_map/ppermute | solution.py:339
  276.3 2.2 copy-start.3
  (2 other events, 2.7 us)
